TPU v7x, 512 devices: a whole 4x4x16 slice. The times are simulated.
512 devices in a mesh: tile: 128 (over y, z, core), vis: 4 (over x).
Axes of the slice: x: 4, y: 4, z: 16, core: 2. Of those that a mesh axis runs over, the one named last changes fastest.
Arguments:
- model_grid: bfloat16 [4, 65536, 128], P(None, 'tile'), may hold values from -6 to 6
- observed: bfloat16 [4, 8192, 256], P(None, ('tile', 'vis')), may hold values from -6 to 6
- kernels: bfloat16 [8192, 256, 128], P(('tile', 'vis')), may hold values from -0.75 to 0.75
- offsets: int32 [8192, 2], P(('tile', 'vis')), may hold values from 0 to 511, as said below
- counts: int32 [512], P(('tile', 'vis')), may hold values from 8 to 16, as said below
Outputs:
- new_model: bfloat16 [4, 65536, 128], P(None, ('tile', 'vis'))
Inputs may be any that keep to these rules, and one draw needn't show every extreme that they name: Column offsets lie in 0 to 64, row offsets in 0 to 511; block 0 sits at row 511 and column 64. `counts`: device 0 has all 16 slots live.
All inputs are finite; a program needn't handle non-finite values.
Results may differ from a plain program's by a relative error of at most 0.0052.
Values may be sent and summed in bfloat16 or wider, within the bound.
No kernel may reach another device: no remote copies, remote signals or barrier semaphores. Data moves between devices by JAX's collectives and lax.ppermute only.
A program may use at most 64 MiB of HBM per device.

v0:
```python
import jax
import jax.numpy as jnp
from jax import lax
from jax.sharding import PartitionSpec as P

SUB = 64
ITERS = 2


sign_table = (1.0, -1.0, 1.0, -1.0)
step_size = 0.5


def from_partner(block, axis, bit):
    count = lax.axis_size(axis)
    route = []
    for low in range(count):
        high = low | 1 << bit
        if high != low and high < count:
            route += [(low, high), (high, low)]
    return lax.ppermute(block, axis, route)


def from_behind(value, axis, steps):
    count = lax.axis_size(axis)
    pairs = [(source, (source + steps) % count) for source in range(count)]
    return lax.ppermute(value, axis, pairs)


def flip_tile_transposed(values):
    tile_count = lax.axis_size("tile")
    flat = values.reshape(tile_count, -1)
    for section in range(2):
        flat = lax.all_to_all(flat, "tile", split_axis=0, concat_axis=0, tiled=True)
        if section == 0:
            flat = flat[::-1]
    return flat.reshape(values.shape)


def flip_tile(values):
    return flip_tile_transposed(values)


def flip_vis(values):
    for bit_pos in range(lax.axis_size("vis").bit_length() - 1):
        values = from_partner(values, "vis", bit_pos)
    return values


def on_device(model_grid, observed, kernels, offsets, counts):
    parity = jnp.array(sign_table, jnp.float32)[:, None, None]
    vis_count = lax.axis_size("vis")
    vis_index = lax.axis_index("vis")
    band_rows = model_grid.shape[1]
    width_cols = model_grid.shape[2]
    quarter = band_rows // vis_count
    blocks = kernels.shape[0]
    active_slot_index = (jnp.arange(blocks, dtype=jnp.int32) < counts[0])[:, None, None]
    kern_u = kernels[:, :, :SUB]
    kern_v = kernels[:, :, SUB:]
    row_start = offsets[:, 0]
    col_start = offsets[:, 1]
    anchor = jnp.zeros((), jnp.int32)
    measured = jnp.transpose(observed, (1, 0, 2)).astype(jnp.float32)
    model_band = model_grid
    result = None
    for cycle in range(ITERS):
        next_rows = from_behind(model_band[:, :SUB], "tile", -1)
        extended = jnp.concatenate([model_band, next_rows], axis=1)

        def cut_block(row_at, col_at):
            return lax.dynamic_slice(extended, (anchor, row_at, col_at), (4, SUB, SUB))

        subgrids = jax.vmap(cut_block)(row_start, col_start)
        inner_sum = jnp.einsum(
            "ncab,nkb->ncak", subgrids, kern_v, preferred_element_type=jnp.float32
        )
        forward_prediction = jnp.einsum(
            "nka,ncak->nck", kern_u, inner_sum, preferred_element_type=jnp.float32
        )
        misfit_values = jnp.where(
            active_slot_index, measured - forward_prediction, jnp.float32(0.0)
        )
        weighted = (kern_u[:, None].astype(jnp.float32) * misfit_values[..., None]).astype(
            jnp.bfloat16
        )
        fresh = jnp.einsum("ncka,nkb->ncab", weighted, kern_v, preferred_element_type=jnp.float32)

        def place_block(block_id, current_sum):
            start = (anchor, row_start[block_id], col_start[block_id])
            current = lax.dynamic_slice(current_sum, start, (4, SUB, SUB))
            return lax.dynamic_update_slice(current_sum, current + fresh[block_id], start)

        empty = jnp.zeros((4, band_rows + SUB, width_cols), jnp.float32)
        gridded = lax.fori_loop(0, blocks, place_block, empty)
        spilled = from_behind(gridded[:, band_rows:], "tile", 1)
        partial_value = gridded[:, :band_rows].at[:, :SUB].add(spilled)
        shard_sum = lax.psum_scatter(partial_value, "vis", scatter_dimension=1, tiled=True)
        partner = flip_vis(flip_tile(shard_sum))
        mirrored = partner[:, ::-1, ::-1]
        own_model = lax.dynamic_slice_in_dim(model_band, vis_index * quarter, quarter, 1)
        updated = own_model.astype(jnp.float32) + step_size * 0.5 * (shard_sum + parity * mirrored)
        result = updated.astype(jnp.bfloat16)
        if cycle + 1 < ITERS:
            model_band = lax.all_gather(result, "vis", axis=1, tiled=True)
    return result


def solution(mesh):
    placed = (
        P(None, "tile", None),
        P(None, ("tile", "vis"), None),
        P(("tile", "vis"), None, None),
        P(("tile", "vis"), None),
        P(("tile", "vis")),
    )
    return jax.shard_map(
        on_device,
        mesh=mesh,
        in_specs=placed,
        out_specs=P(None, ("tile", "vis"), None),
        check_vma=False,
    )
```

profile of v0, /device:TPU:1, one launch (start us, length us, event | category | flops | bytes accessed | tf_op | source)
XLA Modules:
  0.0 655.6 jit_solution(12709803397505289769)
XLA Ops:
  7.5 8.8 %collective-permute-start = (bf16[4,64,128]{2,1,0:T(8,128)(2,1)S(1)}, bf16[4,64,128]{2,1,0:T(8,128)(2,1)S(1)}, u32[]{:S(2)}, u32[]{:S(2)}) collective-permute-start(bf16[4,64,128]{2,1,0:T(8,128)(2,1)S(1)} %slice.83), channel_id=1, source_target_pairs={{0,508},{4,0},{8,4},{12,8},{16,12},{20,16},{24,20},{28,24},{32,28}... | collective-permute-start | bytes 196616 | tf_op jit(solution)/shard_map/ppermute | solution.py:27
  20.7 40.7 %while.32 = (s32[]{:T(128)}, bf16[4,576,128]{2,1,0:T(8,128)(2,1)S(1)}, s32[16,3]{0,1:T(4,128)S(1)}, bf16[16,4,64,64]{3,2,1,0:T(8,128)(2,1)}, s32[]{:T(128)}) while((s32[]{:T(128)}, bf16[4,576,128]{2,1,0:T(8,128)(2,1)S(1)}, s32[16,3]{0,1:T(4,128)S(1)}, bf16[16,4,64,64]{3,2,1,0:T(8,128)(2,1)}, s32[]{:T(128)}) %tuple.90), condition=%wide.while_cond.2, body=%wide.while_body.2.sunk | while | flops 2 | bytes 99945 | solution.py:72
  66.0 139.3 %while.30 = (s32[]{:T(128)}, f32[4,576,128]{2,1,0:T(8,128)S(1)}, s32[16]{0:T(128)S(1)}, s32[16]{0:T(128)S(1)}, f32[16,4,64,64]{3,2,1,0:T(8,128)}, /*index=5*/s32[]{:T(128)}, s32[]{:T(128)}, s32[]{:T(128)}, s32[]{:T(128)}) while((s32[]{:T(128)}, f32[4,576,128]{2,1,0:T(8,128)S(1)}, s32[16]{0:T(128)S(1)}, s32[16]{0:T(128)S(1)}, ...), condition=%wide.region_1.2_spmd, body=%wide.region_0.1_spmd.sunk | while | flops 16392 | bytes 327881 | solution.py:95
  89.9 2.2 dynamic_update_slice.16
  142.1 2.2 dynamic_update_slice.16
  150.8 2.2 dynamic_update_slice.16
  208.3 4.5 collective-permute-done.1
  213.5 28.1 %reduce-scatter.3.cloned.1.call-done = f32[4,128,128]{2,1,0:T(8,128)} async-done(((f32[4,512,128]{2,1,0:T(8,128)}), f32[4,128,128]{2,1,0:T(8,128)}) %reduce-scatter.3.cloned.1.call-update) | async-done | bytes 262160 | tf_op jit(solution)/shard_map/reduce_scatter | solution.py:98
  241.7 40.7 %all_to_all.42 = f32[128,1,512]{2,1,0:T(1,128)S(1)} all-to-all(f32[128,1,512]{2,1,0:T(1,128)} %bitcast.92), channel_id=1, replica_groups=mesh['tile'=128,'vis'=4] {'tile'}, dimensions={0} | all-to-all | bytes 524288 | tf_op jit(solution)/shard_map/all_to_all | solution.py:34
  282.8 29.2 %all_to_all.43 = f32[128,1,512]{2,1,0:T(1,128)S(1)} all-to-all(f32[128,1,512]{2,1,0:T(1,128)S(1)} %copy.20), channel_id=1, replica_groups=mesh['tile'=128,'vis'=4] {'tile'}, dimensions={0} | all-to-all | bytes 524288 | tf_op jit(solution)/shard_map/all_to_all | solution.py:34
  314.0 5.6 collective-permute-done.2
  319.6 3.1 collective-permute-start.3
  322.7 5.5 collective-permute-done.3
  329.6 10.4 %all_gather.3 = bf16[4,512,128]{2,1,0:T(8,128)(2,1)S(1)} all-gather(bf16[4,128,128]{2,1,0:T(8,128)(2,1)S(1)} %add_convert_fusion.1), channel_id=1, replica_groups=mesh['tile'=128,'vis'=4] {'vis'}, dimensions={1}, use_global_device_ids=true | all-gather | bytes 655360 | tf_op jit(solution)/shard_map/all_gather | solution.py:105
  340.0 9.0 %collective-permute-start.4 = (bf16[4,64,128]{2,1,0:T(8,128)(2,1)S(1)}, bf16[4,64,128]{2,1,0:T(8,128)(2,1)S(1)}, u32[]{:S(2)}, u32[]{:S(2)}) collective-permute-start(bf16[4,64,128]{2,1,0:T(8,128)(2,1)S(1)} %slice.122), channel_id=1, source_target_pairs={{0,508},{4,0},{8,4},{12,8},{16,12},{20,16},{24,20},{28,24},{32,28}... | collective-permute-start | bytes 196616 | tf_op jit(solution)/shard_map/ppermute | solution.py:27
  349.0 2.3 collective-permute-done.4
  352.5 42.0 %while.33 = (s32[]{:T(128)}, bf16[4,576,128]{2,1,0:T(8,128)(2,1)S(1)}, s32[16,3]{0,1:T(4,128)S(1)}, bf16[16,4,64,64]{3,2,1,0:T(8,128)(2,1)}, s32[]{:T(128)}) while((s32[]{:T(128)}, bf16[4,576,128]{2,1,0:T(8,128)(2,1)S(1)}, s32[16,3]{0,1:T(4,128)S(1)}, bf16[16,4,64,64]{3,2,1,0:T(8,128)(2,1)}, s32[]{:T(128)}) %tuple.106), condition=%wide.while_cond.3, body=%wide.while_body.3.sunk | while | flops 2 | bytes 99945 | solution.py:72
  399.0 132.4 %while.31 = (s32[]{:T(128)}, f32[4,576,128]{2,1,0:T(8,128)S(1)}, s32[16]{0:T(128)S(1)}, s32[16]{0:T(128)S(1)}, f32[16,4,64,64]{3,2,1,0:T(8,128)}, /*index=5*/s32[]{:T(128)}, s32[]{:T(128)}, s32[]{:T(128)}, s32[]{:T(128)}) while((s32[]{:T(128)}, f32[4,576,128]{2,1,0:T(8,128)S(1)}, s32[16]{0:T(128)S(1)}, s32[16]{0:T(128)S(1)}, ...), condition=%wide.region_4.5_spmd, body=%wide.region_3.4_spmd.sunk | while | flops 16392 | bytes 327881 | solution.py:95
  536.4 23.0 %reduce-scatter.5.cloned.1.call-done = f32[4,128,128]{2,1,0:T(8,128)} async-done(((f32[4,512,128]{2,1,0:T(8,128)}), f32[4,128,128]{2,1,0:T(8,128)}) %reduce-scatter.5.cloned.1.call-update) | async-done | bytes 262160 | tf_op jit(solution)/shard_map/reduce_scatter | solution.py:98
  559.3 41.5 %all_to_all.44 = f32[128,1,512]{2,1,0:T(1,128)S(1)} all-to-all(f32[128,1,512]{2,1,0:T(1,128)} %bitcast.93), channel_id=1, replica_groups=mesh['tile'=128,'vis'=4] {'tile'}, dimensions={0} | all-to-all | bytes 524288 | tf_op jit(solution)/shard_map/all_to_all | solution.py:34
  601.3 29.2 %all_to_all.45 = f32[128,1,512]{2,1,0:T(1,128)S(1)} all-to-all(f32[128,1,512]{2,1,0:T(1,128)S(1)} %copy.22), channel_id=1, replica_groups=mesh['tile'=128,'vis'=4] {'tile'}, dimensions={0} | all-to-all | bytes 524288 | tf_op jit(solution)/shard_map/all_to_all | solution.py:34
  632.4 5.6 collective-permute-done.6
  638.1 3.1 collective-permute-start.7
  641.2 5.5 collective-permute-done.7
  (285 shorter events, 252.4 us)
Async XLA Ops:
  6.5 12.9 %copy-start.5 = (bf16[4,512,128]{2,1,0:T(8,128)(2,1)S(1)}, bf16[4,512,128]{2,1,0:T(8,128)(2,1)}, u32[]{:S(2)}) copy-start(bf16[4,512,128]{2,1,0:T(8,128)(2,1)} %param.14) | copy-start | bytes 1572868
  6.5 235.1 %reduce-scatter.3.cloned.1.call-start = ((), (), s32[]{:S(2)}) async-start(), calls=%async_computation.6 | async-start | bytes 1310720 | tf_op jit(solution)/shard_map/reduce_scatter | solution.py:98
  7.5 12.0 %collective-permute-start = (bf16[4,64,128]{2,1,0:T(8,128)(2,1)S(1)}, bf16[4,64,128]{2,1,0:T(8,128)(2,1)S(1)}, u32[]{:S(2)}, u32[]{:S(2)}) collective-permute-start(bf16[4,64,128]{2,1,0:T(8,128)(2,1)S(1)} %slice.83), channel_id=1, source_target_pairs={{0,508},{4,0},{8,4},{12,8},{16,12},{20,16},{24,20},{28,24},{32,28}... | collective-permute-start | bytes 196616 | tf_op jit(solution)/shard_map/ppermute | solution.py:27
  18.6 42.9 %copy-start = (bf16[16,256,128]{2,1,0:T(8,128)(2,1)S(1)}, bf16[16,256,128]{2,1,0:T(8,128)(2,1)}, u32[]{:S(2)}) copy-start(bf16[16,256,128]{2,1,0:T(8,128)(2,1)} %param.16) | copy-start | bytes 3145732
  61.5 2.1 copy-start.6
  205.3 7.5 %collective-permute-start.1 = (f32[4,64,128]{2,1,0:T(8,128)S(1)}, f32[4,64,128]{2,1,0:T(8,128)S(1)}, u32[]{:S(2)}, u32[]{:S(2)}) collective-permute-start(f32[4,64,128]{2,1,0:T(8,128)S(1)} %slice.87), channel_id=1, source_target_pairs={{0,4},{4,8},{8,12},{12,16},{16,20},{20,24},{24,28},{28,32},{32,36}... | collective-permute-start | bytes 393224 | tf_op jit(solution)/shard_map/ppermute | solution.py:27
  213.5 115.1 %copy-start.7 = (f32[4]{0:T(128)S(1)}, f32[4]{0:T(128)}, u32[]{:S(2)}) copy-start(f32[4]{0:T(128)} %constant.136.clone) | copy-start | bytes 52
  213.5 345.8 %reduce-scatter.5.cloned.1.call-start = ((), (), s32[]{:S(2)}) async-start(), calls=%async_computation.7 | async-start | bytes 1310720 | tf_op jit(solution)/shard_map/reduce_scatter | solution.py:98
  241.7 86.9 %copy-start.3 = (f32[4,128,128]{2,1,0:T(8,128)S(1)}, f32[4,128,128]{2,1,0:T(8,128)}, u32[]{:S(2)}) copy-start(f32[4,128,128]{2,1,0:T(8,128)} %reduce-scatter.3.cloned.1.call-done) | copy-start | bytes 786436
  312.1 7.6 %collective-permute-start.2 = (f32[4,128,128]{2,1,0:T(8,128)S(1)}, f32[4,128,128]{2,1,0:T(8,128)S(1)}, u32[]{:S(2)}, u32[]{:S(2)}) collective-permute-start(f32[4,128,128]{2,1,0:T(8,128)S(1)} %bitcast.98), channel_id=1, source_target_pairs={{0,1},{1,0},{2,3},{3,2},{4,5},{5,4},{6,7},{7,6},{8,9},{9,8},{10,11... | collective-permute-start | bytes 786440 | tf_op jit(solution)/shard_map/ppermute | solution.py:21
  319.6 8.6 %collective-permute-start.3 = (f32[4,128,128]{2,1,0:T(8,128)S(1)}, f32[4,128,128]{2,1,0:T(8,128)S(1)}, u32[]{:S(2)}, u32[]{:S(2)}) collective-permute-start(f32[4,128,128]{2,1,0:T(8,128)S(1)} %collective-permute-done.2), channel_id=1, source_target_pairs={{0,2},{2,0},{1,3},{3,1},{4,6},{6,4},{5,7},{7,5},{8,10},{10,8},{9,1... | collective-permute-start | bytes 786440 | tf_op jit(solution)/shard_map/ppermute | solution.py:21
  340.0 56.7 %copy-start.2 = (bf16[4,512,128]{2,1,0:T(8,128)(2,1)}, bf16[4,512,128]{2,1,0:T(8,128)(2,1)S(1)}, u32[]{:S(2)}) copy-start(bf16[4,512,128]{2,1,0:T(8,128)(2,1)S(1)} %all_gather.3) | copy-start | bytes 1572868
  340.0 11.3 %collective-permute-start.4 = (bf16[4,64,128]{2,1,0:T(8,128)(2,1)S(1)}, bf16[4,64,128]{2,1,0:T(8,128)(2,1)S(1)}, u32[]{:S(2)}, u32[]{:S(2)}) collective-permute-start(bf16[4,64,128]{2,1,0:T(8,128)(2,1)S(1)} %slice.122), channel_id=1, source_target_pairs={{0,508},{4,0},{8,4},{12,8},{16,12},{20,16},{24,20},{28,24},{32,28}... | collective-permute-start | bytes 196616 | tf_op jit(solution)/shard_map/ppermute | solution.py:27
  531.5 3.9 collective-permute-start.5
  535.3 1.0 copy-start.1
  559.3 87.7 %copy-start.4 = (f32[4,128,128]{2,1,0:T(8,128)S(1)}, f32[4,128,128]{2,1,0:T(8,128)}, u32[]{:S(2)}) copy-start(f32[4,128,128]{2,1,0:T(8,128)} %reduce-scatter.5.cloned.1.call-done) | copy-start | bytes 786436
  630.5 7.6 %collective-permute-start.6 = (f32[4,128,128]{2,1,0:T(8,128)S(1)}, f32[4,128,128]{2,1,0:T(8,128)S(1)}, u32[]{:S(2)}, u32[]{:S(2)}) collective-permute-start(f32[4,128,128]{2,1,0:T(8,128)S(1)} %bitcast.99), channel_id=1, source_target_pairs={{0,1},{1,0},{2,3},{3,2},{4,5},{5,4},{6,7},{7,6},{8,9},{9,8},{10,11... | collective-permute-start | bytes 786440 | tf_op jit(solution)/shard_map/ppermute | solution.py:21
  638.1 8.6 %collective-permute-start.7 = (f32[4,128,128]{2,1,0:T(8,128)S(1)}, f32[4,128,128]{2,1,0:T(8,128)S(1)}, u32[]{:S(2)}, u32[]{:S(2)}) collective-permute-start(f32[4,128,128]{2,1,0:T(8,128)S(1)} %collective-permute-done.6), channel_id=1, source_target_pairs={{0,2},{2,0},{1,3},{3,1},{4,6},{6,4},{5,7},{7,5},{8,10},{10,8},{9,1... | collective-permute-start | bytes 786440 | tf_op jit(solution)/shard_map/ppermute | solution.py:21
Sparse Core Ops, SparseCore 0:
  213.6 28.0 reduce-scatter.2
  536.5 22.7 reduce-scatter.4
where the time goes:
time: 662 us; the launch traced here: 656 us
  local copies, waits for them, and re-layouts  204 us (31%)
  blocking collectives  151 us (23%)
  loops' own time  127 us (19%)
  waiting for transfers between devices  82.1 us (12%)
  other arithmetic  37.1 us (6%)
  starting transfers between devices  31.6 us (5%)
  between operations  14.4 us (2%)
  matrix products  8.58 us (1%)
    all_to_all x4, blocking collectives, flip_tile_transposed(): flat = lax.all_to_all(flat, 'tile', split_axis=0, concat_axis=0, tiled=True)  141 us
    another operation x2, loops' own time, on_device(): gridded = lax.fori_loop(0, blocks, place_block, empty)  127 us
    gather x96, local copies, waits for them, and re-layouts  82.7 us
    dynamic_update_slice x32, local copies, waits for them, and re-layouts, place_block(): lax.dynamic_update_slice(current_sum, current + fresh[block_id], start)  70.3 us
    reduce_scatter x2, waiting for transfers between devices, on_device(): lax.psum_scatter(partial_value, 'vis', scatter_dimension=1, tiled=True)  51.1 us
    dynamic_slice x64, local copies, waits for them, and re-layouts, place_block(): start = (anchor, row_start[block_id], col_start[block_id])  42 us
    add x32, other arithmetic, place_block(): current + fresh[block_id]  32.5 us
    ppermute x4, waiting for transfers between devices, from_partner(): return lax.ppermute(block, axis, route)  22.3 us
  transfers between devices with their start and end apart: 10, of which 9 were waited for; matrix products, arithmetic and copies ran while one was open for 1% of the time, Pallas kernels for 0%

commit v1 on v0

v1 whole, which is shorter than its diff:
```python
import functools

import jax
import jax.numpy as jnp
from jax import lax
from jax.experimental import pallas as pl
from jax.experimental.pallas import tpu as pltpu
from jax.sharding import PartitionSpec as P

SUB = 64
GROUP = 4
SIGNS = (1.0, -1.0, 1.0, -1.0)
STEP = 0.5 * 0.5
F32 = jnp.float32
BF16 = jnp.bfloat16
VMEM = pl.BlockSpec(memory_space=pltpu.VMEM)
SMEM = pl.BlockSpec(memory_space=pltpu.SMEM)


def send(value, route):
    tiles = lax.axis_size("tile")
    views = lax.axis_size("vis")
    pairs = []
    for tile in range(tiles):
        for view in range(views):
            to_tile, to_view = route(tile, view)
            pairs.append((tile * views + view, to_tile % tiles * views + to_view % views))
    return lax.ppermute(value, ("tile", "vis"), pairs)


def call(body, outs, scratch=(), flops=0, moved=0):
    return functools.partial(
        pl.pallas_call,
        body,
        out_shape=outs,
        scratch_shapes=list(scratch),
        compiler_params=pltpu.CompilerParams(vmem_limit_bytes=40 * 1024 * 1024),
        cost_estimate=pl.CostEstimate(flops=flops, bytes_accessed=moved, transcendentals=0),
    )


def dot_nn(left, right):
    return lax.dot_general(left, right, (((1,), (0,)), ((), ())), preferred_element_type=F32)


def dot_nt(left, right):
    return lax.dot_general(left, right, (((1,), (1,)), ((), ())), preferred_element_type=F32)


def prepare_body(offsets, kern, ku_t, kv_t, kv):
    blocks = kern.shape[0]
    cols = kern.shape[2]

    def one(block):
        shift = SUB - offsets[block, 1]
        row = lax.broadcasted_iota(jnp.int32, (cols, cols), 0)
        col = lax.broadcasted_iota(jnp.int32, (cols, cols), 1)
        place_t = jnp.where((col == row + shift) & (col >= SUB), 1.0, 0.0).astype(BF16)
        place = jnp.where((row == col + shift) & (row >= SUB), 1.0, 0.0).astype(BF16)
        pick = jnp.where(row == col, 1.0, 0.0).astype(BF16)[:SUB]
        weights = kern[block]
        ku_t[block] = dot_nt(pick, weights).astype(BF16)
        kv_t[block] = dot_nt(place_t, weights).astype(BF16)
        kv[block] = dot_nn(weights, place).astype(BF16)

    def group(index, carry):
        for lane in range(GROUP):
            one(index * GROUP + lane)
        return carry

    lax.fori_loop(0, blocks // GROUP, group, 0)


def grid_blocks(picks, limit, offsets, obs, ku_t, kv_t, kv, grid, acc):
    def group(index, carry):
        staged = []
        for lane in range(GROUP):
            place = index * GROUP + lane
            live = place < limit
            block = picks[jnp.minimum(place, limit - 1)]
            row = offsets[block, 0]
            patch = jnp.concatenate(
                [grid[comp, pl.ds(row, SUB), :] for comp in range(4)], axis=0
            ).astype(BF16)
            inner = dot_nn(patch, kv_t[block])
            along_u = ku_t[block].astype(F32)
            parts = []
            for comp in range(4):
                seen = jnp.sum(along_u * inner[comp * SUB : (comp + 1) * SUB], axis=0, keepdims=True)
                left = jnp.where(live, obs[comp, pl.ds(block, 1), :] - seen, 0.0)
                parts.append((along_u * left).astype(BF16))
            fresh = dot_nn(jnp.concatenate(parts, axis=0), kv[block])
            staged.append((row, fresh))
        for row, fresh in staged:
            for comp in range(4):
                acc[comp, pl.ds(row, SUB), :] += fresh[comp * SUB : (comp + 1) * SUB]
        return carry

    lax.fori_loop(0, (limit + GROUP - 1) // GROUP, group, 0)


def choose(picks, counts, offsets, blocks, keep):
    def add(block, found):
        good = (block < counts[0]) & keep(offsets[block, 0])

        @pl.when(good)
        def _():
            picks[found] = block

        return found + good.astype(jnp.int32)

    return lax.fori_loop(0, blocks, add, 0)


def first_body(offsets, counts, observed, ku_t, kv_t, kv, model, halo, out, picks, obs, grid, acc):
    rows = model.shape[1]
    obs[...] = observed[...].astype(F32)
    grid[:, :rows] = model[...].astype(F32)
    grid[:, rows:] = halo[...].astype(F32)
    acc[...] = jnp.zeros_like(acc)
    limit = choose(picks, counts, offsets, ku_t.shape[0], lambda row: row >= 0)
    grid_blocks(picks, limit, offsets, obs, ku_t, kv_t, kv, grid, acc)
    out[...] = acc[...].astype(BF16)


def border_body(offsets, counts, observed, ku_t, kv_t, kv, model, spill, tail, picks, obs, grid, acc):
    rows = model.shape[1] - SUB
    base = rows - SUB
    obs[...] = observed[...].astype(F32)
    grid[...] = model[...].astype(F32)
    acc[:, base:] = jnp.zeros((4, 2 * SUB, acc.shape[2]), F32)
    limit = choose(picks, counts, offsets, ku_t.shape[0], lambda row: row > base)
    grid_blocks(picks, limit, offsets, obs, ku_t, kv_t, kv, grid, acc)
    spill[...] = acc[:, rows:].astype(BF16)
    tail[...] = acc[:, base:rows]


def inside_body(offsets, counts, observed, ku_t, kv_t, kv, model, tail, out, picks, obs, grid, acc):
    rows = model.shape[1] - SUB
    base = rows - SUB
    obs[...] = observed[...].astype(F32)
    grid[...] = model[...].astype(F32)
    acc[:, :base] = jnp.zeros((4, base, acc.shape[2]), F32)
    acc[:, base:rows] = tail[...]
    limit = choose(picks, counts, offsets, ku_t.shape[0], lambda row: row <= base)
    grid_blocks(picks, limit, offsets, obs, ku_t, kv_t, kv, grid, acc)
    views = out.shape[0]
    quarter = rows // views
    for view in range(views):
        out[view] = acc[:, view * quarter : (view + 1) * quarter].astype(BF16)


def flip(value):
    return value[..., ::-1, ::-1].astype(F32)


def on_device(model, observed, kernels, offsets, counts):
    views = lax.axis_size("vis")
    view = lax.axis_index("vis")
    tiles = lax.axis_size("tile")
    rows, cols = model.shape[1:]
    full = rows + SUB
    quarter = rows // views
    blocks, depth = kernels.shape[:2]
    sds = jax.ShapeDtypeStruct
    scratch = [
        pltpu.SMEM((blocks,), jnp.int32),
        pltpu.VMEM((4, blocks, depth), F32),
        pltpu.VMEM((4, full, cols), F32),
        pltpu.VMEM((4, full, cols), F32),
    ]

    halo = send(model[:, :SUB], lambda tile, view: (tile - 1, view))
    ku_t, kv_t, kv = call(
        prepare_body,
        (
            sds((blocks, SUB, depth), BF16),
            sds((blocks, cols, depth), BF16),
            sds((blocks, depth, cols), BF16),
        ),
        flops=2 * blocks * depth * cols * 320,
        moved=4 * 1024 * 1024,
    )(in_specs=[SMEM, VMEM], out_specs=(VMEM,) * 3)(offsets, kernels)
    flops = 4 * 2 * blocks * depth * cols * SUB * 2
    partial = call(
        first_body, sds((4, full, cols), BF16), scratch, flops=flops, moved=4 * 1024 * 1024
    )(in_specs=[SMEM] * 2 + [VMEM] * 6, out_specs=VMEM)(
        offsets, counts, observed, ku_t, kv_t, kv, model, halo
    )

    parts = lax.all_to_all(partial, "vis", 0, 0, tiled=True)
    own = jnp.sum(parts.astype(F32), axis=0)
    sent = own.astype(BF16)
    across = send(sent[:rows], lambda tile, view: (tiles - 1 - tile, view))
    beside = send(sent[rows - SUB :], lambda tile, view: (tiles - 2 - tile, view))
    before = send(sent[rows:], lambda tile, view: (tile + 1, view))
    after = send(sent[:SUB], lambda tile, view: (tile - 1, view))
    sign = jnp.where(view % 2 == 0, 1.0, -1.0).astype(F32)
    mine = lax.dynamic_index_in_dim(model, view, 0, keepdims=False)
    mine_halo = lax.dynamic_index_in_dim(halo, view, 0, keepdims=False)
    start = jnp.concatenate([mine, mine_halo], axis=0).astype(F32)
    pad = lambda value, low: jnp.pad(value.astype(F32), ((low, full - low - value.shape[0]), (0, 0)))
    summed = own + pad(before, 0) + pad(after, rows)
    mirrored = pad(flip(across), 0) + pad(flip(beside), rows - SUB)
    piece = (start + STEP * (summed + sign * mirrored)).astype(BF16)
    band = lax.all_gather(piece, "vis", axis=0, tiled=False)

    spill, tail = call(
        border_body,
        (sds((4, SUB, cols), BF16), sds((4, SUB, cols), F32)),
        scratch,
        flops=flops // 8,
        moved=4 * 1024 * 1024,
    )(in_specs=[SMEM] * 2 + [VMEM] * 5, out_specs=(VMEM, VMEM))(
        offsets, counts, observed, ku_t, kv_t, kv, band
    )
    spilled = send(spill, lambda tile, view: (tile + 1, view))
    partial = call(
        inside_body,
        sds((views, 4, quarter, cols), BF16),
        scratch,
        flops=flops,
        moved=4 * 1024 * 1024,
    )(in_specs=[SMEM] * 2 + [VMEM] * 6, out_specs=VMEM)(
        offsets, counts, observed, ku_t, kv_t, kv, band, tail
    )
    head = (partial[0, :, :SUB].astype(F32) + spilled.astype(F32)).astype(BF16)
    partial = lax.dynamic_update_slice(partial, head[None], (0, 0, 0, 0))
    parts = lax.all_to_all(partial, "vis", 0, 0, tiled=True)
    own = jnp.sum(parts.astype(F32), axis=0)
    across = send(own.astype(BF16), lambda tile, view: (tiles - 1 - tile, views - 1 - view))
    signs = jnp.array(SIGNS, F32)[:, None, None]
    start = lax.dynamic_slice_in_dim(band, view * quarter, quarter, 1).astype(F32)
    return (start + STEP * (own + signs * flip(across))).astype(BF16)


def solution(mesh):
    placed = (
        P(None, "tile", None),
        P(None, ("tile", "vis"), None),
        P(("tile", "vis"), None, None),
        P(("tile", "vis"), None),
        P(("tile", "vis")),
    )
    return jax.shard_map(
        on_device,
        mesh=mesh,
        in_specs=placed,
        out_specs=P(None, ("tile", "vis"), None),
        check_vma=False,
    )
```

time: 662 us -> 119 us (0.18)
  the two profiles are of different devices: /device:TPU:1 before, /device:TPU:96 now
where the time goes in v1:
time: 119 us; the launch traced here: 118 us
  waiting for transfers between devices  39.9 us (34%)
  starting transfers between devices  33.6 us (28%)
  blocking collectives  27.3 us (23%)
  Pallas kernels  9.36 us (8%)
  local copies, waits for them, and re-layouts  5.17 us (4%)
  other arithmetic  2.2 us (2%)
    ppermute x7, waiting for transfers between devices, send(): return lax.ppermute(value, ('tile', 'vis'), pairs)  29.4 us
    ppermute x7, starting transfers between devices, send(): return lax.ppermute(value, ('tile', 'vis'), pairs)  28.7 us
    all_gather x1, blocking collectives, on_device(): band = lax.all_gather(piece, 'vis', axis=0, tiled=False)  13.7 us
    all_to_all x1, blocking collectives, on_device(): parts = lax.all_to_all(partial, 'vis', 0, 0, tiled=True)  13.6 us
    all_to_all x1, waiting for transfers between devices, on_device(): parts = lax.all_to_all(partial, 'vis', 0, 0, tiled=True)  10.5 us
    all_to_all x1, starting transfers between devices, on_device(): parts = lax.all_to_all(partial, 'vis', 0, 0, tiled=True)  4.86 us
    pallas_call x1, Pallas kernels, on_device(): call(first_body, sds((4, full, cols), BF16), scratch, flops=flops, moved=...  3.59 us
    pallas_call x1, Pallas kernels, on_device(): call(inside_body, sds((views, 4, quarter, cols), BF16), scratch, flops=fl...  2.75 us
  transfers between devices with their start and end apart: 8, of which 4 were waited for; matrix products, arithmetic and copies ran while one was open for 2% of the time, Pallas kernels for 2%

profile of v1, /device:TPU:96, one launch (start us, length us, event | category | flops | bytes accessed | tf_op | source)
XLA Modules:
  0.0 118.3 jit_solution(11016661350928496980)
XLA Ops:
  0.0 0.9 slice.18
  0.9 1.9 %collective-permute-start = (bf16[4,64,128]{2,1,0:T(8,128)(2,1)S(1)}, bf16[4,64,128]{2,1,0:T(8,128)(2,1)S(1)}, u32[]{:S(2)}, u32[]{:S(2)}) collective-permute-start(bf16[4,64,128]{2,1,0:T(8,128)(2,1)S(1)} %slice.18), channel_id=1, source_target_pairs={{0,508},{1,509},{2,510},{3,511},{4,0},{5,1},{6,2},{7,3},{8,4},{9,5... | collective-permute-start | bytes 196616 | tf_op jit(solution)/shard_map/ppermute | solution.py:28
  2.8 0.8 copy.8.offsets
  4.3 1.2 %copy-done.2 = bf16[16,256,128]{2,1,0:T(8,128)(2,1)S(1)} copy-done((bf16[16,256,128]{2,1,0:T(8,128)(2,1)S(1)}, bf16[16,256,128]{2,1,0:T(8,128)(2,1)}, u32[]{:S(2)}) %copy-start.2) | copy-done | bytes 1048600
  5.5 2.0 %shard_map.64 = (bf16[16,64,256]{2,1,0:T(8,128)(2,1)S(1)}, bf16[16,128,256]{2,1,0:T(8,128)(2,1)S(1)}, bf16[16,256,128]{2,1,0:T(8,128)(2,1)S(1)}) custom-call(s32[16,2]{1,0:T(8,128)S(1)} %copy.8.offsets, bf16[16,256,128]{2,1,0:T(8,128)(2,1)S(1)} %copy-done.2), custom_call_target="tpu_custom_call" | custom-call | flops 335544320 | bytes 4194304 | tf_op jit(solution)/shard_map/pallas_call | solution.py:174
  7.6 3.6 %shard_map.65 = bf16[4,576,128]{2,1,0:T(8,128)(2,1)} custom-call(s32[16,2]{1,0:T(8,128)S(1)} %copy.8.offsets, s32[1]{0:T(128)S(6)} %copy.12.counts, bf16[4,16,256]{2,1,0:T(8,128)(2,1)S(1)} %copy-done.1, bf16[16,64,256]{2,1,0:T(8,128)(2,1)S(1)} %get-tuple-element.10.ku_t, bf16[16,128,256]{2,1,0:T(8,128)(2,1)S(1)} %get-tuple-element.11.kv_t, ...), custom_call_target="tpu_custom_call" | custom-call | flops 536870912 | bytes 4194304 | tf_op jit(solution)/shard_map/pallas_call | solution.py:185
  11.2 4.9 %all-to-all-start = ((bf16[4,576,128]{2,1,0:T(8,128)(2,1)}), bf16[4,576,128]{2,1,0:T(8,128)(2,1)}, u32[]{:S(2)}, u32[]{:S(2)}) async-start(bf16[4,576,128]{2,1,0:T(8,128)(2,1)} %shard_map.65), calls=%async_computation | async-start | bytes 1179648 | tf_op jit(solution)/shard_map/all_to_all | solution.py:191
  16.0 10.5 %all-to-all-done = bf16[4,576,128]{2,1,0:T(8,128)(2,1)} async-done(((bf16[4,576,128]{2,1,0:T(8,128)(2,1)}), bf16[4,576,128]{2,1,0:T(8,128)(2,1)}, u32[]{:S(2)}, u32[]{:S(2)}) %all-to-all-start) | async-done | bytes 589856 | tf_op jit(solution)/shard_map/all_to_all | solution.py:191
  26.5 1.2 convert_reduce_fusion
  27.7 0.7 slice.26
  28.4 11.2 %collective-permute-start.3 = (bf16[512,128]{1,0:T(8,128)(2,1)}, bf16[512,128]{1,0:T(8,128)(2,1)S(1)}, u32[]{:S(2)}, u32[]{:S(2)}) collective-permute-start(bf16[512,128]{1,0:T(8,128)(2,1)} %slice.26), channel_id=1, source_target_pairs={{0,508},{1,509},{2,510},{3,511},{4,504},{5,505},{6,506},{7,507},{8... | collective-permute-start | bytes 393224 | tf_op jit(solution)/shard_map/ppermute | solution.py:28
  40.2 5.1 %collective-permute-start.1 = (bf16[64,128]{1,0:T(8,128)(2,1)}, bf16[64,128]{1,0:T(8,128)(2,1)S(1)}, u32[]{:S(2)}, u32[]{:S(2)}) collective-permute-start(bf16[64,128]{1,0:T(8,128)(2,1)} %get-tuple-element.15), channel_id=1, source_target_pairs={{0,4},{1,5},{2,6},{3,7},{4,8},{5,9},{6,10},{7,11},{8,12},{9,13},{1... | collective-permute-start | bytes 49160 | tf_op jit(solution)/shard_map/ppermute | solution.py:28
  45.3 1.9 %collective-permute-start.2 = (bf16[64,128]{1,0:T(8,128)(2,1)S(1)}, bf16[64,128]{1,0:T(8,128)(2,1)S(1)}, u32[]{:S(2)}, u32[]{:S(2)}) collective-permute-start(bf16[64,128]{1,0:T(8,128)(2,1)S(1)} %get-tuple-element.16), channel_id=1, source_target_pairs={{0,508},{1,509},{2,510},{3,511},{4,0},{5,1},{6,2},{7,3},{8,4},{9,5... | collective-permute-start | bytes 49160 | tf_op jit(solution)/shard_map/ppermute | solution.py:28
  47.2 4.7 %collective-permute-start.4 = (bf16[128,128]{1,0:T(8,128)(2,1)S(1)}, bf16[128,128]{1,0:T(8,128)(2,1)S(1)}, u32[]{:S(2)}, u32[]{:S(2)}) collective-permute-start(bf16[128,128]{1,0:T(8,128)(2,1)S(1)} %slice.27), channel_id=1, source_target_pairs={{0,504},{1,505},{2,506},{3,507},{4,500},{5,501},{6,502},{7,503},{8... | collective-permute-start | bytes 98312 | tf_op jit(solution)/shard_map/ppermute | solution.py:28
  52.0 9.7 %collective-permute-done.4 = bf16[128,128]{1,0:T(8,128)(2,1)S(1)} collective-permute-done((bf16[128,128]{1,0:T(8,128)(2,1)S(1)}, bf16[128,128]{1,0:T(8,128)(2,1)S(1)}, u32[]{:S(2)}, u32[]{:S(2)}) %collective-permute-start.4) | collective-permute-done | bytes 32800 | tf_op jit(solution)/shard_map/ppermute | solution.py:28
  62.4 13.7 %all-gather = bf16[2304,128]{1,0:T(8,128)(2,1)S(1)} all-gather(bf16[576,128]{1,0:T(8,128)(2,1)S(1)} %add_convert_fusion), channel_id=2, replica_groups=mesh['tile'=128,'vis'=4] {'vis'}, dimensions={0}, use_global_device_ids=true | all-gather | bytes 737280 | tf_op jit(solution)/shard_map/all_gather | solution.py:206
  76.1 1.0 shard_map.66
  77.0 2.8 %shard_map.67 = bf16[4,4,128,128]{3,2,1,0:T(8,128)(2,1)S(1)} custom-call(s32[16,2]{1,0:T(8,128)S(1)} %copy.8.offsets, s32[1]{0:T(128)S(6)} %copy.12.counts, bf16[4,16,256]{2,1,0:T(8,128)(2,1)S(1)} %copy-done.1, bf16[16,64,256]{2,1,0:T(8,128)(2,1)S(1)} %get-tuple-element.10.ku_t, bf16[16,128,256]{2,1,0:T(8,128)(2,1)S(1)} %get-tuple-element.11.kv_t, ...), custom_call_target="tpu_custom_call" | custom-call | flops 536870912 | bytes 4194304 | tf_op jit(solution)/shard_map/pallas_call | solution.py:218
  79.8 1.9 %collective-permute-start.5 = (bf16[4,64,128]{2,1,0:T(8,128)(2,1)S(1)}, bf16[4,64,128]{2,1,0:T(8,128)(2,1)S(1)}, u32[]{:S(2)}, u32[]{:S(2)}) collective-permute-start(bf16[4,64,128]{2,1,0:T(8,128)(2,1)S(1)} %get-tuple-element.14), channel_id=1, source_target_pairs={{0,4},{1,5},{2,6},{3,7},{4,8},{5,9},{6,10},{7,11},{8,12},{9,13},{1... | collective-permute-start | bytes 196616 | tf_op jit(solution)/shard_map/ppermute | solution.py:28
  81.7 3.6 %collective-permute-done.5 = bf16[4,64,128]{2,1,0:T(8,128)(2,1)S(1)} collective-permute-done((bf16[4,64,128]{2,1,0:T(8,128)(2,1)S(1)}, bf16[4,64,128]{2,1,0:T(8,128)(2,1)S(1)}, u32[]{:S(2)}, u32[]{:S(2)}) %collective-permute-start.5) | collective-permute-done | bytes 65568 | tf_op jit(solution)/shard_map/ppermute | solution.py:28
  85.4 13.6 %all_to_all.10 = bf16[4,4,128,128]{3,2,1,0:T(8,128)(2,1)S(1)} all-to-all(bf16[4,4,128,128]{3,2,1,0:T(8,128)(2,1)S(1)} %fusion.2), channel_id=1, replica_groups=mesh['tile'=128,'vis'=4] {'vis'}, dimensions={0} | all-to-all | bytes 1048576 | tf_op jit(solution)/shard_map/all_to_all | solution.py:229
  99.2 1.9 %collective-permute-start.6 = (bf16[4,128,128]{2,1,0:T(8,128)(2,1)S(1)}, bf16[4,128,128]{2,1,0:T(8,128)(2,1)S(1)}, u32[]{:S(2)}, u32[]{:S(2)}) collective-permute-start(bf16[4,128,128]{2,1,0:T(8,128)(2,1)S(1)} %convert_element_type.61), channel_id=1, source_target_pairs={{0,511},{1,510},{2,509},{3,508},{4,507},{5,506},{6,505},{7,504},{8... | collective-permute-start | bytes 393224 | tf_op jit(solution)/shard_map/ppermute | solution.py:28
  101.1 16.0 %collective-permute-done.6 = bf16[4,128,128]{2,1,0:T(8,128)(2,1)S(1)} collective-permute-done((bf16[4,128,128]{2,1,0:T(8,128)(2,1)S(1)}, bf16[4,128,128]{2,1,0:T(8,128)(2,1)S(1)}, u32[]{:S(2)}, u32[]{:S(2)}) %collective-permute-start.6) | collective-permute-done | bytes 131104 | tf_op jit(solution)/shard_map/ppermute | solution.py:28
  117.5 0.8 add_convert_fusion.1
  (24 shorter events, 1.9 us)
Async XLA Ops:
  0.0 7.5 %copy-start = (bf16[4,512,128]{2,1,0:T(8,128)(2,1)S(1)}, bf16[4,512,128]{2,1,0:T(8,128)(2,1)}, u32[]{:S(2)}) copy-start(bf16[4,512,128]{2,1,0:T(8,128)(2,1)} %model.1) | copy-start | bytes 1572868
  0.0 7.5 %copy-start.1 = (bf16[4,16,256]{2,1,0:T(8,128)(2,1)S(1)}, bf16[4,16,256]{2,1,0:T(8,128)(2,1)}, u32[]{:S(2)}) copy-start(bf16[4,16,256]{2,1,0:T(8,128)(2,1)} %observed.5) | copy-start | bytes 98308
  0.9 6.6 %collective-permute-start = (bf16[4,64,128]{2,1,0:T(8,128)(2,1)S(1)}, bf16[4,64,128]{2,1,0:T(8,128)(2,1)S(1)}, u32[]{:S(2)}, u32[]{:S(2)}) collective-permute-start(bf16[4,64,128]{2,1,0:T(8,128)(2,1)S(1)} %slice.18), channel_id=1, source_target_pairs={{0,508},{1,509},{2,510},{3,511},{4,0},{5,1},{6,2},{7,3},{8,4},{9,5... | collective-permute-start | bytes 196616 | tf_op jit(solution)/shard_map/ppermute | solution.py:28
  4.2 1.2 %copy-start.2 = (bf16[16,256,128]{2,1,0:T(8,128)(2,1)S(1)}, bf16[16,256,128]{2,1,0:T(8,128)(2,1)}, u32[]{:S(2)}) copy-start(bf16[16,256,128]{2,1,0:T(8,128)(2,1)} %kern.1) | copy-start | bytes 3145732
  11.2 15.3 %all-to-all-start = ((bf16[4,576,128]{2,1,0:T(8,128)(2,1)}), bf16[4,576,128]{2,1,0:T(8,128)(2,1)}, u32[]{:S(2)}, u32[]{:S(2)}) async-start(bf16[4,576,128]{2,1,0:T(8,128)(2,1)} %shard_map.65), calls=%async_computation | async-start | bytes 1179648 | tf_op jit(solution)/shard_map/all_to_all | solution.py:191
  28.4 33.5 %collective-permute-start.3 = (bf16[512,128]{1,0:T(8,128)(2,1)}, bf16[512,128]{1,0:T(8,128)(2,1)S(1)}, u32[]{:S(2)}, u32[]{:S(2)}) collective-permute-start(bf16[512,128]{1,0:T(8,128)(2,1)} %slice.26), channel_id=1, source_target_pairs={{0,508},{1,509},{2,510},{3,511},{4,504},{5,505},{6,506},{7,507},{8... | collective-permute-start | bytes 393224 | tf_op jit(solution)/shard_map/ppermute | solution.py:28
  40.2 22.1 %collective-permute-start.1 = (bf16[64,128]{1,0:T(8,128)(2,1)}, bf16[64,128]{1,0:T(8,128)(2,1)S(1)}, u32[]{:S(2)}, u32[]{:S(2)}) collective-permute-start(bf16[64,128]{1,0:T(8,128)(2,1)} %get-tuple-element.15), channel_id=1, source_target_pairs={{0,4},{1,5},{2,6},{3,7},{4,8},{5,9},{6,10},{7,11},{8,12},{9,13},{1... | collective-permute-start | bytes 49160 | tf_op jit(solution)/shard_map/ppermute | solution.py:28
  45.3 17.0 %collective-permute-start.2 = (bf16[64,128]{1,0:T(8,128)(2,1)S(1)}, bf16[64,128]{1,0:T(8,128)(2,1)S(1)}, u32[]{:S(2)}, u32[]{:S(2)}) collective-permute-start(bf16[64,128]{1,0:T(8,128)(2,1)S(1)} %get-tuple-element.16), channel_id=1, source_target_pairs={{0,508},{1,509},{2,510},{3,511},{4,0},{5,1},{6,2},{7,3},{8,4},{9,5... | collective-permute-start | bytes 49160 | tf_op jit(solution)/shard_map/ppermute | solution.py:28
  47.2 14.5 %collective-permute-start.4 = (bf16[128,128]{1,0:T(8,128)(2,1)S(1)}, bf16[128,128]{1,0:T(8,128)(2,1)S(1)}, u32[]{:S(2)}, u32[]{:S(2)}) collective-permute-start(bf16[128,128]{1,0:T(8,128)(2,1)S(1)} %slice.27), channel_id=1, source_target_pairs={{0,504},{1,505},{2,506},{3,507},{4,500},{5,501},{6,502},{7,503},{8... | collective-permute-start | bytes 98312 | tf_op jit(solution)/shard_map/ppermute | solution.py:28
  79.8 5.6 %collective-permute-start.5 = (bf16[4,64,128]{2,1,0:T(8,128)(2,1)S(1)}, bf16[4,64,128]{2,1,0:T(8,128)(2,1)S(1)}, u32[]{:S(2)}, u32[]{:S(2)}) collective-permute-start(bf16[4,64,128]{2,1,0:T(8,128)(2,1)S(1)} %get-tuple-element.14), channel_id=1, source_target_pairs={{0,4},{1,5},{2,6},{3,7},{4,8},{5,9},{6,10},{7,11},{8,12},{9,13},{1... | collective-permute-start | bytes 196616 | tf_op jit(solution)/shard_map/ppermute | solution.py:28
  85.4 32.1 %copy-start.3 = (f32[4]{0:T(128)S(1)}, f32[4]{0:T(128)}, u32[]{:S(2)}) copy-start(f32[4]{0:T(128)} %constant.45.clone) | copy-start | bytes 52
  99.2 17.9 %collective-permute-start.6 = (bf16[4,128,128]{2,1,0:T(8,128)(2,1)S(1)}, bf16[4,128,128]{2,1,0:T(8,128)(2,1)S(1)}, u32[]{:S(2)}, u32[]{:S(2)}) collective-permute-start(bf16[4,128,128]{2,1,0:T(8,128)(2,1)S(1)} %convert_element_type.61), channel_id=1, source_target_pairs={{0,511},{1,510},{2,509},{3,508},{4,507},{5,506},{6,505},{7,504},{8... | collective-permute-start | bytes 393224 | tf_op jit(solution)/shard_map/ppermute | solution.py:28

commit v2 on v1

--- a/solution.py
+++ b/solution.py
@@ -112,42 +112,106 @@
     return lax.fori_loop(0, blocks, add, 0)
 
 
-def first_body(offsets, counts, observed, ku_t, kv_t, kv, model, halo, out, picks, obs, grid, acc):
+def first_body(
+    offsets, counts, observed, where, ku_t, kv_t, kv, model, halo, out, picks, obs, grid, acc
+):
     rows = model.shape[1]
+    full = rows + SUB
+    blocks = ku_t.shape[0]
+    for half in range(2):
+        low = full + half * blocks
+        out[:, low : low + blocks] = observed[:, :, half * 128 : (half + 1) * 128]
+    for comp in range(4):
+        out[comp, full + 2 * blocks :] = where[...]
     obs[...] = observed[...].astype(F32)
     grid[:, :rows] = model[...].astype(F32)
     grid[:, rows:] = halo[...].astype(F32)
     acc[...] = jnp.zeros_like(acc)
     limit = choose(picks, counts, offsets, ku_t.shape[0], lambda row: row >= 0)
     grid_blocks(picks, limit, offsets, obs, ku_t, kv_t, kv, grid, acc)
-    out[...] = acc[...].astype(BF16)
-
-
-def border_body(offsets, counts, observed, ku_t, kv_t, kv, model, spill, tail, picks, obs, grid, acc):
-    rows = model.shape[1] - SUB
-    base = rows - SUB
-    obs[...] = observed[...].astype(F32)
+    out[:, :full] = acc[...].astype(BF16)
+
+
+def lone_blocks(picks, limit, rows, cols, obs, kern, grid, acc):
+    lanes = grid.shape[1]
+    high = lax.broadcasted_iota(jnp.int32, (SUB, lanes), 1) >= SUB
+    pick = jnp.where(
+        lax.broadcasted_iota(jnp.int32, (SUB, lanes), 0)
+        == lax.broadcasted_iota(jnp.int32, (SUB, lanes), 1),
+        1.0,
+        0.0,
+    ).astype(BF16)
+
+    def group(index, carry):
+        staged = []
+        for lane in range(GROUP):
+            place = index * GROUP + lane
+            live = place < limit
+            block = picks[jnp.minimum(place, limit - 1)]
+            row = rows[block]
+            col = cols[block]
+            patch = pltpu.roll(grid[pl.ds(row, SUB), :], SUB - col, 1)
+            patch = jnp.where(high, patch, 0.0).astype(BF16)
+            weights = kern[block]
+            both = dot_nt(jnp.concatenate([pick, patch], axis=0), weights)
+            along_u = both[:SUB]
+            seen = jnp.sum(along_u * both[SUB:], axis=0, keepdims=True)
+            left = jnp.where(live, obs[pl.ds(block, 1), :] - seen, 0.0)
+            fresh = dot_nn((along_u * left).astype(BF16), weights)
+            fresh = pltpu.roll(jnp.where(high, fresh, 0.0), (SUB + col) % lanes, 1)
+            staged.append((row, fresh))
+        for row, fresh in staged:
+            acc[pl.ds(row, SUB), :] += fresh
+        return carry
+
+    lax.fori_loop(0, (limit + GROUP - 1) // GROUP, group, 0)
+
+
+def choose_rows(picks, rows, keep):
+    def add(block, found):
+        row = rows[block]
+        good = (row >= 0) & keep(row)
+
+        @pl.when(good)
+        def _():
+            picks[found] = block
+
+        return found + good.astype(jnp.int32)
+
+    return lax.fori_loop(0, rows.shape[0], add, 0)
+
+
+def spread(observed, obs):
+    blocks = observed.shape[1] // 2
+    for source in range(observed.shape[0]):
+        for half in range(2):
+            obs[source * blocks : (source + 1) * blocks, half * 128 : (half + 1) * 128] = observed[
+                source, half * blocks : (half + 1) * blocks
+            ].astype(F32)
+
+
+def border_body(rows, cols, observed, kern, model, spill, tail, picks, obs, grid, acc):
+    band = model.shape[0] - SUB
+    base = band - SUB
+    spread(observed, obs)
     grid[...] = model[...].astype(F32)
-    acc[:, base:] = jnp.zeros((4, 2 * SUB, acc.shape[2]), F32)
-    limit = choose(picks, counts, offsets, ku_t.shape[0], lambda row: row > base)
-    grid_blocks(picks, limit, offsets, obs, ku_t, kv_t, kv, grid, acc)
-    spill[...] = acc[:, rows:].astype(BF16)
-    tail[...] = acc[:, base:rows]
-
-
-def inside_body(offsets, counts, observed, ku_t, kv_t, kv, model, tail, out, picks, obs, grid, acc):
-    rows = model.shape[1] - SUB
-    base = rows - SUB
-    obs[...] = observed[...].astype(F32)
+    acc[base:] = jnp.zeros((2 * SUB, acc.shape[1]), F32)
+    limit = choose_rows(picks, rows, lambda row: row > base)
+    lone_blocks(picks, limit, rows, cols, obs, kern, grid, acc)
+    spill[...] = acc[band:].astype(BF16)
+    tail[...] = acc[base:band]
+
+
+def inside_body(rows, cols, observed, kern, model, tail, out, picks, obs, grid, acc):
+    band = model.shape[0] - SUB
+    base = band - SUB
+    spread(observed, obs)
     grid[...] = model[...].astype(F32)
-    acc[:, :base] = jnp.zeros((4, base, acc.shape[2]), F32)
-    acc[:, base:rows] = tail[...]
-    limit = choose(picks, counts, offsets, ku_t.shape[0], lambda row: row <= base)
-    grid_blocks(picks, limit, offsets, obs, ku_t, kv_t, kv, grid, acc)
-    views = out.shape[0]
-    quarter = rows // views
-    for view in range(views):
-        out[view] = acc[:, view * quarter : (view + 1) * quarter].astype(BF16)
+    acc[:base] = jnp.zeros((base, acc.shape[1]), F32)
+    acc[base:band] = tail[...]
+    limit = choose_rows(picks, rows, lambda row: row <= base)
+    lone_blocks(picks, limit, rows, cols, obs, kern, grid, acc)
+    out[...] = acc[:band]
 
 
 def flip(value):
@@ -170,6 +234,10 @@
         pltpu.VMEM((4, full, cols), F32),
     ]
 
+    every = lax.all_gather(kernels, "vis", axis=0, tiled=True)
+    live = (jnp.arange(blocks, dtype=jnp.int32) < counts[0]).astype(jnp.int32)
+    where = jnp.stack([offsets[:, 0] // 16, offsets[:, 0] % 16, offsets[:, 1], live], axis=1)
+    where = jnp.pad(where, ((0, 0), (0, cols - 4))).astype(BF16)
     halo = send(model[:, :SUB], lambda tile, view: (tile - 1, view))
     ku_t, kv_t, kv = call(
         prepare_body,
@@ -183,13 +251,21 @@
     )(in_specs=[SMEM, VMEM], out_specs=(VMEM,) * 3)(offsets, kernels)
     flops = 4 * 2 * blocks * depth * cols * SUB * 2
     partial = call(
-        first_body, sds((4, full, cols), BF16), scratch, flops=flops, moved=4 * 1024 * 1024
-    )(in_specs=[SMEM] * 2 + [VMEM] * 6, out_specs=VMEM)(
-        offsets, counts, observed, ku_t, kv_t, kv, model, halo
+        first_body,
+        sds((4, full + 3 * blocks, cols), BF16),
+        scratch,
+        flops=flops,
+        moved=4 * 1024 * 1024,
+    )(in_specs=[SMEM] * 2 + [VMEM] * 7, out_specs=VMEM)(
+        offsets, counts, observed, where, ku_t, kv_t, kv, model, halo
     )
 
     parts = lax.all_to_all(partial, "vis", 0, 0, tiled=True)
-    own = jnp.sum(parts.astype(F32), axis=0)
+    own = jnp.sum(parts[:, :full].astype(F32), axis=0)
+    seen = parts[:, full : full + 2 * blocks]
+    where = parts[:, full + 2 * blocks :, :4].astype(jnp.int32).reshape(-1, 4)
+    block_rows = jnp.where(where[:, 3] > 0, where[:, 0] * 16 + where[:, 1], -1)
+    block_cols = where[:, 2]
     sent = own.astype(BF16)
     across = send(sent[:rows], lambda tile, view: (tiles - 1 - tile, view))
     beside = send(sent[rows - SUB :], lambda tile, view: (tiles - 2 - tile, view))
@@ -203,35 +279,47 @@
     summed = own + pad(before, 0) + pad(after, rows)
     mirrored = pad(flip(across), 0) + pad(flip(beside), rows - SUB)
     piece = (start + STEP * (summed + sign * mirrored)).astype(BF16)
-    band = lax.all_gather(piece, "vis", axis=0, tiled=False)
-
+
+    scratch = [
+        pltpu.SMEM((views * blocks,), jnp.int32),
+        pltpu.VMEM((views * blocks, depth), F32),
+        pltpu.VMEM((full, cols), F32),
+        pltpu.VMEM((full, cols), F32),
+    ]
     spill, tail = call(
         border_body,
-        (sds((4, SUB, cols), BF16), sds((4, SUB, cols), F32)),
+        (sds((SUB, cols), BF16), sds((SUB, cols), F32)),
         scratch,
         flops=flops // 8,
-        moved=4 * 1024 * 1024,
-    )(in_specs=[SMEM] * 2 + [VMEM] * 5, out_specs=(VMEM, VMEM))(
-        offsets, counts, observed, ku_t, kv_t, kv, band
+        moved=6 * 1024 * 1024,
+    )(in_specs=[SMEM] * 2 + [VMEM] * 3, out_specs=(VMEM, VMEM))(
+        block_rows, block_cols, seen, every, piece
     )
     spilled = send(spill, lambda tile, view: (tile + 1, view))
-    partial = call(
-        inside_body,
-        sds((views, 4, quarter, cols), BF16),
-        scratch,
-        flops=flops,
-        moved=4 * 1024 * 1024,
-    )(in_specs=[SMEM] * 2 + [VMEM] * 6, out_specs=VMEM)(
-        offsets, counts, observed, ku_t, kv_t, kv, band, tail
-    )
-    head = (partial[0, :, :SUB].astype(F32) + spilled.astype(F32)).astype(BF16)
-    partial = lax.dynamic_update_slice(partial, head[None], (0, 0, 0, 0))
-    parts = lax.all_to_all(partial, "vis", 0, 0, tiled=True)
-    own = jnp.sum(parts.astype(F32), axis=0)
-    across = send(own.astype(BF16), lambda tile, view: (tiles - 1 - tile, views - 1 - view))
+    own = call(
+        inside_body, sds((rows, cols), F32), scratch, flops=flops, moved=6 * 1024 * 1024
+    )(in_specs=[SMEM] * 2 + [VMEM] * 4, out_specs=VMEM)(
+        block_rows, block_cols, seen, every, piece, tail
+    )
+    own = own + jnp.pad(spilled.astype(F32), ((0, rows - SUB), (0, 0)))
+    near = (piece[:rows].astype(F32) + STEP * own).astype(BF16).reshape(views, quarter, cols)
+    far = own.astype(BF16).reshape(views, quarter, cols)[::-1]
+
+    tile = lax.axis_index("tile")
+    low = tile < tiles // 2
+    groups = []
+    for one in range(tiles // 2):
+        groups.append(
+            [pick * views + member for pick in (one, tiles - 1 - one) for member in range(views)]
+        )
+    packed = jnp.where(
+        low, jnp.concatenate([near, far], axis=0), jnp.concatenate([far, near], axis=0)
+    )
+    got = lax.all_to_all(packed, ("tile", "vis"), 0, 0, axis_index_groups=groups, tiled=True)
     signs = jnp.array(SIGNS, F32)[:, None, None]
-    start = lax.dynamic_slice_in_dim(band, view * quarter, quarter, 1).astype(F32)
-    return (start + STEP * (own + signs * flip(across))).astype(BF16)
+    near = jnp.where(low, got[:views], got[views:])
+    far = jnp.where(low, got[views:], got[:views])
+    return (near.astype(F32) + STEP * signs * flip(far)).astype(BF16)
 
 
 def solution(mesh):

time: 119 us -> 131 us (1.10)
  the two profiles are of different devices: /device:TPU:96 before, /device:TPU:1 now
where the time goes in v2:
time: 131 us; the launch traced here: 130 us
  starting transfers between devices  34 us (26%)
  waiting for transfers between devices  25.7 us (20%)
  blocking collectives  23.7 us (18%)
  Pallas kernels  20.8 us (16%)
  between operations  14.3 us (11%)
  local copies, waits for them, and re-layouts  9.3 us (7%)
  other arithmetic  2.46 us (2%)
    ppermute x6, starting transfers between devices, send(): return lax.ppermute(value, ('tile', 'vis'), pairs)  30.5 us
    all_to_all x1, blocking collectives, on_device(): lax.all_to_all(packed, ('tile', 'vis'), 0, 0, axis_index_groups=groups, t...  23.7 us
    all_to_all x1, waiting for transfers between devices, on_device(): parts = lax.all_to_all(partial, 'vis', 0, 0, tiled=True)  13.9 us
    ppermute x6, waiting for transfers between devices, send(): return lax.ppermute(value, ('tile', 'vis'), pairs)  11.1 us
    pallas_call x1, Pallas kernels, on_device(): call(inside_body, sds((rows, cols), F32), scratch, flops=flops, moved=6 *...  9.87 us
    unnamed x15, local copies, waits for them, and re-layouts  6.28 us
    pallas_call x1, Pallas kernels, on_device(): call(border_body, (sds((SUB, cols), BF16), sds((SUB, cols), F32)), scratc...  4.69 us
    pallas_call x1, Pallas kernels, on_device(): call(first_body, sds((4, full + 3 * blocks, cols), BF16), scratch, flops=...  4.17 us
  transfers between devices with their start and end apart: 8, of which 2 were waited for; matrix products, arithmetic and copies ran while one was open for 4% of the time, Pallas kernels for 12%

profile of v2, /device:TPU:1, one launch (start us, length us, event | category | flops | bytes accessed | tf_op | source)
XLA Modules:
  0.0 130.3 jit_solution(10196430004194629582)
XLA Ops:
  6.5 0.7 all-gather.2.cloned.1.call-update
  7.3 0.8 slice.55
  8.1 8.8 %collective-permute-start = (bf16[4,64,128]{2,1,0:T(8,128)(2,1)S(1)}, bf16[4,64,128]{2,1,0:T(8,128)(2,1)S(1)}, u32[]{:S(2)}, u32[]{:S(2)}) collective-permute-start(bf16[4,64,128]{2,1,0:T(8,128)(2,1)S(1)} %slice.55), channel_id=1, source_target_pairs={{0,508},{1,509},{2,510},{3,511},{4,0},{5,1},{6,2},{7,3},{8,4},{9,5... | collective-permute-start | bytes 196616 | tf_op jit(solution)/shard_map/ppermute | solution.py:28
  18.2 0.7 fusion.4
  19.0 0.8 copy.17.offsets
  19.8 1.2 copy-done.1
  21.0 2.0 %shard_map.64 = (bf16[16,64,256]{2,1,0:T(8,128)(2,1)S(1)}, bf16[16,128,256]{2,1,0:T(8,128)(2,1)S(1)}, bf16[16,256,128]{2,1,0:T(8,128)(2,1)S(1)}) custom-call(s32[16,2]{1,0:T(8,128)S(1)} %copy.17.offsets, bf16[16,256,128]{2,1,0:T(8,128)(2,1)S(1)} %copy-done.1), custom_call_target="tpu_custom_call" | custom-call | flops 335544320 | bytes 4194304 | tf_op jit(solution)/shard_map/pallas_call | solution.py:242
  23.1 1.0 copy-done.2
  24.2 0.8 copy-done.3
  24.9 4.2 %shard_map.65 = bf16[4,624,128]{2,1,0:T(8,128)(2,1)} custom-call(s32[16,2]{1,0:T(8,128)S(1)} %copy.17.offsets, s32[1]{0:T(128)} %copy.26.counts, bf16[4,16,256]{2,1,0:T(8,128)(2,1)S(1)} %copy-done.3, bf16[16,128]{1,0:T(8,128)(2,1)S(1)} %pad.40.where, bf16[16,64,256]{2,1,0:T(8,128)(2,1)S(1)} %get-tuple-element.10.ku_t, ...), custom_call_target="tpu_custom_call" | custom-call | flops 536870912 | bytes 4194304 | tf_op jit(solution)/shard_map/pallas_call | solution.py:253
  29.1 3.5 %all-to-all-start = ((bf16[4,624,128]{2,1,0:T(8,128)(2,1)}), bf16[4,624,128]{2,1,0:T(8,128)(2,1)S(1)}, u32[]{:S(2)}, u32[]{:S(2)}) async-start(bf16[4,624,128]{2,1,0:T(8,128)(2,1)} %shard_map.65), calls=%async_computation | async-start | bytes 1277952 | tf_op jit(solution)/shard_map/all_to_all | solution.py:263
  32.6 0.9 dynamic-slice_bitcast_fusion
  33.6 13.9 %all-to-all-done = bf16[4,624,128]{2,1,0:T(8,128)(2,1)S(1)} async-done(((bf16[4,624,128]{2,1,0:T(8,128)(2,1)}), bf16[4,624,128]{2,1,0:T(8,128)(2,1)S(1)}, u32[]{:S(2)}, u32[]{:S(2)}) %all-to-all-start) | async-done | bytes 639008 | tf_op jit(solution)/shard_map/all_to_all | solution.py:263
  47.6 1.9 %collective-permute-start.1 = (bf16[64,128]{1,0:T(8,128)(2,1)S(1)}, bf16[64,128]{1,0:T(8,128)(2,1)S(1)}, u32[]{:S(2)}, u32[]{:S(2)}) collective-permute-start(bf16[64,128]{1,0:T(8,128)(2,1)S(1)} %get-tuple-element.19), channel_id=1, source_target_pairs={{0,4},{1,5},{2,6},{3,7},{4,8},{5,9},{6,10},{7,11},{8,12},{9,13},{1... | collective-permute-start | bytes 49160 | tf_op jit(solution)/shard_map/ppermute | solution.py:28
  49.5 10.2 %collective-permute-start.2 = (bf16[64,128]{1,0:T(8,128)(2,1)S(1)}, bf16[64,128]{1,0:T(8,128)(2,1)S(1)}, u32[]{:S(2)}, u32[]{:S(2)}) collective-permute-start(bf16[64,128]{1,0:T(8,128)(2,1)S(1)} %get-tuple-element.20), channel_id=1, source_target_pairs={{0,508},{1,509},{2,510},{3,511},{4,0},{5,1},{6,2},{7,3},{8,4},{9,5... | collective-permute-start | bytes 49160 | tf_op jit(solution)/shard_map/ppermute | solution.py:28
  59.7 5.8 %collective-permute-start.3 = (bf16[512,128]{1,0:T(8,128)(2,1)S(1)}, bf16[512,128]{1,0:T(8,128)(2,1)S(1)}, u32[]{:S(2)}, u32[]{:S(2)}) collective-permute-start(bf16[512,128]{1,0:T(8,128)(2,1)S(1)} %slice.75), channel_id=1, source_target_pairs={{0,508},{1,509},{2,510},{3,511},{4,504},{5,505},{6,506},{7,507},{8... | collective-permute-start | bytes 393224 | tf_op jit(solution)/shard_map/ppermute | solution.py:28
  65.5 1.9 %collective-permute-start.4 = (bf16[128,128]{1,0:T(8,128)(2,1)S(1)}, bf16[128,128]{1,0:T(8,128)(2,1)S(1)}, u32[]{:S(2)}, u32[]{:S(2)}) collective-permute-start(bf16[128,128]{1,0:T(8,128)(2,1)S(1)} %slice.76), channel_id=1, source_target_pairs={{0,504},{1,505},{2,506},{3,507},{4,500},{5,501},{6,502},{7,503},{8... | collective-permute-start | bytes 98312 | tf_op jit(solution)/shard_map/ppermute | solution.py:28
  67.9 11.1 %collective-permute-done.4 = bf16[128,128]{1,0:T(8,128)(2,1)S(1)} collective-permute-done((bf16[128,128]{1,0:T(8,128)(2,1)S(1)}, bf16[128,128]{1,0:T(8,128)(2,1)S(1)}, u32[]{:S(2)}, u32[]{:S(2)}) %collective-permute-start.4) | collective-permute-done | bytes 32800 | tf_op jit(solution)/shard_map/ppermute | solution.py:28
  79.7 2.2 %copy-done = bf16[64,256,128]{2,1,0:T(8,128)(2,1)S(1)} copy-done((bf16[64,256,128]{2,1,0:T(8,128)(2,1)S(1)}, bf16[64,256,128]{2,1,0:T(8,128)(2,1)}, u32[]{:S(2)}) %copy-start) | copy-done | bytes 4194328
  81.9 4.7 %shard_map.66 = (bf16[64,128]{1,0:T(8,128)(2,1)S(1)}, f32[64,128]{1,0:T(8,128)S(1)}) custom-call(s32[64]{0:T(128)S(1)} %fusion.3.rows, s32[64]{0:T(128)S(1)} %bitcast.14, bf16[4,32,128]{2,1,0:T(8,128)(2,1)S(1)} %slice.83.observed, bf16[64,256,128]{2,1,0:T(8,128)(2,1)S(1)} %copy-done, bf16[576,128]{1,0:T(8,128)(2,1)S(1)} %add_convert_fusion.model), custom_call_target="tpu_custom_call" | custom-call | flops 67108864 | bytes 6291456 | tf_op jit(solution)/shard_map/pallas_call | solution.py:289
  86.6 1.9 %collective-permute-start.5 = (bf16[64,128]{1,0:T(8,128)(2,1)S(1)}, bf16[64,128]{1,0:T(8,128)(2,1)S(1)}, u32[]{:S(2)}, u32[]{:S(2)}) collective-permute-start(bf16[64,128]{1,0:T(8,128)(2,1)S(1)} %get-tuple-element.14), channel_id=1, source_target_pairs={{0,4},{1,5},{2,6},{3,7},{4,8},{5,9},{6,10},{7,11},{8,12},{9,13},{1... | collective-permute-start | bytes 49160 | tf_op jit(solution)/shard_map/ppermute | solution.py:28
  88.5 9.9 %shard_map.67 = f32[512,128]{1,0:T(8,128)S(1)} custom-call(s32[64]{0:T(128)S(1)} %fusion.3.rows, s32[64]{0:T(128)S(1)} %bitcast.15, bf16[4,32,128]{2,1,0:T(8,128)(2,1)S(1)} %slice.83.observed, bf16[64,256,128]{2,1,0:T(8,128)(2,1)S(1)} %copy-done, bf16[576,128]{1,0:T(8,128)(2,1)S(1)} %add_convert_fusion.model, f32[64,128]{1,0:T(8,128)S(1)} %get-tuple-element.13.tail), custom_call_target="tpu_custom_call" | custom-call | flops 536870912 | bytes 6291456 | tf_op jit(solution)/shard_map/pallas_call | solution.py:299
  98.5 23.7 %all_to_all.10 = bf16[8,128,128]{2,1,0:T(8,128)(2,1)S(1)} all-to-all(bf16[8,128,128]{2,1,0:T(8,128)(2,1)S(1)} %maximum_select_fusion), channel_id=1, replica_groups={{0,1,2,3,508,509,510,511},{4,5,6,7,504,505,506,507},{8,9,10,11,500,501,..., dimensions={0} | all-to-all | bytes 524288 | tf_op jit(solution)/shard_map/all_to_all | solution.py:318
  122.7 0.8 add_convert_fusion.1
  (43 shorter events, 2.6 us)
Async XLA Ops:
  6.5 73.1 %all-gather.2.cloned.1.call-start = ((), (), s32[]{:S(2)}) async-start(), calls=%async_computation.2 | async-start | bytes 5242880 | tf_op jit(solution)/shard_map/all_gather | solution.py:237
  8.1 15.0 %collective-permute-start = (bf16[4,64,128]{2,1,0:T(8,128)(2,1)S(1)}, bf16[4,64,128]{2,1,0:T(8,128)(2,1)S(1)}, u32[]{:S(2)}, u32[]{:S(2)}) collective-permute-start(bf16[4,64,128]{2,1,0:T(8,128)(2,1)S(1)} %slice.55), channel_id=1, source_target_pairs={{0,508},{1,509},{2,510},{3,511},{4,0},{5,1},{6,2},{7,3},{8,4},{9,5... | collective-permute-start | bytes 196616 | tf_op jit(solution)/shard_map/ppermute | solution.py:28
  19.8 1.2 copy-start.1
  23.1 1.0 copy-start.2
  24.2 0.8 copy-start.3
  29.1 18.3 %all-to-all-start = ((bf16[4,624,128]{2,1,0:T(8,128)(2,1)}), bf16[4,624,128]{2,1,0:T(8,128)(2,1)S(1)}, u32[]{:S(2)}, u32[]{:S(2)}) async-start(bf16[4,624,128]{2,1,0:T(8,128)(2,1)} %shard_map.65), calls=%async_computation | async-start | bytes 1277952 | tf_op jit(solution)/shard_map/all_to_all | solution.py:263
  47.6 32.0 %collective-permute-start.1 = (bf16[64,128]{1,0:T(8,128)(2,1)S(1)}, bf16[64,128]{1,0:T(8,128)(2,1)S(1)}, u32[]{:S(2)}, u32[]{:S(2)}) collective-permute-start(bf16[64,128]{1,0:T(8,128)(2,1)S(1)} %get-tuple-element.19), channel_id=1, source_target_pairs={{0,4},{1,5},{2,6},{3,7},{4,8},{5,9},{6,10},{7,11},{8,12},{9,13},{1... | collective-permute-start | bytes 49160 | tf_op jit(solution)/shard_map/ppermute | solution.py:28
  49.5 30.0 %collective-permute-start.2 = (bf16[64,128]{1,0:T(8,128)(2,1)S(1)}, bf16[64,128]{1,0:T(8,128)(2,1)S(1)}, u32[]{:S(2)}, u32[]{:S(2)}) collective-permute-start(bf16[64,128]{1,0:T(8,128)(2,1)S(1)} %get-tuple-element.20), channel_id=1, source_target_pairs={{0,508},{1,509},{2,510},{3,511},{4,0},{5,1},{6,2},{7,3},{8,4},{9,5... | collective-permute-start | bytes 49160 | tf_op jit(solution)/shard_map/ppermute | solution.py:28
  59.7 19.3 %collective-permute-start.3 = (bf16[512,128]{1,0:T(8,128)(2,1)S(1)}, bf16[512,128]{1,0:T(8,128)(2,1)S(1)}, u32[]{:S(2)}, u32[]{:S(2)}) collective-permute-start(bf16[512,128]{1,0:T(8,128)(2,1)S(1)} %slice.75), channel_id=1, source_target_pairs={{0,508},{1,509},{2,510},{3,511},{4,504},{5,505},{6,506},{7,507},{8... | collective-permute-start | bytes 393224 | tf_op jit(solution)/shard_map/ppermute | solution.py:28
  65.5 13.4 %collective-permute-start.4 = (bf16[128,128]{1,0:T(8,128)(2,1)S(1)}, bf16[128,128]{1,0:T(8,128)(2,1)S(1)}, u32[]{:S(2)}, u32[]{:S(2)}) collective-permute-start(bf16[128,128]{1,0:T(8,128)(2,1)S(1)} %slice.76), channel_id=1, source_target_pairs={{0,504},{1,505},{2,506},{3,507},{4,500},{5,501},{6,502},{7,503},{8... | collective-permute-start | bytes 98312 | tf_op jit(solution)/shard_map/ppermute | solution.py:28
  79.7 2.2 %copy-start = (bf16[64,256,128]{2,1,0:T(8,128)(2,1)S(1)}, bf16[64,256,128]{2,1,0:T(8,128)(2,1)}, u32[]{:S(2)}) copy-start(bf16[64,256,128]{2,1,0:T(8,128)(2,1)} %all-gather.2.cloned.1.call-done.kern) | copy-start | bytes 12582916
  86.5 36.2 %copy-start.4 = (f32[4]{0:T(128)S(1)}, f32[4]{0:T(128)}, u32[]{:S(2)}) copy-start(f32[4]{0:T(128)} %constant.95) | copy-start | bytes 52
  86.6 11.8 %collective-permute-start.5 = (bf16[64,128]{1,0:T(8,128)(2,1)S(1)}, bf16[64,128]{1,0:T(8,128)(2,1)S(1)}, u32[]{:S(2)}, u32[]{:S(2)}) collective-permute-start(bf16[64,128]{1,0:T(8,128)(2,1)S(1)} %get-tuple-element.14), channel_id=1, source_target_pairs={{0,4},{1,5},{2,6},{3,7},{4,8},{5,9},{6,10},{7,11},{8,12},{9,13},{1... | collective-permute-start | bytes 49160 | tf_op jit(solution)/shard_map/ppermute | solution.py:28
Sparse Core Ops, SparseCore 0:
  9.5 68.0 all-gather.1

commit v3 on v1

v3 whole, which is shorter than its diff:
```python
import functools

import jax
import jax.numpy as jnp
from jax import lax
from jax.experimental import pallas as pl
from jax.experimental.pallas import tpu as pltpu
from jax.sharding import PartitionSpec as P

SUB = 64
GROUP = 8
WEIGHT = 16
SIGNS = (1.0, -1.0, 1.0, -1.0)
STEP = 0.5 * 0.5
F32 = jnp.float32
BF16 = jnp.bfloat16
VMEM = pl.BlockSpec(memory_space=pltpu.VMEM)
SMEM = pl.BlockSpec(memory_space=pltpu.SMEM)


def send(value, route):
    tiles = lax.axis_size("tile")
    views = lax.axis_size("vis")
    pairs = []
    for tile in range(tiles):
        for view in range(views):
            to_tile, to_view = route(tile, view)
            pairs.append((tile * views + view, to_tile % tiles * views + to_view % views))
    return lax.ppermute(value, ("tile", "vis"), pairs)


def call(body, outs, scratch=(), flops=0, moved=0, vmem=16):
    return functools.partial(
        pl.pallas_call,
        body,
        out_shape=outs,
        scratch_shapes=list(scratch),
        compiler_params=pltpu.CompilerParams(vmem_limit_bytes=vmem * 1024 * 1024),
        cost_estimate=pl.CostEstimate(flops=flops, bytes_accessed=moved, transcendentals=0),
    )


def dot_nn(left, right):
    return lax.dot_general(left, right, (((1,), (0,)), ((), ())), preferred_element_type=F32)


def dot_nt(left, right):
    return lax.dot_general(left, right, (((1,), (1,)), ((), ())), preferred_element_type=F32)


def masks(shift, cols):
    row = lax.broadcasted_iota(jnp.int32, (cols, cols), 0)
    col = lax.broadcasted_iota(jnp.int32, (cols, cols), 1)
    pick = jnp.where(row == col, 1.0, 0.0)[:SUB]
    place_t = jnp.where((col == row + shift) & (col >= SUB), 1.0, 0.0)
    place = jnp.where((row == col + shift) & (row >= SUB), 1.0, 0.0)
    return jnp.concatenate([pick, place_t], axis=0).astype(BF16), place.astype(BF16)


def grid_one(row, live, block, obs, along_u, kv_t, kv, grid):
    patch = jnp.concatenate([grid[comp, pl.ds(row, SUB), :] for comp in range(4)], axis=0)
    inner = dot_nn(patch.astype(BF16), kv_t)
    parts = []
    for comp in range(4):
        seen = jnp.sum(along_u * inner[comp * SUB : (comp + 1) * SUB], axis=0, keepdims=True)
        left = jnp.where(live, obs[comp, pl.ds(block, 1), :] - seen, 0.0)
        parts.append((along_u * left).astype(BF16))
    return dot_nn(jnp.concatenate(parts, axis=0), kv)


def add_one(row, fresh, acc):
    for comp in range(4):
        acc[comp, pl.ds(row, SUB), :] += fresh[comp * SUB : (comp + 1) * SUB]


def prepare_body(offsets, kernels, ku_t, kv_t, kv):
    blocks, _, cols = kernels.shape
    for block in range(blocks):
        both, place = masks(SUB - offsets[1, block], cols)
        weights = kernels[block]
        turned = dot_nt(both, weights).astype(BF16)
        ku_t[block] = turned[:SUB]
        kv_t[block] = turned[SUB:]
        kv[block] = dot_nn(weights, place).astype(BF16)


def grid_all(offsets, counts, base, obs, ku_t, kv_t, kv, grid, acc):
    blocks = ku_t.shape[0]
    for group in range(blocks // GROUP):
        staged = []
        for block in range(group * GROUP, (group + 1) * GROUP):
            row = offsets[0, block]
            live = (block < counts[0]) & (row <= base)
            row = jnp.minimum(row, base)
            along_u = ku_t[block].astype(F32)
            fresh = grid_one(row, live, block, obs, along_u, kv_t[block], kv[block], grid)
            staged.append((row, fresh))
        for row, fresh in staged:
            add_one(row, fresh, acc)


def first_body(offsets, counts, observed, ku_t, kv_t, kv, model, halo, out, obs, grid, acc):
    rows = model.shape[1]
    obs[...] = observed[...].astype(F32)
    grid[:, :rows] = model[...].astype(F32)
    grid[:, rows:] = halo[...].astype(F32)
    acc[...] = jnp.zeros_like(acc)
    grid_all(offsets, counts, rows - 1, obs, ku_t, kv_t, kv, grid, acc)
    out[...] = acc[...].astype(BF16)


def inside_body(offsets, counts, observed, ku_t, kv_t, kv, model, tail, out, obs, grid, acc):
    rows = model.shape[1] - SUB
    base = rows - SUB
    obs[...] = observed[...].astype(F32)
    grid[...] = model[:, :rows].astype(F32)
    acc[:, :base] = jnp.zeros((4, base, acc.shape[2]), F32)
    acc[:, base:] = tail[...]
    grid_all(offsets, counts, base, obs, ku_t, kv_t, kv, grid, acc)
    views = out.shape[0]
    quarter = rows // views
    for view in range(views):
        out[view] = acc[:, view * quarter : (view + 1) * quarter].astype(BF16)


def cross(picks, offsets, counts, obs, ku_t, kv_t, kv, grid, acc, base):
    blocks = ku_t.shape[0]

    def add(block, found):
        good = (block < counts[0]) & (offsets[0, block] > base)

        @pl.when(good)
        def _():
            picks[found] = block

        return found + good.astype(jnp.int32)

    limit = lax.fori_loop(0, blocks, add, 0, unroll=True)

    def pair(index, carry):
        staged = []
        for lane in range(2):
            place = 2 * index + lane
            block = picks[jnp.minimum(place, limit - 1)]
            row = offsets[0, block] - base
            along_u = ku_t[block].astype(F32)
            fresh = grid_one(
                row, place < limit, block, obs, along_u, kv_t[block], kv[block], grid
            )
            staged.append((row, fresh))
        for row, fresh in staged:
            add_one(row, fresh, acc)
        return carry

    lax.fori_loop(0, (limit + 1) // 2, pair, 0)


def border_body(offsets, counts, observed, ku_t, kv_t, kv, model, spill, tail, picks, obs, grid, acc):
    base = model.shape[1] - 2 * SUB
    obs[...] = observed[...].astype(F32)
    grid[...] = model[:, base:].astype(F32)
    acc[...] = jnp.zeros_like(acc)
    cross(picks, offsets, counts, obs, ku_t, kv_t, kv, grid, acc, base)
    spill[...] = acc[:, SUB:].astype(BF16)
    tail[...] = acc[:, :SUB]


def total_body(parts, own, across, beside, before, after):
    rows = across.shape[0]
    total = parts[0].astype(F32)
    for source in range(1, parts.shape[0]):
        total = total + parts[source].astype(F32)
    own[...] = total
    sent = total.astype(BF16)
    across[...] = sent[:rows]
    beside[...] = sent[rows - SUB :]
    before[...] = sent[rows:]
    after[...] = sent[:SUB]


def flip(value):
    return value[..., ::-1, ::-1].astype(F32)


def on_device(model, observed, kernels, offsets, counts):
    views = lax.axis_size("vis")
    view = lax.axis_index("vis")
    tiles = lax.axis_size("tile")
    rows, cols = model.shape[1:]
    full = rows + SUB
    quarter = rows // views
    blocks, depth = kernels.shape[:2]
    sds = jax.ShapeDtypeStruct
    picks = pltpu.SMEM((blocks,), jnp.int32)
    obs = pltpu.VMEM(observed.shape, F32)
    full_rows = pltpu.VMEM((4, full, cols), F32)
    inner_rows = pltpu.VMEM((4, rows, cols), F32)
    end_rows = pltpu.VMEM((4, 2 * SUB, cols), F32)
    flops = 4 * 2 * blocks * depth * cols * SUB * 2
    moved = 4 * 1024 * 1024

    offsets = offsets.T
    halo = send(model[:, :SUB], lambda tile, view: (tile - 1, view))
    ku_t, kv_t, kv = call(
        prepare_body,
        (
            sds((blocks, SUB, depth), BF16),
            sds((blocks, cols, depth), BF16),
            sds((blocks, depth, cols), BF16),
        ),
        flops=WEIGHT * flops,
        moved=moved,
    )(in_specs=[SMEM, VMEM], out_specs=(VMEM,) * 3)(offsets, kernels)
    partial = call(
        first_body,
        sds((4, full, cols), BF16),
        [obs, full_rows, full_rows],
        flops=WEIGHT * flops,
        moved=moved,
    )(in_specs=[SMEM] * 2 + [VMEM] * 6, out_specs=VMEM)(
        offsets, counts, observed, ku_t, kv_t, kv, model, halo
    )

    parts = lax.all_to_all(partial, "vis", 0, 0, tiled=True)
    own, across, beside, before, after = call(
        total_body,
        (
            sds((full, cols), F32),
            sds((rows, cols), BF16),
            sds((2 * SUB, cols), BF16),
            sds((SUB, cols), BF16),
            sds((SUB, cols), BF16),
        ),
        moved=moved,
        vmem=58,
    )(in_specs=[VMEM], out_specs=(VMEM,) * 5)(parts)
    across = send(across, lambda tile, view: (tiles - 1 - tile, view))
    beside = send(beside, lambda tile, view: (tiles - 2 - tile, view))
    before = send(before, lambda tile, view: (tile + 1, view))
    after = send(after, lambda tile, view: (tile - 1, view))
    sign = jnp.where(view % 2 == 0, 1.0, -1.0).astype(F32)
    mine = lax.dynamic_index_in_dim(model, view, 0, keepdims=False)
    mine_halo = lax.dynamic_index_in_dim(halo, view, 0, keepdims=False)
    start = jnp.concatenate([mine, mine_halo], axis=0).astype(F32)
    pad = lambda value, low: jnp.pad(value.astype(F32), ((low, full - low - value.shape[0]), (0, 0)))
    summed = own + pad(before, 0) + pad(after, rows)
    mirrored = pad(flip(across), 0) + pad(flip(beside), rows - SUB)
    piece = (start + STEP * (summed + sign * mirrored)).astype(BF16)
    band = lax.all_gather(piece, "vis", axis=0, tiled=False)

    spill, tail = call(
        border_body,
        (sds((4, SUB, cols), BF16), sds((4, SUB, cols), F32)),
        [picks, obs, end_rows, end_rows],
        flops=flops,
        moved=moved,
    )(in_specs=[SMEM] * 2 + [VMEM] * 5, out_specs=(VMEM, VMEM))(
        offsets, counts, observed, ku_t, kv_t, kv, band
    )
    spilled = send(spill, lambda tile, view: (tile + 1, view))
    partial = call(
        inside_body,
        sds((views, 4, quarter, cols), BF16),
        [obs, inner_rows, inner_rows],
        flops=WEIGHT * flops,
        moved=moved,
    )(in_specs=[SMEM] * 2 + [VMEM] * 6, out_specs=VMEM)(
        offsets, counts, observed, ku_t, kv_t, kv, band, tail
    )
    spilled = jnp.pad(spilled.astype(F32)[None], ((0, views - 1), (0, 0), (0, quarter - SUB), (0, 0)))
    partial = (partial.astype(F32) + spilled).astype(BF16)
    parts = lax.all_to_all(partial, "vis", 0, 0, tiled=True)
    own = jnp.sum(parts.astype(F32), axis=0)
    across = send(own.astype(BF16), lambda tile, view: (tiles - 1 - tile, views - 1 - view))
    signs = jnp.array(SIGNS, F32)[:, None, None]
    start = lax.dynamic_slice_in_dim(band, view * quarter, quarter, 1).astype(F32)
    return (start + STEP * (own + signs * flip(across))).astype(BF16)


def solution(mesh):
    placed = (
        P(None, "tile", None),
        P(None, ("tile", "vis"), None),
        P(("tile", "vis"), None, None),
        P(("tile", "vis"), None),
        P(("tile", "vis")),
    )
    return jax.shard_map(
        on_device,
        mesh=mesh,
        in_specs=placed,
        out_specs=P(None, ("tile", "vis"), None),
        check_vma=False,
    )
```

time: 119 us -> 110 us (0.924)
  the two profiles are of different devices: /device:TPU:96 before, /device:TPU:1 now
where the time goes in v3:
time: 110 us
  starting transfers between devices  47.7 us (43%)
  waiting for transfers between devices  26.3 us (24%)
  blocking collectives  20.2 us (18%)
  Pallas kernels  9.48 us (9%)
  local copies, waits for them, and re-layouts  3.06 us (3%)
  other arithmetic  1.99 us (2%)
    ppermute x7, starting transfers between devices, send(): return lax.ppermute(value, ('tile', 'vis'), pairs)  43.6 us
    ppermute x7, waiting for transfers between devices, send(): return lax.ppermute(value, ('tile', 'vis'), pairs)  18.9 us
    all_gather x1, blocking collectives, on_device(): band = lax.all_gather(piece, 'vis', axis=0, tiled=False)  10.9 us
    all_to_all x1, blocking collectives, on_device(): parts = lax.all_to_all(partial, 'vis', 0, 0, tiled=True)  9.33 us
    all_to_all x1, waiting for transfers between devices, on_device(): parts = lax.all_to_all(partial, 'vis', 0, 0, tiled=True)  7.34 us
    all_to_all x1, starting transfers between devices, on_device(): parts = lax.all_to_all(partial, 'vis', 0, 0, tiled=True)  4.15 us
    pallas_call x1, Pallas kernels, on_device(): call(first_body, sds((4, full, cols), BF16), [obs, full_rows, full_rows],...  3.01 us
  transfers between devices with their start and end apart: 8, of which 5 were waited for; matrix products, arithmetic and copies ran while one was open for 1% of the time, Pallas kernels for 3%

profile of v3, /device:TPU:1, one launch (start us, length us, event | category | flops | bytes accessed | tf_op | source)
XLA Modules:
  0.0 109.7 jit_solution(14308709857033484756)
XLA Ops:
  0.0 0.8 slice.3
  0.8 8.9 %collective-permute-start = (bf16[4,64,128]{2,1,0:T(8,128)(2,1)S(1)}, bf16[4,64,128]{2,1,0:T(8,128)(2,1)S(1)}, u32[]{:S(2)}, u32[]{:S(2)}) collective-permute-start(bf16[4,64,128]{2,1,0:T(8,128)(2,1)S(1)} %slice.3), channel_id=1, source_target_pairs={{0,508},{1,509},{2,510},{3,511},{4,0},{5,1},{6,2},{7,3},{8,4},{9,5... | collective-permute-start | bytes 196616 | tf_op jit(solution)/shard_map/ppermute | solution.py:29
  9.8 1.2 %copy-done.3 = bf16[16,256,128]{2,1,0:T(8,128)(2,1)S(1)} copy-done((bf16[16,256,128]{2,1,0:T(8,128)(2,1)S(1)}, bf16[16,256,128]{2,1,0:T(8,128)(2,1)}, u32[]{:S(2)}) %copy-start.3) | copy-done | bytes 1048600
  11.0 1.4 %shard_map.64 = (bf16[16,64,256]{2,1,0:T(8,128)(2,1)S(1)}, bf16[16,128,256]{2,1,0:T(8,128)(2,1)S(1)}, bf16[16,256,128]{2,1,0:T(8,128)(2,1)S(1)}) custom-call(s32[2,16]{1,0:T(2,128)S(1)} %bitcast.10, bf16[16,256,128]{2,1,0:T(8,128)(2,1)S(1)} %copy-done.3), custom_call_target="tpu_custom_call" | custom-call | flops 8589934592 | bytes 4194304 | tf_op jit(solution)/shard_map/pallas_call | solution.py:204
  13.1 3.0 %shard_map.65 = bf16[4,576,128]{2,1,0:T(8,128)(2,1)} custom-call(s32[2,16]{1,0:T(2,128)S(1)} %bitcast.11, s32[1]{0:T(128)S(6)} %copy.7.counts, bf16[4,16,256]{2,1,0:T(8,128)(2,1)S(1)} %copy-done.1, bf16[16,64,256]{2,1,0:T(8,128)(2,1)S(1)} %get-tuple-element.15.ku_t, bf16[16,128,256]{2,1,0:T(8,128)(2,1)S(1)} %get-tuple-element.16.kv_t, ...), custom_call_target="tpu_custom_call" | custom-call | flops 8589934592 | bytes 4194304 | tf_op jit(solution)/shard_map/pallas_call | solution.py:214
  16.1 4.2 %all-to-all-start = ((bf16[4,576,128]{2,1,0:T(8,128)(2,1)}), bf16[4,576,128]{2,1,0:T(8,128)(2,1)}, u32[]{:S(2)}, u32[]{:S(2)}) async-start(bf16[4,576,128]{2,1,0:T(8,128)(2,1)} %shard_map.65), calls=%async_computation | async-start | bytes 1179648 | tf_op jit(solution)/shard_map/all_to_all | solution.py:224
  20.3 7.3 %all-to-all-done.parts = bf16[4,576,128]{2,1,0:T(8,128)(2,1)} async-done(((bf16[4,576,128]{2,1,0:T(8,128)(2,1)}), bf16[4,576,128]{2,1,0:T(8,128)(2,1)}, u32[]{:S(2)}, u32[]{:S(2)}) %all-to-all-start) | async-done | bytes 589856 | tf_op jit(solution)/shard_map/all_to_all | solution.py:224
  27.6 1.9 %shard_map.66 = (f32[576,128]{1,0:T(8,128)}, bf16[512,128]{1,0:T(8,128)(2,1)}, bf16[128,128]{1,0:T(8,128)(2,1)}, bf16[64,128]{1,0:T(8,128)(2,1)}, bf16[64,128]{1,0:T(8,128)(2,1)}) custom-call(bf16[4,576,128]{2,1,0:T(8,128)(2,1)} %all-to-all-done.parts), custom_call_target="tpu_custom_call" | custom-call | bytes 4194304 | tf_op jit(solution)/shard_map/pallas_call | solution.py:225
  29.5 11.1 %collective-permute-start.3 = (bf16[512,128]{1,0:T(8,128)(2,1)}, bf16[512,128]{1,0:T(8,128)(2,1)S(1)}, u32[]{:S(2)}, u32[]{:S(2)}) collective-permute-start(bf16[512,128]{1,0:T(8,128)(2,1)} %get-tuple-element.21), channel_id=1, source_target_pairs={{0,508},{1,509},{2,510},{3,511},{4,504},{5,505},{6,506},{7,507},{8... | collective-permute-start | bytes 393224 | tf_op jit(solution)/shard_map/ppermute | solution.py:29
  40.7 1.9 %collective-permute-start.4 = (bf16[128,128]{1,0:T(8,128)(2,1)S(1)}, bf16[128,128]{1,0:T(8,128)(2,1)S(1)}, u32[]{:S(2)}, u32[]{:S(2)}) collective-permute-start(bf16[128,128]{1,0:T(8,128)(2,1)S(1)} %copy-done.5), channel_id=1, source_target_pairs={{0,504},{1,505},{2,506},{3,507},{4,500},{5,501},{6,502},{7,503},{8... | collective-permute-start | bytes 98312 | tf_op jit(solution)/shard_map/ppermute | solution.py:29
  42.6 4.7 %collective-permute-start.1 = (bf16[64,128]{1,0:T(8,128)(2,1)}, bf16[64,128]{1,0:T(8,128)(2,1)S(1)}, u32[]{:S(2)}, u32[]{:S(2)}) collective-permute-start(bf16[64,128]{1,0:T(8,128)(2,1)} %get-tuple-element.19), channel_id=1, source_target_pairs={{0,4},{1,5},{2,6},{3,7},{4,8},{5,9},{6,10},{7,11},{8,12},{9,13},{1... | collective-permute-start | bytes 49160 | tf_op jit(solution)/shard_map/ppermute | solution.py:29
  47.4 1.9 %collective-permute-start.2 = (bf16[64,128]{1,0:T(8,128)(2,1)S(1)}, bf16[64,128]{1,0:T(8,128)(2,1)S(1)}, u32[]{:S(2)}, u32[]{:S(2)}) collective-permute-start(bf16[64,128]{1,0:T(8,128)(2,1)S(1)} %copy-done.6), channel_id=1, source_target_pairs={{0,508},{1,509},{2,510},{3,511},{4,0},{5,1},{6,2},{7,3},{8,4},{9,5... | collective-permute-start | bytes 49160 | tf_op jit(solution)/shard_map/ppermute | solution.py:29
  49.3 4.5 %collective-permute-done.4 = bf16[128,128]{1,0:T(8,128)(2,1)S(1)} collective-permute-done((bf16[128,128]{1,0:T(8,128)(2,1)S(1)}, bf16[128,128]{1,0:T(8,128)(2,1)S(1)}, u32[]{:S(2)}, u32[]{:S(2)}) %collective-permute-start.4) | collective-permute-done | bytes 32800 | tf_op jit(solution)/shard_map/ppermute | solution.py:29
  53.9 1.0 collective-permute-done.3
  55.4 1.1 add_convert_fusion.1
  56.4 10.9 %all-gather = bf16[2304,128]{1,0:T(8,128)(2,1)S(1)} all-gather(bf16[576,128]{1,0:T(8,128)(2,1)S(1)} %add_convert_fusion.1), channel_id=2, replica_groups=mesh['tile'=128,'vis'=4] {'vis'}, dimensions={0}, use_global_device_ids=true | all-gather | bytes 737280 | tf_op jit(solution)/shard_map/all_gather | solution.py:249
  67.3 1.0 shard_map.67
  68.4 3.0 %collective-permute-start.5 = (bf16[4,64,128]{2,1,0:T(8,128)(2,1)S(1)}, bf16[4,64,128]{2,1,0:T(8,128)(2,1)S(1)}, u32[]{:S(2)}, u32[]{:S(2)}) collective-permute-start(bf16[4,64,128]{2,1,0:T(8,128)(2,1)S(1)} %get-tuple-element.24), channel_id=1, source_target_pairs={{0,4},{1,5},{2,6},{3,7},{4,8},{5,9},{6,10},{7,11},{8,12},{9,13},{1... | collective-permute-start | bytes 196616 | tf_op jit(solution)/shard_map/ppermute | solution.py:29
  71.4 2.2 %shard_map.68 = bf16[4,4,128,128]{3,2,1,0:T(8,128)(2,1)S(1)} custom-call(s32[2,16]{1,0:T(2,128)S(1)} %bitcast.13, s32[1]{0:T(128)S(6)} %copy.7.counts, bf16[4,16,256]{2,1,0:T(8,128)(2,1)S(1)} %copy-done.1, bf16[16,64,256]{2,1,0:T(8,128)(2,1)S(1)} %get-tuple-element.15.ku_t, bf16[16,128,256]{2,1,0:T(8,128)(2,1)S(1)} %get-tuple-element.16.kv_t, ...), custom_call_target="tpu_custom_call" | custom-call | flops 8589934592 | bytes 4194304 | tf_op jit(solution)/shard_map/pallas_call | solution.py:261
  73.5 1.8 %collective-permute-done.5 = bf16[4,64,128]{2,1,0:T(8,128)(2,1)S(1)} collective-permute-done((bf16[4,64,128]{2,1,0:T(8,128)(2,1)S(1)}, bf16[4,64,128]{2,1,0:T(8,128)(2,1)S(1)}, u32[]{:S(2)}, u32[]{:S(2)}) %collective-permute-start.5) | collective-permute-done | bytes 65568 | tf_op jit(solution)/shard_map/ppermute | solution.py:29
  75.3 9.3 %all_to_all.10 = bf16[4,4,128,128]{3,2,1,0:T(8,128)(2,1)S(1)} all-to-all(bf16[4,4,128,128]{3,2,1,0:T(8,128)(2,1)S(1)} %add_convert_fusion), channel_id=1, replica_groups=mesh['tile'=128,'vis'=4] {'vis'}, dimensions={0} | all-to-all | bytes 1048576 | tf_op jit(solution)/shard_map/all_to_all | solution.py:272
  84.8 12.0 %collective-permute-start.6 = (bf16[4,128,128]{2,1,0:T(8,128)(2,1)S(1)}, bf16[4,128,128]{2,1,0:T(8,128)(2,1)S(1)}, u32[]{:S(2)}, u32[]{:S(2)}) collective-permute-start(bf16[4,128,128]{2,1,0:T(8,128)(2,1)S(1)} %convert_element_type.48), channel_id=1, source_target_pairs={{0,511},{1,510},{2,509},{3,508},{4,507},{5,506},{6,505},{7,504},{8... | collective-permute-start | bytes 393224 | tf_op jit(solution)/shard_map/ppermute | solution.py:29
  96.8 11.6 %collective-permute-done.6 = bf16[4,128,128]{2,1,0:T(8,128)(2,1)S(1)} collective-permute-done((bf16[4,128,128]{2,1,0:T(8,128)(2,1)S(1)}, bf16[4,128,128]{2,1,0:T(8,128)(2,1)S(1)}, u32[]{:S(2)}, u32[]{:S(2)}) %collective-permute-start.6) | collective-permute-done | bytes 131104 | tf_op jit(solution)/shard_map/ppermute | solution.py:29
  108.9 0.8 add_convert_fusion.2
  (24 shorter events, 1.1 us)
Async XLA Ops:
  0.8 8.9 %copy-start.2 = (s32[16,2]{0,1:T(2,128)S(1)}, s32[16,2]{0,1:T(2,128)}, u32[]{:S(2)}) copy-start(s32[16,2]{0,1:T(2,128)} %param.9) | copy-start | bytes 388
  0.8 12.2 %collective-permute-start = (bf16[4,64,128]{2,1,0:T(8,128)(2,1)S(1)}, bf16[4,64,128]{2,1,0:T(8,128)(2,1)S(1)}, u32[]{:S(2)}, u32[]{:S(2)}) collective-permute-start(bf16[4,64,128]{2,1,0:T(8,128)(2,1)S(1)} %slice.3), channel_id=1, source_target_pairs={{0,508},{1,509},{2,510},{3,511},{4,0},{5,1},{6,2},{7,3},{8,4},{9,5... | collective-permute-start | bytes 196616 | tf_op jit(solution)/shard_map/ppermute | solution.py:29
  9.8 1.2 %copy-start.3 = (bf16[16,256,128]{2,1,0:T(8,128)(2,1)S(1)}, bf16[16,256,128]{2,1,0:T(8,128)(2,1)}, u32[]{:S(2)}) copy-start(bf16[16,256,128]{2,1,0:T(8,128)(2,1)} %kernels.1) | copy-start | bytes 3145732
  11.0 2.1 %copy-start = (bf16[4,512,128]{2,1,0:T(8,128)(2,1)S(1)}, bf16[4,512,128]{2,1,0:T(8,128)(2,1)}, u32[]{:S(2)}) copy-start(bf16[4,512,128]{2,1,0:T(8,128)(2,1)} %model.1) | copy-start | bytes 1572868
  11.0 2.1 %copy-start.1 = (bf16[4,16,256]{2,1,0:T(8,128)(2,1)S(1)}, bf16[4,16,256]{2,1,0:T(8,128)(2,1)}, u32[]{:S(2)}) copy-start(bf16[4,16,256]{2,1,0:T(8,128)(2,1)} %observed.5) | copy-start | bytes 98308
  16.1 11.5 %all-to-all-start = ((bf16[4,576,128]{2,1,0:T(8,128)(2,1)}), bf16[4,576,128]{2,1,0:T(8,128)(2,1)}, u32[]{:S(2)}, u32[]{:S(2)}) async-start(bf16[4,576,128]{2,1,0:T(8,128)(2,1)} %shard_map.65), calls=%async_computation | async-start | bytes 1179648 | tf_op jit(solution)/shard_map/all_to_all | solution.py:224
  29.5 11.2 %copy-start.5 = (bf16[128,128]{1,0:T(8,128)(2,1)S(1)}, bf16[128,128]{1,0:T(8,128)(2,1)}, u32[]{:S(2)}) copy-start(bf16[128,128]{1,0:T(8,128)(2,1)} %get-tuple-element.22) | copy-start | bytes 98308
  29.5 25.5 %collective-permute-start.3 = (bf16[512,128]{1,0:T(8,128)(2,1)}, bf16[512,128]{1,0:T(8,128)(2,1)S(1)}, u32[]{:S(2)}, u32[]{:S(2)}) collective-permute-start(bf16[512,128]{1,0:T(8,128)(2,1)} %get-tuple-element.21), channel_id=1, source_target_pairs={{0,508},{1,509},{2,510},{3,511},{4,504},{5,505},{6,506},{7,507},{8... | collective-permute-start | bytes 393224 | tf_op jit(solution)/shard_map/ppermute | solution.py:29
  40.7 6.7 %copy-start.6 = (bf16[64,128]{1,0:T(8,128)(2,1)S(1)}, bf16[64,128]{1,0:T(8,128)(2,1)}, u32[]{:S(2)}) copy-start(bf16[64,128]{1,0:T(8,128)(2,1)} %get-tuple-element.20) | copy-start | bytes 49156
  40.7 13.1 %collective-permute-start.4 = (bf16[128,128]{1,0:T(8,128)(2,1)S(1)}, bf16[128,128]{1,0:T(8,128)(2,1)S(1)}, u32[]{:S(2)}, u32[]{:S(2)}) collective-permute-start(bf16[128,128]{1,0:T(8,128)(2,1)S(1)} %copy-done.5), channel_id=1, source_target_pairs={{0,504},{1,505},{2,506},{3,507},{4,500},{5,501},{6,502},{7,503},{8... | collective-permute-start | bytes 98312 | tf_op jit(solution)/shard_map/ppermute | solution.py:29
  42.6 12.7 %collective-permute-start.1 = (bf16[64,128]{1,0:T(8,128)(2,1)}, bf16[64,128]{1,0:T(8,128)(2,1)S(1)}, u32[]{:S(2)}, u32[]{:S(2)}) collective-permute-start(bf16[64,128]{1,0:T(8,128)(2,1)} %get-tuple-element.19), channel_id=1, source_target_pairs={{0,4},{1,5},{2,6},{3,7},{4,8},{5,9},{6,10},{7,11},{8,12},{9,13},{1... | collective-permute-start | bytes 49160 | tf_op jit(solution)/shard_map/ppermute | solution.py:29
  47.4 8.0 %collective-permute-start.2 = (bf16[64,128]{1,0:T(8,128)(2,1)S(1)}, bf16[64,128]{1,0:T(8,128)(2,1)S(1)}, u32[]{:S(2)}, u32[]{:S(2)}) collective-permute-start(bf16[64,128]{1,0:T(8,128)(2,1)S(1)} %copy-done.6), channel_id=1, source_target_pairs={{0,508},{1,509},{2,510},{3,511},{4,0},{5,1},{6,2},{7,3},{8,4},{9,5... | collective-permute-start | bytes 49160 | tf_op jit(solution)/shard_map/ppermute | solution.py:29
  68.4 6.9 %collective-permute-start.5 = (bf16[4,64,128]{2,1,0:T(8,128)(2,1)S(1)}, bf16[4,64,128]{2,1,0:T(8,128)(2,1)S(1)}, u32[]{:S(2)}, u32[]{:S(2)}) collective-permute-start(bf16[4,64,128]{2,1,0:T(8,128)(2,1)S(1)} %get-tuple-element.24), channel_id=1, source_target_pairs={{0,4},{1,5},{2,6},{3,7},{4,8},{5,9},{6,10},{7,11},{8,12},{9,13},{1... | collective-permute-start | bytes 196616 | tf_op jit(solution)/shard_map/ppermute | solution.py:29
  84.8 23.7 %collective-permute-start.6 = (bf16[4,128,128]{2,1,0:T(8,128)(2,1)S(1)}, bf16[4,128,128]{2,1,0:T(8,128)(2,1)S(1)}, u32[]{:S(2)}, u32[]{:S(2)}) collective-permute-start(bf16[4,128,128]{2,1,0:T(8,128)(2,1)S(1)} %convert_element_type.48), channel_id=1, source_target_pairs={{0,511},{1,510},{2,509},{3,508},{4,507},{5,506},{6,505},{7,504},{8... | collective-permute-start | bytes 393224 | tf_op jit(solution)/shard_map/ppermute | solution.py:29
  96.8 12.1 %copy-start.4 = (f32[4]{0:T(128)S(1)}, f32[4]{0:T(128)}, u32[]{:S(2)}) copy-start(f32[4]{0:T(128)} %constant.45.clone) | copy-start | bytes 52

commit v4 on v3

--- a/solution.py
+++ b/solution.py
@@ -165,16 +165,14 @@
     tail[...] = acc[:, :SUB]
 
 
-def total_body(parts, own, across, beside, before, after):
-    rows = across.shape[0]
+def total_body(parts, own, across, before, after):
     total = parts[0].astype(F32)
     for source in range(1, parts.shape[0]):
         total = total + parts[source].astype(F32)
     own[...] = total
     sent = total.astype(BF16)
-    across[...] = sent[:rows]
-    beside[...] = sent[rows - SUB :]
-    before[...] = sent[rows:]
+    across[...] = sent[SUB:-SUB]
+    before[...] = sent[-2 * SUB :]
     after[...] = sent[:SUB]
 
 
@@ -222,28 +220,28 @@
     )
 
     parts = lax.all_to_all(partial, "vis", 0, 0, tiled=True)
-    own, across, beside, before, after = call(
+    own, across, before, after = call(
         total_body,
         (
             sds((full, cols), F32),
-            sds((rows, cols), BF16),
+            sds((rows - SUB, cols), BF16),
             sds((2 * SUB, cols), BF16),
             sds((SUB, cols), BF16),
-            sds((SUB, cols), BF16),
         ),
         moved=moved,
         vmem=58,
-    )(in_specs=[VMEM], out_specs=(VMEM,) * 5)(parts)
+    )(in_specs=[VMEM], out_specs=(VMEM,) * 4)(parts)
     across = send(across, lambda tile, view: (tiles - 1 - tile, view))
-    beside = send(beside, lambda tile, view: (tiles - 2 - tile, view))
-    before = send(before, lambda tile, view: (tile + 1, view))
+    before = send(before, lambda tile, view: (tile + 1, view)).astype(F32)
     after = send(after, lambda tile, view: (tile - 1, view))
+    beside = (before + jnp.pad(own[:SUB], ((SUB, 0), (0, 0)))).astype(BF16)
+    beside = send(beside, lambda tile, view: (tiles - 1 - tile, view))
     sign = jnp.where(view % 2 == 0, 1.0, -1.0).astype(F32)
     mine = lax.dynamic_index_in_dim(model, view, 0, keepdims=False)
     mine_halo = lax.dynamic_index_in_dim(halo, view, 0, keepdims=False)
     start = jnp.concatenate([mine, mine_halo], axis=0).astype(F32)
     pad = lambda value, low: jnp.pad(value.astype(F32), ((low, full - low - value.shape[0]), (0, 0)))
-    summed = own + pad(before, 0) + pad(after, rows)
+    summed = own + pad(before[SUB:], 0) + pad(after, rows)
     mirrored = pad(flip(across), 0) + pad(flip(beside), rows - SUB)
     piece = (start + STEP * (summed + sign * mirrored)).astype(BF16)
     band = lax.all_gather(piece, "vis", axis=0, tiled=False)

time: 110 us -> 115 us (1.045)
  the two profiles are of different devices: /device:TPU:1 before, /device:TPU:97 now
where the time goes in v4:
time: 115 us; the launch traced here: 114 us
  starting transfers between devices  39.9 us (35%)
  waiting for transfers between devices  36 us (31%)
  blocking collectives  23.2 us (20%)
  Pallas kernels  9.05 us (8%)
  local copies, waits for them, and re-layouts  4.08 us (4%)
    ppermute x7, starting transfers between devices, send(): return lax.ppermute(value, ('tile', 'vis'), pairs)  35.7 us
    ppermute x7, waiting for transfers between devices, send(): return lax.ppermute(value, ('tile', 'vis'), pairs)  26.2 us
    all_to_all x1, blocking collectives, on_device(): parts = lax.all_to_all(partial, 'vis', 0, 0, tiled=True)  12.2 us
    all_gather x1, blocking collectives, on_device(): band = lax.all_gather(piece, 'vis', axis=0, tiled=False)  11 us
    all_to_all x1, waiting for transfers between devices, on_device(): parts = lax.all_to_all(partial, 'vis', 0, 0, tiled=True)  9.8 us
    all_to_all x1, starting transfers between devices, on_device(): parts = lax.all_to_all(partial, 'vis', 0, 0, tiled=True)  4.15 us
    pallas_call x1, Pallas kernels, on_device(): call(first_body, sds((4, full, cols), BF16), [obs, full_rows, full_rows],...  3.01 us
  transfers between devices with their start and end apart: 8, of which 4 were waited for; matrix products, arithmetic and copies ran while one was open for 1% of the time, Pallas kernels for 3%

profile of v4, /device:TPU:97, one launch (start us, length us, event | category | flops | bytes accessed | tf_op | source)
XLA Modules:
  0.0 114.1 jit_solution(972103336651563706)
XLA Ops:
  0.0 0.8 slice.9
  0.8 2.7 %collective-permute-start = (bf16[4,64,128]{2,1,0:T(8,128)(2,1)S(1)}, bf16[4,64,128]{2,1,0:T(8,128)(2,1)S(1)}, u32[]{:S(2)}, u32[]{:S(2)}) collective-permute-start(bf16[4,64,128]{2,1,0:T(8,128)(2,1)S(1)} %slice.9), channel_id=1, source_target_pairs={{0,508},{1,509},{2,510},{3,511},{4,0},{5,1},{6,2},{7,3},{8,4},{9,5... | collective-permute-start | bytes 196616 | tf_op jit(solution)/shard_map/ppermute | solution.py:29
  3.6 1.2 %copy-done.3 = bf16[16,256,128]{2,1,0:T(8,128)(2,1)S(1)} copy-done((bf16[16,256,128]{2,1,0:T(8,128)(2,1)S(1)}, bf16[16,256,128]{2,1,0:T(8,128)(2,1)}, u32[]{:S(2)}) %copy-start.3) | copy-done | bytes 1048600
  4.8 1.4 %shard_map.64 = (bf16[16,64,256]{2,1,0:T(8,128)(2,1)S(1)}, bf16[16,128,256]{2,1,0:T(8,128)(2,1)S(1)}, bf16[16,256,128]{2,1,0:T(8,128)(2,1)S(1)}) custom-call(s32[2,16]{1,0:T(2,128)S(1)} %bitcast.10, bf16[16,256,128]{2,1,0:T(8,128)(2,1)S(1)} %copy-done.3), custom_call_target="tpu_custom_call" | custom-call | flops 8589934592 | bytes 4194304 | tf_op jit(solution)/shard_map/pallas_call | solution.py:202
  6.8 1.4 %collective-permute-done.halo = bf16[4,64,128]{2,1,0:T(8,128)(2,1)S(1)} collective-permute-done((bf16[4,64,128]{2,1,0:T(8,128)(2,1)S(1)}, bf16[4,64,128]{2,1,0:T(8,128)(2,1)S(1)}, u32[]{:S(2)}, u32[]{:S(2)}) %collective-permute-start) | collective-permute-done | bytes 65568 | tf_op jit(solution)/shard_map/ppermute | solution.py:29
  8.2 3.0 %shard_map.65 = bf16[4,576,128]{2,1,0:T(8,128)(2,1)} custom-call(s32[2,16]{1,0:T(2,128)S(1)} %bitcast.11, s32[1]{0:T(128)S(6)} %copy.7.counts, bf16[4,16,256]{2,1,0:T(8,128)(2,1)S(1)} %copy-done.1, bf16[16,64,256]{2,1,0:T(8,128)(2,1)S(1)} %get-tuple-element.14.ku_t, bf16[16,128,256]{2,1,0:T(8,128)(2,1)S(1)} %get-tuple-element.15.kv_t, ...), custom_call_target="tpu_custom_call" | custom-call | flops 8589934592 | bytes 4194304 | tf_op jit(solution)/shard_map/pallas_call | solution.py:212
  11.2 4.2 %all-to-all-start = ((bf16[4,576,128]{2,1,0:T(8,128)(2,1)}), bf16[4,576,128]{2,1,0:T(8,128)(2,1)}, u32[]{:S(2)}, u32[]{:S(2)}) async-start(bf16[4,576,128]{2,1,0:T(8,128)(2,1)} %shard_map.65), calls=%async_computation | async-start | bytes 1179648 | tf_op jit(solution)/shard_map/all_to_all | solution.py:222
  15.4 9.8 %all-to-all-done.parts = bf16[4,576,128]{2,1,0:T(8,128)(2,1)} async-done(((bf16[4,576,128]{2,1,0:T(8,128)(2,1)}), bf16[4,576,128]{2,1,0:T(8,128)(2,1)}, u32[]{:S(2)}, u32[]{:S(2)}) %all-to-all-start) | async-done | bytes 589856 | tf_op jit(solution)/shard_map/all_to_all | solution.py:222
  25.2 1.9 %shard_map.66 = (f32[576,128]{1,0:T(8,128)}, bf16[448,128]{1,0:T(8,128)(2,1)}, bf16[128,128]{1,0:T(8,128)(2,1)}, bf16[64,128]{1,0:T(8,128)(2,1)}) custom-call(bf16[4,576,128]{2,1,0:T(8,128)(2,1)} %all-to-all-done.parts), custom_call_target="tpu_custom_call" | custom-call | bytes 4194304 | tf_op jit(solution)/shard_map/pallas_call | solution.py:223
  27.1 4.8 %collective-permute-start.1 = (bf16[128,128]{1,0:T(8,128)(2,1)}, bf16[128,128]{1,0:T(8,128)(2,1)S(1)}, u32[]{:S(2)}, u32[]{:S(2)}) collective-permute-start(bf16[128,128]{1,0:T(8,128)(2,1)} %get-tuple-element.18), channel_id=1, source_target_pairs={{0,4},{1,5},{2,6},{3,7},{4,8},{5,9},{6,10},{7,11},{8,12},{9,13},{1... | collective-permute-start | bytes 98312 | tf_op jit(solution)/shard_map/ppermute | solution.py:29
  32.0 0.8 slice.11
  32.8 10.5 %collective-permute-start.3 = (bf16[448,128]{1,0:T(8,128)(2,1)}, bf16[448,128]{1,0:T(8,128)(2,1)S(1)}, u32[]{:S(2)}, u32[]{:S(2)}) collective-permute-start(bf16[448,128]{1,0:T(8,128)(2,1)} %get-tuple-element.20), channel_id=1, source_target_pairs={{0,508},{1,509},{2,510},{3,511},{4,504},{5,505},{6,506},{7,507},{8... | collective-permute-start | bytes 344072 | tf_op jit(solution)/shard_map/ppermute | solution.py:29
  43.3 3.0 %collective-permute-start.2 = (bf16[64,128]{1,0:T(8,128)(2,1)S(1)}, bf16[64,128]{1,0:T(8,128)(2,1)S(1)}, u32[]{:S(2)}, u32[]{:S(2)}) collective-permute-start(bf16[64,128]{1,0:T(8,128)(2,1)S(1)} %copy-done.6), channel_id=1, source_target_pairs={{0,508},{1,509},{2,510},{3,511},{4,0},{5,1},{6,2},{7,3},{8,4},{9,5... | collective-permute-start | bytes 49160 | tf_op jit(solution)/shard_map/ppermute | solution.py:29
  46.4 3.7 %collective-permute-start.4 = (bf16[128,128]{1,0:T(8,128)(2,1)S(1)}, bf16[128,128]{1,0:T(8,128)(2,1)S(1)}, u32[]{:S(2)}, u32[]{:S(2)}) collective-permute-start(bf16[128,128]{1,0:T(8,128)(2,1)S(1)} %add_convert_fusion.3), channel_id=1, source_target_pairs={{0,508},{1,509},{2,510},{3,511},{4,504},{5,505},{6,506},{7,507},{8... | collective-permute-start | bytes 98312 | tf_op jit(solution)/shard_map/ppermute | solution.py:29
  50.2 10.2 %collective-permute-done.4 = bf16[128,128]{1,0:T(8,128)(2,1)S(1)} collective-permute-done((bf16[128,128]{1,0:T(8,128)(2,1)S(1)}, bf16[128,128]{1,0:T(8,128)(2,1)S(1)}, u32[]{:S(2)}, u32[]{:S(2)}) %collective-permute-start.4) | collective-permute-done | bytes 32800 | tf_op jit(solution)/shard_map/ppermute | solution.py:29
  60.5 0.6 rev.9
  61.2 11.0 %all-gather = bf16[2304,128]{1,0:T(8,128)(2,1)S(1)} all-gather(bf16[576,128]{1,0:T(8,128)(2,1)S(1)} %add_convert_fusion.1), channel_id=2, replica_groups=mesh['tile'=128,'vis'=4] {'vis'}, dimensions={0}, use_global_device_ids=true | all-gather | bytes 737280 | tf_op jit(solution)/shard_map/all_gather | solution.py:247
  72.2 0.6 shard_map.67
  72.9 6.8 %collective-permute-start.5 = (bf16[4,64,128]{2,1,0:T(8,128)(2,1)S(1)}, bf16[4,64,128]{2,1,0:T(8,128)(2,1)S(1)}, u32[]{:S(2)}, u32[]{:S(2)}) collective-permute-start(bf16[4,64,128]{2,1,0:T(8,128)(2,1)S(1)} %get-tuple-element.22), channel_id=1, source_target_pairs={{0,4},{1,5},{2,6},{3,7},{4,8},{5,9},{6,10},{7,11},{8,12},{9,13},{1... | collective-permute-start | bytes 196616 | tf_op jit(solution)/shard_map/ppermute | solution.py:29
  79.6 2.2 %shard_map.68 = bf16[4,4,128,128]{3,2,1,0:T(8,128)(2,1)S(1)} custom-call(s32[2,16]{1,0:T(2,128)S(1)} %bitcast.13, s32[1]{0:T(128)S(6)} %copy.7.counts, bf16[4,16,256]{2,1,0:T(8,128)(2,1)S(1)} %copy-done.1, bf16[16,64,256]{2,1,0:T(8,128)(2,1)S(1)} %get-tuple-element.14.ku_t, bf16[16,128,256]{2,1,0:T(8,128)(2,1)S(1)} %get-tuple-element.15.kv_t, ...), custom_call_target="tpu_custom_call" | custom-call | flops 8589934592 | bytes 4194304 | tf_op jit(solution)/shard_map/pallas_call | solution.py:259
  81.9 12.2 %all_to_all.10 = bf16[4,4,128,128]{3,2,1,0:T(8,128)(2,1)S(1)} all-to-all(bf16[4,4,128,128]{3,2,1,0:T(8,128)(2,1)S(1)} %add_convert_fusion), channel_id=1, replica_groups=mesh['tile'=128,'vis'=4] {'vis'}, dimensions={0} | all-to-all | bytes 1048576 | tf_op jit(solution)/shard_map/all_to_all | solution.py:270
  94.1 4.1 %collective-permute-start.6 = (bf16[4,128,128]{2,1,0:T(8,128)(2,1)S(1)}, bf16[4,128,128]{2,1,0:T(8,128)(2,1)S(1)}, u32[]{:S(2)}, u32[]{:S(2)}) collective-permute-start(bf16[4,128,128]{2,1,0:T(8,128)(2,1)S(1)} %convert_element_type.57), channel_id=1, source_target_pairs={{0,511},{1,510},{2,509},{3,508},{4,507},{5,506},{6,505},{7,504},{8... | collective-permute-start | bytes 393224 | tf_op jit(solution)/shard_map/ppermute | solution.py:29
  98.3 14.6 %collective-permute-done.6 = bf16[4,128,128]{2,1,0:T(8,128)(2,1)S(1)} collective-permute-done((bf16[4,128,128]{2,1,0:T(8,128)(2,1)S(1)}, bf16[4,128,128]{2,1,0:T(8,128)(2,1)S(1)}, u32[]{:S(2)}, u32[]{:S(2)}) %collective-permute-start.6) | collective-permute-done | bytes 131104 | tf_op jit(solution)/shard_map/ppermute | solution.py:29
  113.3 0.8 add_convert_fusion.2
  (27 shorter events, 0.8 us)
Async XLA Ops:
  0.8 2.7 %copy-start.2 = (s32[16,2]{0,1:T(2,128)S(1)}, s32[16,2]{0,1:T(2,128)}, u32[]{:S(2)}) copy-start(s32[16,2]{0,1:T(2,128)} %param.9) | copy-start | bytes 388
  0.8 7.4 %collective-permute-start = (bf16[4,64,128]{2,1,0:T(8,128)(2,1)S(1)}, bf16[4,64,128]{2,1,0:T(8,128)(2,1)S(1)}, u32[]{:S(2)}, u32[]{:S(2)}) collective-permute-start(bf16[4,64,128]{2,1,0:T(8,128)(2,1)S(1)} %slice.9), channel_id=1, source_target_pairs={{0,508},{1,509},{2,510},{3,511},{4,0},{5,1},{6,2},{7,3},{8,4},{9,5... | collective-permute-start | bytes 196616 | tf_op jit(solution)/shard_map/ppermute | solution.py:29
  3.6 1.2 %copy-start.3 = (bf16[16,256,128]{2,1,0:T(8,128)(2,1)S(1)}, bf16[16,256,128]{2,1,0:T(8,128)(2,1)}, u32[]{:S(2)}) copy-start(bf16[16,256,128]{2,1,0:T(8,128)(2,1)} %kernels.1) | copy-start | bytes 3145732
  4.8 3.4 %copy-start = (bf16[4,512,128]{2,1,0:T(8,128)(2,1)S(1)}, bf16[4,512,128]{2,1,0:T(8,128)(2,1)}, u32[]{:S(2)}) copy-start(bf16[4,512,128]{2,1,0:T(8,128)(2,1)} %model.1) | copy-start | bytes 1572868
  4.8 3.4 %copy-start.1 = (bf16[4,16,256]{2,1,0:T(8,128)(2,1)S(1)}, bf16[4,16,256]{2,1,0:T(8,128)(2,1)}, u32[]{:S(2)}) copy-start(bf16[4,16,256]{2,1,0:T(8,128)(2,1)} %observed.5) | copy-start | bytes 98308
  11.2 14.0 %all-to-all-start = ((bf16[4,576,128]{2,1,0:T(8,128)(2,1)}), bf16[4,576,128]{2,1,0:T(8,128)(2,1)}, u32[]{:S(2)}, u32[]{:S(2)}) async-start(bf16[4,576,128]{2,1,0:T(8,128)(2,1)} %shard_map.65), calls=%async_computation | async-start | bytes 1179648 | tf_op jit(solution)/shard_map/all_to_all | solution.py:222
  27.1 19.3 %collective-permute-start.1 = (bf16[128,128]{1,0:T(8,128)(2,1)}, bf16[128,128]{1,0:T(8,128)(2,1)S(1)}, u32[]{:S(2)}, u32[]{:S(2)}) collective-permute-start(bf16[128,128]{1,0:T(8,128)(2,1)} %get-tuple-element.18), channel_id=1, source_target_pairs={{0,4},{1,5},{2,6},{3,7},{4,8},{5,9},{6,10},{7,11},{8,12},{9,13},{1... | collective-permute-start | bytes 98312 | tf_op jit(solution)/shard_map/ppermute | solution.py:29
  31.9 11.4 %copy-start.6 = (bf16[64,128]{1,0:T(8,128)(2,1)S(1)}, bf16[64,128]{1,0:T(8,128)(2,1)}, u32[]{:S(2)}) copy-start(bf16[64,128]{1,0:T(8,128)(2,1)} %get-tuple-element.19) | copy-start | bytes 49156
  31.9 29.2 %copy-start.4 = (f32[576,128]{1,0:T(8,128)S(1)}, f32[576,128]{1,0:T(8,128)}, u32[]{:S(2)}) copy-start(f32[576,128]{1,0:T(8,128)} %get-tuple-element.17) | copy-start | bytes 884740
  32.8 27.7 %collective-permute-start.3 = (bf16[448,128]{1,0:T(8,128)(2,1)}, bf16[448,128]{1,0:T(8,128)(2,1)S(1)}, u32[]{:S(2)}, u32[]{:S(2)}) collective-permute-start(bf16[448,128]{1,0:T(8,128)(2,1)} %get-tuple-element.20), channel_id=1, source_target_pairs={{0,508},{1,509},{2,510},{3,511},{4,504},{5,505},{6,506},{7,507},{8... | collective-permute-start | bytes 344072 | tf_op jit(solution)/shard_map/ppermute | solution.py:29
  43.3 17.8 %collective-permute-start.2 = (bf16[64,128]{1,0:T(8,128)(2,1)S(1)}, bf16[64,128]{1,0:T(8,128)(2,1)S(1)}, u32[]{:S(2)}, u32[]{:S(2)}) collective-permute-start(bf16[64,128]{1,0:T(8,128)(2,1)S(1)} %copy-done.6), channel_id=1, source_target_pairs={{0,508},{1,509},{2,510},{3,511},{4,0},{5,1},{6,2},{7,3},{8,4},{9,5... | collective-permute-start | bytes 49160 | tf_op jit(solution)/shard_map/ppermute | solution.py:29
  46.4 13.9 %collective-permute-start.4 = (bf16[128,128]{1,0:T(8,128)(2,1)S(1)}, bf16[128,128]{1,0:T(8,128)(2,1)S(1)}, u32[]{:S(2)}, u32[]{:S(2)}) collective-permute-start(bf16[128,128]{1,0:T(8,128)(2,1)S(1)} %add_convert_fusion.3), channel_id=1, source_target_pairs={{0,508},{1,509},{2,510},{3,511},{4,504},{5,505},{6,506},{7,507},{8... | collective-permute-start | bytes 98312 | tf_op jit(solution)/shard_map/ppermute | solution.py:29
  72.9 8.9 %collective-permute-start.5 = (bf16[4,64,128]{2,1,0:T(8,128)(2,1)S(1)}, bf16[4,64,128]{2,1,0:T(8,128)(2,1)S(1)}, u32[]{:S(2)}, u32[]{:S(2)}) collective-permute-start(bf16[4,64,128]{2,1,0:T(8,128)(2,1)S(1)} %get-tuple-element.22), channel_id=1, source_target_pairs={{0,4},{1,5},{2,6},{3,7},{4,8},{5,9},{6,10},{7,11},{8,12},{9,13},{1... | collective-permute-start | bytes 196616 | tf_op jit(solution)/shard_map/ppermute | solution.py:29
  94.1 18.8 %collective-permute-start.6 = (bf16[4,128,128]{2,1,0:T(8,128)(2,1)S(1)}, bf16[4,128,128]{2,1,0:T(8,128)(2,1)S(1)}, u32[]{:S(2)}, u32[]{:S(2)}) collective-permute-start(bf16[4,128,128]{2,1,0:T(8,128)(2,1)S(1)} %convert_element_type.57), channel_id=1, source_target_pairs={{0,511},{1,510},{2,509},{3,508},{4,507},{5,506},{6,505},{7,504},{8... | collective-permute-start | bytes 393224 | tf_op jit(solution)/shard_map/ppermute | solution.py:29
  98.2 15.1 %copy-start.5 = (f32[4]{0:T(128)S(1)}, f32[4]{0:T(128)}, u32[]{:S(2)}) copy-start(f32[4]{0:T(128)} %constant.45.clone) | copy-start | bytes 52

commit v5 on v4

--- a/solution.py
+++ b/solution.py
@@ -27,6 +27,17 @@
             to_tile, to_view = route(tile, view)
             pairs.append((tile * views + view, to_tile % tiles * views + to_view % views))
     return lax.ppermute(value, ("tile", "vis"), pairs)
+
+
+def with_mirror(value, route):
+    tiles = lax.axis_size("tile")
+    views = lax.axis_size("vis")
+    pairs = []
+    for tile in range(tiles // 2):
+        for view in range(views):
+            to_tile, to_view = route(tile, view)
+            pairs.append([tile * views + view, to_tile * views + to_view])
+    return lax.all_gather(value, ("tile", "vis"), axis_index_groups=pairs)
 
 
 def call(body, outs, scratch=(), flops=0, moved=0, vmem=16):
@@ -165,25 +176,53 @@
     tail[...] = acc[:, :SUB]
 
 
-def total_body(parts, own, across, before, after):
-    total = parts[0].astype(F32)
-    for source in range(1, parts.shape[0]):
-        total = total + parts[source].astype(F32)
-    own[...] = total
-    sent = total.astype(BF16)
-    across[...] = sent[SUB:-SUB]
-    before[...] = sent[-2 * SUB :]
-    after[...] = sent[:SUB]
-
-
-def flip(value):
-    return value[..., ::-1, ::-1].astype(F32)
+def backwards(size):
+    row = lax.broadcasted_iota(jnp.int32, (size, size), 0)
+    col = lax.broadcasted_iota(jnp.int32, (size, size), 1)
+    return jnp.where(row + col == size - 1, 1.0, 0.0).astype(BF16)
+
+
+def flipped(value):
+    turned = dot_nn(value, backwards(value.shape[1])).astype(BF16)
+    return dot_nn(backwards(value.shape[0]), turned)
+
+
+def update_body(place, pair, own, before, after, model, halo, out):
+    full = own.shape[0]
+    far = place[0]
+    view = place[1]
+    sign = jnp.where(view % 2 == 0, STEP, -STEP).astype(F32)
+    last = full // SUB - 1
+    for tile in range(last + 1):
+        part = pl.ds(tile * SUB, SUB)
+        total = own[part, :]
+        if tile == 0:
+            total = total + before[SUB:].astype(F32)
+        if tile == last:
+            total = total + after[...].astype(F32)
+            start = halo[view]
+        else:
+            start = model[view, part, :]
+        mirrored = flipped(pair[far, pl.ds((last - tile) * SUB, SUB), :])
+        out[part, :] = (start.astype(F32) + STEP * total + sign * mirrored).astype(BF16)
+
+
+def finish_body(place, pair, own, band, out):
+    far = place[0]
+    quarter = own.shape[1]
+    low = pl.multiple_of(place[1] * quarter, quarter)
+    for comp in range(4):
+        start = band[comp, pl.ds(low, quarter), :].astype(F32)
+        mirrored = flipped(pair[far, comp])
+        step = SIGNS[comp] * STEP
+        out[comp] = (start + STEP * own[comp] + step * mirrored).astype(BF16)
 
 
 def on_device(model, observed, kernels, offsets, counts):
     views = lax.axis_size("vis")
     view = lax.axis_index("vis")
     tiles = lax.axis_size("tile")
+    tile = lax.axis_index("tile")
     rows, cols = model.shape[1:]
     full = rows + SUB
     quarter = rows // views
@@ -220,30 +259,20 @@
     )
 
     parts = lax.all_to_all(partial, "vis", 0, 0, tiled=True)
-    own, across, before, after = call(
-        total_body,
-        (
-            sds((full, cols), F32),
-            sds((rows - SUB, cols), BF16),
-            sds((2 * SUB, cols), BF16),
-            sds((SUB, cols), BF16),
-        ),
-        moved=moved,
-        vmem=58,
-    )(in_specs=[VMEM], out_specs=(VMEM,) * 4)(parts)
-    across = send(across, lambda tile, view: (tiles - 1 - tile, view))
-    before = send(before, lambda tile, view: (tile + 1, view)).astype(F32)
-    after = send(after, lambda tile, view: (tile - 1, view))
-    beside = (before + jnp.pad(own[:SUB], ((SUB, 0), (0, 0)))).astype(BF16)
-    beside = send(beside, lambda tile, view: (tiles - 1 - tile, view))
-    sign = jnp.where(view % 2 == 0, 1.0, -1.0).astype(F32)
-    mine = lax.dynamic_index_in_dim(model, view, 0, keepdims=False)
-    mine_halo = lax.dynamic_index_in_dim(halo, view, 0, keepdims=False)
-    start = jnp.concatenate([mine, mine_halo], axis=0).astype(F32)
-    pad = lambda value, low: jnp.pad(value.astype(F32), ((low, full - low - value.shape[0]), (0, 0)))
-    summed = own + pad(before[SUB:], 0) + pad(after, rows)
-    mirrored = pad(flip(across), 0) + pad(flip(beside), rows - SUB)
-    piece = (start + STEP * (summed + sign * mirrored)).astype(BF16)
+    own = jnp.sum(parts.astype(F32), axis=0)
+    before = send(own[rows - SUB :].astype(BF16), lambda tile, view: (tile + 1, view))
+    after = send(own[:SUB].astype(BF16), lambda tile, view: (tile - 1, view))
+    whole = jnp.pad(own[:rows], ((SUB, 0), (0, 0)))
+    whole = (whole + jnp.pad(before.astype(F32), ((0, full - 2 * SUB), (0, 0)))).astype(BF16)
+    pair = with_mirror(whole, lambda tile, view: (tiles - 1 - tile, view))
+    place = jnp.stack([(tile < tiles // 2).astype(jnp.int32), view])
+    piece = call(
+        update_body,
+        sds((full, cols), BF16),
+        moved=moved,
+    )(in_specs=[SMEM] + [VMEM] * 6, out_specs=VMEM)(
+        place, pair, own, before, after, model, halo
+    )
     band = lax.all_gather(piece, "vis", axis=0, tiled=False)
 
     spill, tail = call(
@@ -269,10 +298,12 @@
     partial = (partial.astype(F32) + spilled).astype(BF16)
     parts = lax.all_to_all(partial, "vis", 0, 0, tiled=True)
     own = jnp.sum(parts.astype(F32), axis=0)
-    across = send(own.astype(BF16), lambda tile, view: (tiles - 1 - tile, views - 1 - view))
-    signs = jnp.array(SIGNS, F32)[:, None, None]
-    start = lax.dynamic_slice_in_dim(band, view * quarter, quarter, 1).astype(F32)
-    return (start + STEP * (own + signs * flip(across))).astype(BF16)
+    pair = with_mirror(own.astype(BF16), lambda tile, view: (tiles - 1 - tile, views - 1 - view))
+    return call(
+        finish_body,
+        sds((4, quarter, cols), BF16),
+        moved=moved,
+    )(in_specs=[SMEM] + [VMEM] * 3, out_specs=VMEM)(place, pair, own, band)
 
 
 def solution(mesh):

time: 115 us -> 112 us (0.974)
  the two profiles are of different devices: /device:TPU:97 before, /device:TPU:1 now
where the time goes in v5:
time: 112 us; the launch traced here: 111 us
  blocking collectives  59.1 us (53%)
  starting transfers between devices  27.9 us (25%)
  Pallas kernels  11.1 us (10%)
  waiting for transfers between devices  8.03 us (7%)
  local copies, waits for them, and re-layouts  2.78 us (2%)
  other arithmetic  1.44 us (1%)
    all_gather x2, blocking collectives, with_mirror(): return lax.all_gather(value, ('tile', 'vis'), axis_index_groups=pairs)  39.7 us
    ppermute x4, starting transfers between devices, send(): return lax.ppermute(value, ('tile', 'vis'), pairs)  23.7 us
    all_gather x1, blocking collectives, on_device(): band = lax.all_gather(piece, 'vis', axis=0, tiled=False)  10 us
    all_to_all x1, blocking collectives, on_device(): parts = lax.all_to_all(partial, 'vis', 0, 0, tiled=True)  9.33 us
    all_to_all x1, waiting for transfers between devices, on_device(): parts = lax.all_to_all(partial, 'vis', 0, 0, tiled=True)  7.34 us
    all_to_all x1, starting transfers between devices, on_device(): parts = lax.all_to_all(partial, 'vis', 0, 0, tiled=True)  4.15 us
    pallas_call x1, Pallas kernels, on_device(): call(first_body, sds((4, full, cols), BF16), [obs, full_rows, full_rows],...  3.01 us
  transfers between devices with their start and end apart: 5, of which 2 were waited for; matrix products, arithmetic and copies ran while one was open for 0% of the time, Pallas kernels for 3%

profile of v5, /device:TPU:1, one launch (start us, length us, event | category | flops | bytes accessed | tf_op | source)
XLA Modules:
  0.0 111.1 jit_solution(10411390156229529394)
XLA Ops:
  0.0 0.8 slice.14
  0.8 8.8 %collective-permute-start = (bf16[4,64,128]{2,1,0:T(8,128)(2,1)S(1)}, bf16[4,64,128]{2,1,0:T(8,128)(2,1)S(1)}, u32[]{:S(2)}, u32[]{:S(2)}) collective-permute-start(bf16[4,64,128]{2,1,0:T(8,128)(2,1)S(1)} %slice.14), channel_id=1, source_target_pairs={{0,508},{1,509},{2,510},{3,511},{4,0},{5,1},{6,2},{7,3},{8,4},{9,5... | collective-permute-start | bytes 196616 | tf_op jit(solution)/shard_map/ppermute | solution.py:29
  9.6 0.7 copy-done.2
  10.3 1.2 %copy-done.4 = bf16[16,256,128]{2,1,0:T(8,128)(2,1)S(1)} copy-done((bf16[16,256,128]{2,1,0:T(8,128)(2,1)S(1)}, bf16[16,256,128]{2,1,0:T(8,128)(2,1)}, u32[]{:S(2)}) %copy-start.4) | copy-done | bytes 1048600
  11.5 1.4 %shard_map.55 = (bf16[16,64,256]{2,1,0:T(8,128)(2,1)S(1)}, bf16[16,128,256]{2,1,0:T(8,128)(2,1)S(1)}, bf16[16,256,128]{2,1,0:T(8,128)(2,1)S(1)}) custom-call(s32[2,16]{1,0:T(2,128)S(1)} %bitcast.12, bf16[16,256,128]{2,1,0:T(8,128)(2,1)S(1)} %copy-done.4), custom_call_target="tpu_custom_call" | custom-call | flops 8589934592 | bytes 4194304 | tf_op jit(solution)/shard_map/pallas_call | solution.py:241
  13.6 3.0 %shard_map.56 = bf16[4,576,128]{2,1,0:T(8,128)(2,1)} custom-call(s32[2,16]{1,0:T(2,128)S(1)} %bitcast.13, s32[1]{0:T(128)S(6)} %copy.6.counts, bf16[4,16,256]{2,1,0:T(8,128)(2,1)S(1)} %copy-done.1, bf16[16,64,256]{2,1,0:T(8,128)(2,1)S(1)} %get-tuple-element.10.ku_t, bf16[16,128,256]{2,1,0:T(8,128)(2,1)S(1)} %get-tuple-element.11.kv_t, ...), custom_call_target="tpu_custom_call" | custom-call | flops 8589934592 | bytes 4194304 | tf_op jit(solution)/shard_map/pallas_call | solution.py:251
  16.6 4.1 %all-to-all-start = ((bf16[4,576,128]{2,1,0:T(8,128)(2,1)}), bf16[4,576,128]{2,1,0:T(8,128)(2,1)}, u32[]{:S(2)}, u32[]{:S(2)}) async-start(bf16[4,576,128]{2,1,0:T(8,128)(2,1)} %shard_map.56), calls=%async_computation | async-start | bytes 1179648 | tf_op jit(solution)/shard_map/all_to_all | solution.py:261
  20.8 7.3 %all-to-all-done = bf16[4,576,128]{2,1,0:T(8,128)(2,1)} async-done(((bf16[4,576,128]{2,1,0:T(8,128)(2,1)}), bf16[4,576,128]{2,1,0:T(8,128)(2,1)}, u32[]{:S(2)}, u32[]{:S(2)}) %all-to-all-start) | async-done | bytes 589856 | tf_op jit(solution)/shard_map/all_to_all | solution.py:261
  28.1 1.2 %convert_reduce_fusion.own = f32[576,128]{1,0:T(8,128)S(1)} fusion(bf16[4,576,128]{2,1,0:T(8,128)(2,1)} %all-to-all-done), kind=kLoop, calls=%fused_computation | loop fusion | flops 516096 | bytes 884736 | tf_op jit(solution)/shard_map/reduce_sum | solution.py:262
  29.3 1.9 %collective-permute-start.1 = (bf16[128,128]{1,0:T(8,128)(2,1)S(1)}, bf16[128,128]{1,0:T(8,128)(2,1)S(1)}, u32[]{:S(2)}, u32[]{:S(2)}) collective-permute-start(bf16[128,128]{1,0:T(8,128)(2,1)S(1)} %slice.19), channel_id=1, source_target_pairs={{0,4},{1,5},{2,6},{3,7},{4,8},{5,9},{6,10},{7,11},{8,12},{9,13},{1... | collective-permute-start | bytes 98312 | tf_op jit(solution)/shard_map/ppermute | solution.py:29
  31.3 0.1 pad_add_fusion.place
  31.4 9.3 %collective-permute-start.2 = (bf16[64,128]{1,0:T(8,128)(2,1)S(1)}, bf16[64,128]{1,0:T(8,128)(2,1)S(1)}, u32[]{:S(2)}, u32[]{:S(2)}) collective-permute-start(bf16[64,128]{1,0:T(8,128)(2,1)S(1)} %slice.20), channel_id=1, source_target_pairs={{0,508},{1,509},{2,510},{3,511},{4,0},{5,1},{6,2},{7,3},{8,4},{9,5... | collective-permute-start | bytes 49160 | tf_op jit(solution)/shard_map/ppermute | solution.py:29
  40.7 18.2 %all-gather = bf16[1152,128]{1,0:T(8,128)(2,1)S(1)} all-gather(bf16[576,128]{1,0:T(8,128)(2,1)S(1)} %add_convert_fusion.1), channel_id=2, replica_groups={{0,508},{1,509},{2,510},{3,511},{4,504},{5,505},{6,506},{7,507},{8,500}..., dimensions={0}, use_global_device_ids=true | all-gather | bytes 442368 | tf_op jit(solution)/shard_map/all_gather | solution.py:40
  58.8 1.9 %shard_map.57 = bf16[576,128]{1,0:T(8,128)(2,1)S(1)} custom-call(s32[2]{0:T(128)S(1)} %pad_add_fusion.place, bf16[2,576,128]{2,1,0:T(8,128)(2,1)S(1)} %bitcast.10, f32[576,128]{1,0:T(8,128)S(1)} %convert_reduce_fusion.own, bf16[128,128]{1,0:T(8,128)(2,1)S(1)} %collective-permute-done.1.before, bf16[64,128]{1,0:T(8,128)(2,1)S(1)} %collective-permute-done.2.after, ...), custom_call_target="tpu_custom_call" | custom-call | bytes 4194304 | tf_op jit(solution)/shard_map/pallas_call | solution.py:269
  60.8 10.0 %all-gather.1 = bf16[2304,128]{1,0:T(8,128)(2,1)S(1)} all-gather(bf16[576,128]{1,0:T(8,128)(2,1)S(1)} %shard_map.57), channel_id=3, replica_groups=mesh['tile'=128,'vis'=4] {'vis'}, dimensions={0}, use_global_device_ids=true | all-gather | bytes 737280 | tf_op jit(solution)/shard_map/all_gather | solution.py:276
  70.8 1.0 shard_map.58
  71.8 3.8 %collective-permute-start.3 = (bf16[4,64,128]{2,1,0:T(8,128)(2,1)S(1)}, bf16[4,64,128]{2,1,0:T(8,128)(2,1)S(1)}, u32[]{:S(2)}, u32[]{:S(2)}) collective-permute-start(bf16[4,64,128]{2,1,0:T(8,128)(2,1)S(1)} %get-tuple-element.14), channel_id=1, source_target_pairs={{0,4},{1,5},{2,6},{3,7},{4,8},{5,9},{6,10},{7,11},{8,12},{9,13},{1... | collective-permute-start | bytes 196616 | tf_op jit(solution)/shard_map/ppermute | solution.py:29
  75.6 2.2 %shard_map.59 = bf16[4,4,128,128]{3,2,1,0:T(8,128)(2,1)S(1)} custom-call(s32[2,16]{1,0:T(2,128)S(1)} %bitcast.15, s32[1]{0:T(128)S(6)} %copy.6.counts, bf16[4,16,256]{2,1,0:T(8,128)(2,1)S(1)} %copy-done.1, bf16[16,64,256]{2,1,0:T(8,128)(2,1)S(1)} %get-tuple-element.10.ku_t, bf16[16,128,256]{2,1,0:T(8,128)(2,1)S(1)} %get-tuple-element.11.kv_t, ...), custom_call_target="tpu_custom_call" | custom-call | flops 8589934592 | bytes 4194304 | tf_op jit(solution)/shard_map/pallas_call | solution.py:288
  77.8 0.7 collective-permute-done.3
  78.5 0.1 add_convert_fusion
  78.5 9.3 %all_to_all.10 = bf16[4,4,128,128]{3,2,1,0:T(8,128)(2,1)S(1)} all-to-all(bf16[4,4,128,128]{3,2,1,0:T(8,128)(2,1)S(1)} %add_convert_fusion), channel_id=1, replica_groups=mesh['tile'=128,'vis'=4] {'vis'}, dimensions={0} | all-to-all | bytes 1048576 | tf_op jit(solution)/shard_map/all_to_all | solution.py:299
  87.8 0.1 convert_reduce_fusion.1.own
  88.0 21.6 %all-gather.2 = bf16[8,128,128]{2,1,0:T(8,128)(2,1)S(1)} all-gather(bf16[4,128,128]{2,1,0:T(8,128)(2,1)S(1)} %convert_element_type.44), channel_id=4, replica_groups={{0,511},{1,510},{2,509},{3,508},{4,507},{5,506},{6,505},{7,504},{8,503}..., dimensions={0}, use_global_device_ids=true | all-gather | bytes 393216 | tf_op jit(solution)/shard_map/all_gather | solution.py:40
  109.5 1.5 %shard_map.60 = bf16[4,128,128]{2,1,0:T(8,128)(2,1)} custom-call(s32[2]{0:T(128)S(1)} %pad_add_fusion.place, bf16[2,4,128,128]{3,2,1,0:T(8,128)(2,1)S(1)} %bitcast.11, f32[4,128,128]{2,1,0:T(8,128)S(1)} %convert_reduce_fusion.1.own, bf16[4,576,128]{2,1,0:T(8,128)(2,1)S(1)} %bitcast.9), custom_call_target="tpu_custom_call" | custom-call | bytes 4194304 | tf_op jit(solution)/shard_map/pallas_call | solution.py:302
  (17 shorter events, 0.1 us)
Async XLA Ops:
  0.8 12.7 %collective-permute-start = (bf16[4,64,128]{2,1,0:T(8,128)(2,1)S(1)}, bf16[4,64,128]{2,1,0:T(8,128)(2,1)S(1)}, u32[]{:S(2)}, u32[]{:S(2)}) collective-permute-start(bf16[4,64,128]{2,1,0:T(8,128)(2,1)S(1)} %slice.14), channel_id=1, source_target_pairs={{0,508},{1,509},{2,510},{3,511},{4,0},{5,1},{6,2},{7,3},{8,4},{9,5... | collective-permute-start | bytes 196616 | tf_op jit(solution)/shard_map/ppermute | solution.py:29
  9.6 0.7 copy-start.2
  10.3 1.2 %copy-start.4 = (bf16[16,256,128]{2,1,0:T(8,128)(2,1)S(1)}, bf16[16,256,128]{2,1,0:T(8,128)(2,1)}, u32[]{:S(2)}) copy-start(bf16[16,256,128]{2,1,0:T(8,128)(2,1)} %kernels.1) | copy-start | bytes 3145732
  11.5 2.1 %copy-start = (bf16[4,512,128]{2,1,0:T(8,128)(2,1)S(1)}, bf16[4,512,128]{2,1,0:T(8,128)(2,1)}, u32[]{:S(2)}) copy-start(bf16[4,512,128]{2,1,0:T(8,128)(2,1)} %model.3) | copy-start | bytes 1572868
  11.5 2.1 %copy-start.1 = (bf16[4,16,256]{2,1,0:T(8,128)(2,1)S(1)}, bf16[4,16,256]{2,1,0:T(8,128)(2,1)}, u32[]{:S(2)}) copy-start(bf16[4,16,256]{2,1,0:T(8,128)(2,1)} %observed.5) | copy-start | bytes 98308
  16.6 11.5 %all-to-all-start = ((bf16[4,576,128]{2,1,0:T(8,128)(2,1)}), bf16[4,576,128]{2,1,0:T(8,128)(2,1)}, u32[]{:S(2)}, u32[]{:S(2)}) async-start(bf16[4,576,128]{2,1,0:T(8,128)(2,1)} %shard_map.56), calls=%async_computation | async-start | bytes 1179648 | tf_op jit(solution)/shard_map/all_to_all | solution.py:261
  29.3 11.3 %collective-permute-start.1 = (bf16[128,128]{1,0:T(8,128)(2,1)S(1)}, bf16[128,128]{1,0:T(8,128)(2,1)S(1)}, u32[]{:S(2)}, u32[]{:S(2)}) collective-permute-start(bf16[128,128]{1,0:T(8,128)(2,1)S(1)} %slice.19), channel_id=1, source_target_pairs={{0,4},{1,5},{2,6},{3,7},{4,8},{5,9},{6,10},{7,11},{8,12},{9,13},{1... | collective-permute-start | bytes 98312 | tf_op jit(solution)/shard_map/ppermute | solution.py:29
  31.4 27.5 %collective-permute-start.2 = (bf16[64,128]{1,0:T(8,128)(2,1)S(1)}, bf16[64,128]{1,0:T(8,128)(2,1)S(1)}, u32[]{:S(2)}, u32[]{:S(2)}) collective-permute-start(bf16[64,128]{1,0:T(8,128)(2,1)S(1)} %slice.20), channel_id=1, source_target_pairs={{0,508},{1,509},{2,510},{3,511},{4,0},{5,1},{6,2},{7,3},{8,4},{9,5... | collective-permute-start | bytes 49160 | tf_op jit(solution)/shard_map/ppermute | solution.py:29
  58.8 12.0 %copy-start.3 = (s32[16,2]{0,1:T(2,128)S(1)}, s32[16,2]{0,1:T(2,128)}, u32[]{:S(2)}) copy-start(s32[16,2]{0,1:T(2,128)} %param.8) | copy-start | bytes 388
  71.8 6.6 %collective-permute-start.3 = (bf16[4,64,128]{2,1,0:T(8,128)(2,1)S(1)}, bf16[4,64,128]{2,1,0:T(8,128)(2,1)S(1)}, u32[]{:S(2)}, u32[]{:S(2)}) collective-permute-start(bf16[4,64,128]{2,1,0:T(8,128)(2,1)S(1)} %get-tuple-element.14), channel_id=1, source_target_pairs={{0,4},{1,5},{2,6},{3,7},{4,8},{5,9},{6,10},{7,11},{8,12},{9,13},{1... | collective-permute-start | bytes 196616 | tf_op jit(solution)/shard_map/ppermute | solution.py:29

commit v6 on v5

--- a/solution.py
+++ b/solution.py
@@ -84,10 +84,10 @@
         acc[comp, pl.ds(row, SUB), :] += fresh[comp * SUB : (comp + 1) * SUB]
 
 
-def prepare_body(offsets, kernels, ku_t, kv_t, kv):
+def prepare_body(table, kernels, ku_t, kv_t, kv):
     blocks, _, cols = kernels.shape
     for block in range(blocks):
-        both, place = masks(SUB - offsets[1, block], cols)
+        both, place = masks(SUB - table[kernels.shape[0] + block], cols)
         weights = kernels[block]
         turned = dot_nt(both, weights).astype(BF16)
         ku_t[block] = turned[:SUB]
@@ -95,13 +95,13 @@
         kv[block] = dot_nn(weights, place).astype(BF16)
 
 
-def grid_all(offsets, counts, base, obs, ku_t, kv_t, kv, grid, acc):
+def grid_all(table, base, obs, ku_t, kv_t, kv, grid, acc):
     blocks = ku_t.shape[0]
     for group in range(blocks // GROUP):
         staged = []
         for block in range(group * GROUP, (group + 1) * GROUP):
-            row = offsets[0, block]
-            live = (block < counts[0]) & (row <= base)
+            row = table[block]
+            live = (block < table[2 * ku_t.shape[0]]) & (row <= base)
             row = jnp.minimum(row, base)
             along_u = ku_t[block].astype(F32)
             fresh = grid_one(row, live, block, obs, along_u, kv_t[block], kv[block], grid)
@@ -110,35 +110,35 @@
             add_one(row, fresh, acc)
 
 
-def first_body(offsets, counts, observed, ku_t, kv_t, kv, model, halo, out, obs, grid, acc):
+def first_body(table, observed, ku_t, kv_t, kv, model, halo, out, obs, grid, acc):
     rows = model.shape[1]
     obs[...] = observed[...].astype(F32)
     grid[:, :rows] = model[...].astype(F32)
     grid[:, rows:] = halo[...].astype(F32)
     acc[...] = jnp.zeros_like(acc)
-    grid_all(offsets, counts, rows - 1, obs, ku_t, kv_t, kv, grid, acc)
+    grid_all(table, rows - 1, obs, ku_t, kv_t, kv, grid, acc)
     out[...] = acc[...].astype(BF16)
 
 
-def inside_body(offsets, counts, observed, ku_t, kv_t, kv, model, tail, out, obs, grid, acc):
+def inside_body(table, observed, ku_t, kv_t, kv, model, tail, out, obs, grid, acc):
     rows = model.shape[1] - SUB
     base = rows - SUB
     obs[...] = observed[...].astype(F32)
     grid[...] = model[:, :rows].astype(F32)
     acc[:, :base] = jnp.zeros((4, base, acc.shape[2]), F32)
     acc[:, base:] = tail[...]
-    grid_all(offsets, counts, base, obs, ku_t, kv_t, kv, grid, acc)
+    grid_all(table, base, obs, ku_t, kv_t, kv, grid, acc)
     views = out.shape[0]
     quarter = rows // views
     for view in range(views):
         out[view] = acc[:, view * quarter : (view + 1) * quarter].astype(BF16)
 
 
-def cross(picks, offsets, counts, obs, ku_t, kv_t, kv, grid, acc, base):
+def cross(picks, table, obs, ku_t, kv_t, kv, grid, acc, base):
     blocks = ku_t.shape[0]
 
     def add(block, found):
-        good = (block < counts[0]) & (offsets[0, block] > base)
+        good = (block < table[2 * ku_t.shape[0]]) & (table[block] > base)
 
         @pl.when(good)
         def _():
@@ -153,7 +153,7 @@
         for lane in range(2):
             place = 2 * index + lane
             block = picks[jnp.minimum(place, limit - 1)]
-            row = offsets[0, block] - base
+            row = table[block] - base
             along_u = ku_t[block].astype(F32)
             fresh = grid_one(
                 row, place < limit, block, obs, along_u, kv_t[block], kv[block], grid
@@ -166,12 +166,12 @@
     lax.fori_loop(0, (limit + 1) // 2, pair, 0)
 
 
-def border_body(offsets, counts, observed, ku_t, kv_t, kv, model, spill, tail, picks, obs, grid, acc):
+def border_body(table, observed, ku_t, kv_t, kv, model, spill, tail, picks, obs, grid, acc):
     base = model.shape[1] - 2 * SUB
     obs[...] = observed[...].astype(F32)
     grid[...] = model[:, base:].astype(F32)
     acc[...] = jnp.zeros_like(acc)
-    cross(picks, offsets, counts, obs, ku_t, kv_t, kv, grid, acc, base)
+    cross(picks, table, obs, ku_t, kv_t, kv, grid, acc, base)
     spill[...] = acc[:, SUB:].astype(BF16)
     tail[...] = acc[:, :SUB]
 
@@ -182,17 +182,14 @@
     return jnp.where(row + col == size - 1, 1.0, 0.0).astype(BF16)
 
 
-def flipped(value):
-    turned = dot_nn(value, backwards(value.shape[1])).astype(BF16)
-    return dot_nn(backwards(value.shape[0]), turned)
-
-
-def update_body(place, pair, own, before, after, model, halo, out):
+def update_body(table, pair, own, before, after, model, halo, out):
     full = own.shape[0]
-    far = place[0]
-    view = place[1]
+    far = table[table.shape[0] - 2]
+    view = table[table.shape[0] - 1]
     sign = jnp.where(view % 2 == 0, STEP, -STEP).astype(F32)
     last = full // SUB - 1
+    turned = dot_nn(pair[far], backwards(own.shape[1])).astype(BF16)
+    swap = backwards(SUB)
     for tile in range(last + 1):
         part = pl.ds(tile * SUB, SUB)
         total = own[part, :]
@@ -203,17 +200,19 @@
             start = halo[view]
         else:
             start = model[view, part, :]
-        mirrored = flipped(pair[far, pl.ds((last - tile) * SUB, SUB), :])
+        mirrored = dot_nn(swap, turned[(last - tile) * SUB : (last - tile + 1) * SUB])
         out[part, :] = (start.astype(F32) + STEP * total + sign * mirrored).astype(BF16)
 
 
-def finish_body(place, pair, own, band, out):
-    far = place[0]
-    quarter = own.shape[1]
-    low = pl.multiple_of(place[1] * quarter, quarter)
+def finish_body(table, pair, own, band, out):
+    far = table[table.shape[0] - 2]
+    quarter, cols = own.shape[1:]
+    low = pl.multiple_of(table[table.shape[0] - 1] * quarter, quarter)
+    turned = dot_nn(pair[far].reshape(4 * quarter, cols), backwards(cols)).astype(BF16)
+    swap = backwards(quarter)
     for comp in range(4):
         start = band[comp, pl.ds(low, quarter), :].astype(F32)
-        mirrored = flipped(pair[far, comp])
+        mirrored = dot_nn(swap, turned[comp * quarter : (comp + 1) * quarter])
         step = SIGNS[comp] * STEP
         out[comp] = (start + STEP * own[comp] + step * mirrored).astype(BF16)
 
@@ -236,7 +235,10 @@
     flops = 4 * 2 * blocks * depth * cols * SUB * 2
     moved = 4 * 1024 * 1024
 
-    offsets = offsets.T
+    low = tile < tiles // 2
+    table = jnp.concatenate(
+        [offsets[:, 0], offsets[:, 1], counts, jnp.stack([low.astype(jnp.int32), view])]
+    )
     halo = send(model[:, :SUB], lambda tile, view: (tile - 1, view))
     ku_t, kv_t, kv = call(
         prepare_body,
@@ -247,17 +249,18 @@
         ),
         flops=WEIGHT * flops,
         moved=moved,
-    )(in_specs=[SMEM, VMEM], out_specs=(VMEM,) * 3)(offsets, kernels)
+    )(in_specs=[SMEM, VMEM], out_specs=(VMEM,) * 3)(table, kernels)
     partial = call(
         first_body,
         sds((4, full, cols), BF16),
         [obs, full_rows, full_rows],
         flops=WEIGHT * flops,
         moved=moved,
-    )(in_specs=[SMEM] * 2 + [VMEM] * 6, out_specs=VMEM)(
-        offsets, counts, observed, ku_t, kv_t, kv, model, halo
-    )
-
+    )(in_specs=[SMEM] + [VMEM] * 6, out_specs=VMEM)(
+        table, observed, ku_t, kv_t, kv, model, halo
+    )
+
+    partial, table = lax.optimization_barrier((partial, table))
     parts = lax.all_to_all(partial, "vis", 0, 0, tiled=True)
     own = jnp.sum(parts.astype(F32), axis=0)
     before = send(own[rows - SUB :].astype(BF16), lambda tile, view: (tile + 1, view))
@@ -265,13 +268,12 @@
     whole = jnp.pad(own[:rows], ((SUB, 0), (0, 0)))
     whole = (whole + jnp.pad(before.astype(F32), ((0, full - 2 * SUB), (0, 0)))).astype(BF16)
     pair = with_mirror(whole, lambda tile, view: (tiles - 1 - tile, view))
-    place = jnp.stack([(tile < tiles // 2).astype(jnp.int32), view])
     piece = call(
         update_body,
         sds((full, cols), BF16),
         moved=moved,
     )(in_specs=[SMEM] + [VMEM] * 6, out_specs=VMEM)(
-        place, pair, own, before, after, model, halo
+        table, pair, own, before, after, model, halo
     )
     band = lax.all_gather(piece, "vis", axis=0, tiled=False)
 
@@ -281,8 +283,8 @@
         [picks, obs, end_rows, end_rows],
         flops=flops,
         moved=moved,
-    )(in_specs=[SMEM] * 2 + [VMEM] * 5, out_specs=(VMEM, VMEM))(
-        offsets, counts, observed, ku_t, kv_t, kv, band
+    )(in_specs=[SMEM] + [VMEM] * 5, out_specs=(VMEM, VMEM))(
+        table, observed, ku_t, kv_t, kv, band
     )
     spilled = send(spill, lambda tile, view: (tile + 1, view))
     partial = call(
@@ -291,8 +293,8 @@
         [obs, inner_rows, inner_rows],
         flops=WEIGHT * flops,
         moved=moved,
-    )(in_specs=[SMEM] * 2 + [VMEM] * 6, out_specs=VMEM)(
-        offsets, counts, observed, ku_t, kv_t, kv, band, tail
+    )(in_specs=[SMEM] + [VMEM] * 6, out_specs=VMEM)(
+        table, observed, ku_t, kv_t, kv, band, tail
     )
     spilled = jnp.pad(spilled.astype(F32)[None], ((0, views - 1), (0, 0), (0, quarter - SUB), (0, 0)))
     partial = (partial.astype(F32) + spilled).astype(BF16)
@@ -303,7 +305,7 @@
         finish_body,
         sds((4, quarter, cols), BF16),
         moved=moved,
-    )(in_specs=[SMEM] + [VMEM] * 3, out_specs=VMEM)(place, pair, own, band)
+    )(in_specs=[SMEM] + [VMEM] * 3, out_specs=VMEM)(table, pair, own, band)
 
 
 def solution(mesh):

time: 112 us -> 109 us (0.973)
  blocking collectives: 59.1 us -> 69 us
  waiting for transfers between devices: 8.03 us -> 1.32 us
  starting transfers between devices: 27.9 us -> 25 us
  Pallas kernels: 11.1 us -> 9.21 us
  other arithmetic: 1.44 us -> 0.26 us
    all_to_all x1 -> x2, blocking collectives: 9.33 us -> 19 us  [on_device(): parts = lax.all_to_all(partial, 'vis', 0, 0, tiled=True)]
    all_to_all x1 -> x0, waiting for transfers between devices: 7.34 us -> none  [on_device(): parts = lax.all_to_all(partial, 'vis', 0, 0, tiled=True)]
    all_to_all x1 -> x0, starting transfers between devices: 4.15 us -> none  [on_device(): parts = lax.all_to_all(partial, 'vis', 0, 0, tiled=True)]
    ppermute x4, starting transfers between devices: 23.7 us -> 25 us  [send(): return lax.ppermute(value, ('tile', 'vis'), pairs)]
  transfers between devices with their start and end apart: 5 -> 4, of which waited for: 2 -> 1; matrix products, arithmetic and copies ran while one was open for 0% -> 1% of each run, Pallas kernels for 3% -> 3%
where the time goes in v6:
time: 109 us
  blocking collectives  69 us (63%)
  starting transfers between devices  25 us (23%)
  Pallas kernels  9.21 us (8%)
  local copies, waits for them, and re-layouts  2.95 us (3%)
  waiting for transfers between devices  1.32 us (1%)
    all_gather x2, blocking collectives, with_mirror(): return lax.all_gather(value, ('tile', 'vis'), axis_index_groups=pairs)  40 us
    ppermute x4, starting transfers between devices, send(): return lax.ppermute(value, ('tile', 'vis'), pairs)  25 us
    all_to_all x2, blocking collectives, on_device(): parts = lax.all_to_all(partial, 'vis', 0, 0, tiled=True)  19 us
    all_gather x1, blocking collectives, on_device(): band = lax.all_gather(piece, 'vis', axis=0, tiled=False)  10 us
  transfers between devices with their start and end apart: 4, of which 1 were waited for; matrix products, arithmetic and copies ran while one was open for 1% of the time, Pallas kernels for 3%

profile of v6, /device:TPU:1, one launch (start us, length us, event | category | flops | bytes accessed | tf_op | source)
XLA Modules:
  0.0 108.6 jit_solution(1499934599955740416)
XLA Ops:
  0.0 0.8 slice.22
  0.8 8.8 %collective-permute-start = (bf16[4,64,128]{2,1,0:T(8,128)(2,1)S(1)}, bf16[4,64,128]{2,1,0:T(8,128)(2,1)S(1)}, u32[]{:S(2)}, u32[]{:S(2)}) collective-permute-start(bf16[4,64,128]{2,1,0:T(8,128)(2,1)S(1)} %slice.22), channel_id=1, source_target_pairs={{0,508},{1,509},{2,510},{3,511},{4,0},{5,1},{6,2},{7,3},{8,4},{9,5... | collective-permute-start | bytes 196616 | tf_op jit(solution)/shard_map/ppermute | solution.py:29
  10.3 0.8 slice_bitcast_fusion
  11.0 0.1 concatenate.3.table
  11.1 1.2 %copy-done.2 = bf16[16,256,128]{2,1,0:T(8,128)(2,1)S(1)} copy-done((bf16[16,256,128]{2,1,0:T(8,128)(2,1)S(1)}, bf16[16,256,128]{2,1,0:T(8,128)(2,1)}, u32[]{:S(2)}) %copy-start.2) | copy-done | bytes 1048600
  12.4 1.4 %shard_map.55 = (bf16[16,64,256]{2,1,0:T(8,128)(2,1)S(1)}, bf16[16,128,256]{2,1,0:T(8,128)(2,1)S(1)}, bf16[16,256,128]{2,1,0:T(8,128)(2,1)S(1)}) custom-call(s32[35]{0:T(128)S(1)} %concatenate.3.table, bf16[16,256,128]{2,1,0:T(8,128)(2,1)S(1)} %copy-done.2), custom_call_target="tpu_custom_call" | custom-call | flops 8589934592 | bytes 4194304 | tf_op jit(solution)/shard_map/pallas_call | solution.py:243
  13.7 0.0 collective-permute-done.halo
  13.8 2.2 %shard_map.56 = bf16[4,576,128]{2,1,0:T(8,128)(2,1)S(1)} custom-call(s32[35]{0:T(128)S(1)} %concatenate.3.table, bf16[4,16,256]{2,1,0:T(8,128)(2,1)S(1)} %copy-done.1, bf16[16,64,256]{2,1,0:T(8,128)(2,1)S(1)} %get-tuple-element.12.ku_t, bf16[16,128,256]{2,1,0:T(8,128)(2,1)S(1)} %get-tuple-element.13.kv_t, bf16[16,256,128]{2,1,0:T(8,128)(2,1)S(1)} %get-tuple-element.14.kv, ...), custom_call_target="tpu_custom_call" | custom-call | flops 8589934592 | bytes 4194304 | tf_op jit(solution)/shard_map/pallas_call | solution.py:253
  16.0 9.7 %all_to_all.10 = bf16[4,576,128]{2,1,0:T(8,128)(2,1)S(1)} all-to-all(bf16[4,576,128]{2,1,0:T(8,128)(2,1)S(1)} %shard_map.56), channel_id=1, replica_groups=mesh['tile'=128,'vis'=4] {'vis'}, dimensions={0} | all-to-all | bytes 1179648 | tf_op jit(solution)/shard_map/all_to_all | solution.py:264
  25.6 0.1 convert_reduce_fusion.own
  25.7 3.3 %collective-permute-start.1 = (bf16[128,128]{1,0:T(8,128)(2,1)S(1)}, bf16[128,128]{1,0:T(8,128)(2,1)S(1)}, u32[]{:S(2)}, u32[]{:S(2)}) collective-permute-start(bf16[128,128]{1,0:T(8,128)(2,1)S(1)} %slice.27), channel_id=1, source_target_pairs={{0,4},{1,5},{2,6},{3,7},{4,8},{5,9},{6,10},{7,11},{8,12},{9,13},{1... | collective-permute-start | bytes 98312 | tf_op jit(solution)/shard_map/ppermute | solution.py:29
  29.1 9.4 %collective-permute-start.2 = (bf16[64,128]{1,0:T(8,128)(2,1)S(1)}, bf16[64,128]{1,0:T(8,128)(2,1)S(1)}, u32[]{:S(2)}, u32[]{:S(2)}) collective-permute-start(bf16[64,128]{1,0:T(8,128)(2,1)S(1)} %slice.28), channel_id=1, source_target_pairs={{0,508},{1,509},{2,510},{3,511},{4,0},{5,1},{6,2},{7,3},{8,4},{9,5... | collective-permute-start | bytes 49160 | tf_op jit(solution)/shard_map/ppermute | solution.py:29
  38.5 0.0 collective-permute-done.1.before
  38.5 18.4 %all-gather = bf16[1152,128]{1,0:T(8,128)(2,1)S(1)} all-gather(bf16[576,128]{1,0:T(8,128)(2,1)S(1)} %add_convert_fusion.1), channel_id=2, replica_groups={{0,508},{1,509},{2,510},{3,511},{4,504},{5,505},{6,506},{7,507},{8,500}..., dimensions={0}, use_global_device_ids=true | all-gather | bytes 442368 | tf_op jit(solution)/shard_map/all_gather | solution.py:40
  57.0 0.9 shard_map.57
  57.9 10.0 %all-gather.1 = bf16[2304,128]{1,0:T(8,128)(2,1)S(1)} all-gather(bf16[576,128]{1,0:T(8,128)(2,1)S(1)} %shard_map.57), channel_id=3, replica_groups=mesh['tile'=128,'vis'=4] {'vis'}, dimensions={0}, use_global_device_ids=true | all-gather | bytes 737280 | tf_op jit(solution)/shard_map/all_gather | solution.py:278
  67.9 1.0 shard_map.58
  69.0 3.5 %collective-permute-start.3 = (bf16[4,64,128]{2,1,0:T(8,128)(2,1)S(1)}, bf16[4,64,128]{2,1,0:T(8,128)(2,1)S(1)}, u32[]{:S(2)}, u32[]{:S(2)}) collective-permute-start(bf16[4,64,128]{2,1,0:T(8,128)(2,1)S(1)} %get-tuple-element.18), channel_id=1, source_target_pairs={{0,4},{1,5},{2,6},{3,7},{4,8},{5,9},{6,10},{7,11},{8,12},{9,13},{1... | collective-permute-start | bytes 196616 | tf_op jit(solution)/shard_map/ppermute | solution.py:29
  72.5 2.2 %shard_map.59 = bf16[4,4,128,128]{3,2,1,0:T(8,128)(2,1)S(1)} custom-call(s32[35]{0:T(128)S(1)} %concatenate.3.table, bf16[4,16,256]{2,1,0:T(8,128)(2,1)S(1)} %copy-done.1, bf16[16,64,256]{2,1,0:T(8,128)(2,1)S(1)} %get-tuple-element.12.ku_t, bf16[16,128,256]{2,1,0:T(8,128)(2,1)S(1)} %get-tuple-element.13.kv_t, ...), custom_call_target="tpu_custom_call" | custom-call | flops 8589934592 | bytes 4194304 | tf_op jit(solution)/shard_map/pallas_call | solution.py:290
  74.7 1.3 %collective-permute-done.3 = bf16[4,64,128]{2,1,0:T(8,128)(2,1)S(1)} collective-permute-done((bf16[4,64,128]{2,1,0:T(8,128)(2,1)S(1)}, bf16[4,64,128]{2,1,0:T(8,128)(2,1)S(1)}, u32[]{:S(2)}, u32[]{:S(2)}) %collective-permute-start.3) | collective-permute-done | bytes 65568 | tf_op jit(solution)/shard_map/ppermute | solution.py:29
  76.1 9.3 %all_to_all.11 = bf16[4,4,128,128]{3,2,1,0:T(8,128)(2,1)S(1)} all-to-all(bf16[4,4,128,128]{3,2,1,0:T(8,128)(2,1)S(1)} %add_convert_fusion), channel_id=1, replica_groups=mesh['tile'=128,'vis'=4] {'vis'}, dimensions={0} | all-to-all | bytes 1048576 | tf_op jit(solution)/shard_map/all_to_all | solution.py:301
  85.4 0.1 convert_reduce_fusion.1.own
  85.5 21.6 %all-gather.2 = bf16[8,128,128]{2,1,0:T(8,128)(2,1)S(1)} all-gather(bf16[4,128,128]{2,1,0:T(8,128)(2,1)S(1)} %convert_element_type.44), channel_id=4, replica_groups={{0,511},{1,510},{2,509},{3,508},{4,507},{5,506},{6,505},{7,504},{8,503}..., dimensions={0}, use_global_device_ids=true | all-gather | bytes 393216 | tf_op jit(solution)/shard_map/all_gather | solution.py:40
  107.1 1.5 %shard_map.60 = bf16[4,128,128]{2,1,0:T(8,128)(2,1)} custom-call(s32[35]{0:T(128)S(1)} %concatenate.3.table, bf16[2,4,128,128]{3,2,1,0:T(8,128)(2,1)S(1)} %bitcast.14, f32[4,128,128]{2,1,0:T(8,128)S(1)} %convert_reduce_fusion.1.own, bf16[4,576,128]{2,1,0:T(8,128)(2,1)S(1)} %bitcast.12), custom_call_target="tpu_custom_call" | custom-call | bytes 4194304 | tf_op jit(solution)/shard_map/pallas_call | solution.py:304
  (13 shorter events, 0.1 us)
Async XLA Ops:
  0.8 12.9 %collective-permute-start = (bf16[4,64,128]{2,1,0:T(8,128)(2,1)S(1)}, bf16[4,64,128]{2,1,0:T(8,128)(2,1)S(1)}, u32[]{:S(2)}, u32[]{:S(2)}) collective-permute-start(bf16[4,64,128]{2,1,0:T(8,128)(2,1)S(1)} %slice.22), channel_id=1, source_target_pairs={{0,508},{1,509},{2,510},{3,511},{4,0},{5,1},{6,2},{7,3},{8,4},{9,5... | collective-permute-start | bytes 196616 | tf_op jit(solution)/shard_map/ppermute | solution.py:29
  11.1 1.2 %copy-start.2 = (bf16[16,256,128]{2,1,0:T(8,128)(2,1)S(1)}, bf16[16,256,128]{2,1,0:T(8,128)(2,1)}, u32[]{:S(2)}) copy-start(bf16[16,256,128]{2,1,0:T(8,128)(2,1)} %kernels.1) | copy-start | bytes 3145732
  12.4 1.4 %copy-start = (bf16[4,512,128]{2,1,0:T(8,128)(2,1)S(1)}, bf16[4,512,128]{2,1,0:T(8,128)(2,1)}, u32[]{:S(2)}) copy-start(bf16[4,512,128]{2,1,0:T(8,128)(2,1)} %model.3) | copy-start | bytes 1572868
  12.4 1.4 %copy-start.1 = (bf16[4,16,256]{2,1,0:T(8,128)(2,1)S(1)}, bf16[4,16,256]{2,1,0:T(8,128)(2,1)}, u32[]{:S(2)}) copy-start(bf16[4,16,256]{2,1,0:T(8,128)(2,1)} %observed.5) | copy-start | bytes 98308
  25.7 12.8 %collective-permute-start.1 = (bf16[128,128]{1,0:T(8,128)(2,1)S(1)}, bf16[128,128]{1,0:T(8,128)(2,1)S(1)}, u32[]{:S(2)}, u32[]{:S(2)}) collective-permute-start(bf16[128,128]{1,0:T(8,128)(2,1)S(1)} %slice.27), channel_id=1, source_target_pairs={{0,4},{1,5},{2,6},{3,7},{4,8},{5,9},{6,10},{7,11},{8,12},{9,13},{1... | collective-permute-start | bytes 98312 | tf_op jit(solution)/shard_map/ppermute | solution.py:29
  29.1 27.8 %collective-permute-start.2 = (bf16[64,128]{1,0:T(8,128)(2,1)S(1)}, bf16[64,128]{1,0:T(8,128)(2,1)S(1)}, u32[]{:S(2)}, u32[]{:S(2)}) collective-permute-start(bf16[64,128]{1,0:T(8,128)(2,1)S(1)} %slice.28), channel_id=1, source_target_pairs={{0,508},{1,509},{2,510},{3,511},{4,0},{5,1},{6,2},{7,3},{8,4},{9,5... | collective-permute-start | bytes 49160 | tf_op jit(solution)/shard_map/ppermute | solution.py:29
  69.0 7.0 %collective-permute-start.3 = (bf16[4,64,128]{2,1,0:T(8,128)(2,1)S(1)}, bf16[4,64,128]{2,1,0:T(8,128)(2,1)S(1)}, u32[]{:S(2)}, u32[]{:S(2)}) collective-permute-start(bf16[4,64,128]{2,1,0:T(8,128)(2,1)S(1)} %get-tuple-element.18), channel_id=1, source_target_pairs={{0,4},{1,5},{2,6},{3,7},{4,8},{5,9},{6,10},{7,11},{8,12},{9,13},{1... | collective-permute-start | bytes 196616 | tf_op jit(solution)/shard_map/ppermute | solution.py:29

commit v7 on v6

--- a/solution.py
+++ b/solution.py
@@ -63,12 +63,11 @@
     row = lax.broadcasted_iota(jnp.int32, (cols, cols), 0)
     col = lax.broadcasted_iota(jnp.int32, (cols, cols), 1)
     pick = jnp.where(row == col, 1.0, 0.0)[:SUB]
-    place_t = jnp.where((col == row + shift) & (col >= SUB), 1.0, 0.0)
-    place = jnp.where((row == col + shift) & (row >= SUB), 1.0, 0.0)
-    return jnp.concatenate([pick, place_t], axis=0).astype(BF16), place.astype(BF16)
-
-
-def grid_one(row, live, block, obs, along_u, kv_t, kv, grid):
+    place = jnp.where((col == row + shift) & (col >= SUB), 1.0, 0.0)
+    return jnp.concatenate([pick, place], axis=0).astype(BF16)
+
+
+def grid_one(row, live, block, obs, along_u, kv_t, grid):
     patch = jnp.concatenate([grid[comp, pl.ds(row, SUB), :] for comp in range(4)], axis=0)
     inner = dot_nn(patch.astype(BF16), kv_t)
     parts = []
@@ -76,7 +75,7 @@
         seen = jnp.sum(along_u * inner[comp * SUB : (comp + 1) * SUB], axis=0, keepdims=True)
         left = jnp.where(live, obs[comp, pl.ds(block, 1), :] - seen, 0.0)
         parts.append((along_u * left).astype(BF16))
-    return dot_nn(jnp.concatenate(parts, axis=0), kv)
+    return dot_nt(jnp.concatenate(parts, axis=0), kv_t)
 
 
 def add_one(row, fresh, acc):
@@ -84,61 +83,58 @@
         acc[comp, pl.ds(row, SUB), :] += fresh[comp * SUB : (comp + 1) * SUB]
 
 
-def prepare_body(table, kernels, ku_t, kv_t, kv):
+def prepare_body(table, kernels, ku_t, kv_t):
     blocks, _, cols = kernels.shape
     for block in range(blocks):
-        both, place = masks(SUB - table[kernels.shape[0] + block], cols)
-        weights = kernels[block]
-        turned = dot_nt(both, weights).astype(BF16)
+        turned = dot_nt(masks(SUB - table[1, block], cols), kernels[block]).astype(BF16)
         ku_t[block] = turned[:SUB]
         kv_t[block] = turned[SUB:]
-        kv[block] = dot_nn(weights, place).astype(BF16)
-
-
-def grid_all(table, base, obs, ku_t, kv_t, kv, grid, acc):
+
+
+def grid_all(table, base, obs, ku_t, kv_t, grid, acc):
     blocks = ku_t.shape[0]
     for group in range(blocks // GROUP):
         staged = []
         for block in range(group * GROUP, (group + 1) * GROUP):
-            row = table[block]
-            live = (block < table[2 * ku_t.shape[0]]) & (row <= base)
+            row = table[0, block]
+            live = (block < table[2, 0]) & (row <= base)
             row = jnp.minimum(row, base)
             along_u = ku_t[block].astype(F32)
-            fresh = grid_one(row, live, block, obs, along_u, kv_t[block], kv[block], grid)
+            fresh = grid_one(row, live, block, obs, along_u, kv_t[block], grid)
             staged.append((row, fresh))
         for row, fresh in staged:
             add_one(row, fresh, acc)
 
 
-def first_body(table, observed, ku_t, kv_t, kv, model, halo, out, obs, grid, acc):
+def first_body(table, observed, ku_t, kv_t, model, halo, out, obs, grid, acc):
     rows = model.shape[1]
     obs[...] = observed[...].astype(F32)
     grid[:, :rows] = model[...].astype(F32)
     grid[:, rows:] = halo[...].astype(F32)
     acc[...] = jnp.zeros_like(acc)
-    grid_all(table, rows - 1, obs, ku_t, kv_t, kv, grid, acc)
+    grid_all(table, rows - 1, obs, ku_t, kv_t, grid, acc)
     out[...] = acc[...].astype(BF16)
 
 
-def inside_body(table, observed, ku_t, kv_t, kv, model, tail, out, obs, grid, acc):
+def inside_body(table, observed, ku_t, kv_t, model, tail, out, obs, grid, acc):
     rows = model.shape[1] - SUB
     base = rows - SUB
     obs[...] = observed[...].astype(F32)
     grid[...] = model[:, :rows].astype(F32)
     acc[:, :base] = jnp.zeros((4, base, acc.shape[2]), F32)
     acc[:, base:] = tail[...]
-    grid_all(table, base, obs, ku_t, kv_t, kv, grid, acc)
+    grid_all(table, base, obs, ku_t, kv_t, grid, acc)
     views = out.shape[0]
     quarter = rows // views
     for view in range(views):
         out[view] = acc[:, view * quarter : (view + 1) * quarter].astype(BF16)
 
 
-def cross(picks, table, obs, ku_t, kv_t, kv, grid, acc, base):
+def cross(picks, table, obs, ku_t, kv_t, grid, acc, base):
     blocks = ku_t.shape[0]
 
     def add(block, found):
-        good = (block < table[2 * ku_t.shape[0]]) & (table[block] > base)
+        good = (block < table[2, 0]) & (table[0, block] > base)
 
         @pl.when(good)
         def _():
@@ -153,10 +149,10 @@
         for lane in range(2):
             place = 2 * index + lane
             block = picks[jnp.minimum(place, limit - 1)]
-            row = table[block] - base
+            row = table[0, block] - base
             along_u = ku_t[block].astype(F32)
             fresh = grid_one(
-                row, place < limit, block, obs, along_u, kv_t[block], kv[block], grid
+                row, place < limit, block, obs, along_u, kv_t[block], grid
             )
             staged.append((row, fresh))
         for row, fresh in staged:
@@ -166,12 +162,12 @@
     lax.fori_loop(0, (limit + 1) // 2, pair, 0)
 
 
-def border_body(table, observed, ku_t, kv_t, kv, model, spill, tail, picks, obs, grid, acc):
+def border_body(table, observed, ku_t, kv_t, model, spill, tail, picks, obs, grid, acc):
     base = model.shape[1] - 2 * SUB
     obs[...] = observed[...].astype(F32)
     grid[...] = model[:, base:].astype(F32)
     acc[...] = jnp.zeros_like(acc)
-    cross(picks, table, obs, ku_t, kv_t, kv, grid, acc, base)
+    cross(picks, table, obs, ku_t, kv_t, grid, acc, base)
     spill[...] = acc[:, SUB:].astype(BF16)
     tail[...] = acc[:, :SUB]
 
@@ -184,8 +180,8 @@
 
 def update_body(table, pair, own, before, after, model, halo, out):
     full = own.shape[0]
-    far = table[table.shape[0] - 2]
-    view = table[table.shape[0] - 1]
+    far = table[2, 1]
+    view = table[2, 2]
     sign = jnp.where(view % 2 == 0, STEP, -STEP).astype(F32)
     last = full // SUB - 1
     turned = dot_nn(pair[far], backwards(own.shape[1])).astype(BF16)
@@ -204,17 +200,21 @@
         out[part, :] = (start.astype(F32) + STEP * total + sign * mirrored).astype(BF16)
 
 
-def finish_body(table, pair, own, band, out):
-    far = table[table.shape[0] - 2]
+def finish_body(table, pair, own, band, out, done, sems):
+    far = table[2, 1]
     quarter, cols = own.shape[1:]
-    low = pl.multiple_of(table[table.shape[0] - 1] * quarter, quarter)
+    low = pl.multiple_of(table[2, 2] * quarter, quarter)
     turned = dot_nn(pair[far].reshape(4 * quarter, cols), backwards(cols)).astype(BF16)
     swap = backwards(quarter)
+    stores = [pltpu.make_async_copy(done.at[comp], out.at[comp], sems.at[comp]) for comp in range(4)]
     for comp in range(4):
         start = band[comp, pl.ds(low, quarter), :].astype(F32)
         mirrored = dot_nn(swap, turned[comp * quarter : (comp + 1) * quarter])
         step = SIGNS[comp] * STEP
-        out[comp] = (start + STEP * own[comp] + step * mirrored).astype(BF16)
+        done[comp] = (start + STEP * own[comp] + step * mirrored).astype(BF16)
+        stores[comp].start()
+    for store in stores:
+        store.wait()
 
 
 def on_device(model, observed, kernels, offsets, counts):
@@ -236,28 +236,29 @@
     moved = 4 * 1024 * 1024
 
     low = tile < tiles // 2
-    table = jnp.concatenate(
-        [offsets[:, 0], offsets[:, 1], counts, jnp.stack([low.astype(jnp.int32), view])]
-    )
+    row = lax.broadcasted_iota(jnp.int32, (3, blocks), 0)
+    col = lax.broadcasted_iota(jnp.int32, (3, blocks), 1)
+    table = jnp.pad(offsets.T, ((0, 1), (0, 0)))
+    for index, item in enumerate((counts[0], low.astype(jnp.int32), view)):
+        table = table + jnp.where((row == 2) & (col == index), item, 0)
     halo = send(model[:, :SUB], lambda tile, view: (tile - 1, view))
-    ku_t, kv_t, kv = call(
+    ku_t, kv_t = call(
         prepare_body,
         (
             sds((blocks, SUB, depth), BF16),
             sds((blocks, cols, depth), BF16),
-            sds((blocks, depth, cols), BF16),
         ),
         flops=WEIGHT * flops,
         moved=moved,
-    )(in_specs=[SMEM, VMEM], out_specs=(VMEM,) * 3)(table, kernels)
+    )(in_specs=[SMEM, VMEM], out_specs=(VMEM, VMEM))(table, kernels)
     partial = call(
         first_body,
         sds((4, full, cols), BF16),
         [obs, full_rows, full_rows],
         flops=WEIGHT * flops,
         moved=moved,
-    )(in_specs=[SMEM] + [VMEM] * 6, out_specs=VMEM)(
-        table, observed, ku_t, kv_t, kv, model, halo
+    )(in_specs=[SMEM] + [VMEM] * 5, out_specs=VMEM)(
+        table, observed, ku_t, kv_t, model, halo
     )
 
     partial, table = lax.optimization_barrier((partial, table))
@@ -283,8 +284,8 @@
         [picks, obs, end_rows, end_rows],
         flops=flops,
         moved=moved,
-    )(in_specs=[SMEM] + [VMEM] * 5, out_specs=(VMEM, VMEM))(
-        table, observed, ku_t, kv_t, kv, band
+    )(in_specs=[SMEM] + [VMEM] * 4, out_specs=(VMEM, VMEM))(
+        table, observed, ku_t, kv_t, band
     )
     spilled = send(spill, lambda tile, view: (tile + 1, view))
     partial = call(
@@ -293,8 +294,8 @@
         [obs, inner_rows, inner_rows],
         flops=WEIGHT * flops,
         moved=moved,
-    )(in_specs=[SMEM] + [VMEM] * 6, out_specs=VMEM)(
-        table, observed, ku_t, kv_t, kv, band, tail
+    )(in_specs=[SMEM] + [VMEM] * 5, out_specs=VMEM)(
+        table, observed, ku_t, kv_t, band, tail
     )
     spilled = jnp.pad(spilled.astype(F32)[None], ((0, views - 1), (0, 0), (0, quarter - SUB), (0, 0)))
     partial = (partial.astype(F32) + spilled).astype(BF16)
@@ -304,8 +305,9 @@
     return call(
         finish_body,
         sds((4, quarter, cols), BF16),
-        moved=moved,
-    )(in_specs=[SMEM] + [VMEM] * 3, out_specs=VMEM)(table, pair, own, band)
+        [pltpu.VMEM((4, quarter, cols), BF16), pltpu.SemaphoreType.DMA((4,))],
+        moved=moved,
+    )(in_specs=[SMEM] + [VMEM] * 3, out_specs=pl.BlockSpec(memory_space=pltpu.HBM))(table, pair, own, band)
 
 
 def solution(mesh):

time: 109 us -> 109 us (level)
  no operation moved by 1% of the time
where the time goes in v7:
time: 109 us; the launch traced here: 108 us
  blocking collectives  69 us (63%)
  starting transfers between devices  25.1 us (23%)
  Pallas kernels  8.67 us (8%)
  local copies, waits for them, and re-layouts  2.1 us (2%)
  waiting for transfers between devices  1.67 us (2%)
    all_gather x2, blocking collectives, with_mirror(): return lax.all_gather(value, ('tile', 'vis'), axis_index_groups=pairs)  40 us
    ppermute x4, starting transfers between devices, send(): return lax.ppermute(value, ('tile', 'vis'), pairs)  25.1 us
    all_to_all x2, blocking collectives, on_device(): parts = lax.all_to_all(partial, 'vis', 0, 0, tiled=True)  19 us
    all_gather x1, blocking collectives, on_device(): band = lax.all_gather(piece, 'vis', axis=0, tiled=False)  10 us
    pallas_call x1, Pallas kernels, on_device(): call(first_body, sds((4, full, cols), BF16), [obs, full_rows, full_rows],...  2.2 us
  transfers between devices with their start and end apart: 4, of which 1 were waited for; matrix products, arithmetic and copies ran while one was open for 1% of the time, Pallas kernels for 3%

profile of v7, /device:TPU:1, one launch (start us, length us, event | category | flops | bytes accessed | tf_op | source)
XLA Modules:
  0.0 108.4 jit_solution(15538358230859767085)
XLA Ops:
  0.0 0.8 slice.14
  0.8 8.8 %collective-permute-start = (bf16[4,64,128]{2,1,0:T(8,128)(2,1)S(1)}, bf16[4,64,128]{2,1,0:T(8,128)(2,1)S(1)}, u32[]{:S(2)}, u32[]{:S(2)}) collective-permute-start(bf16[4,64,128]{2,1,0:T(8,128)(2,1)S(1)} %slice.14), channel_id=1, source_target_pairs={{0,508},{1,509},{2,510},{3,511},{4,0},{5,1},{6,2},{7,3},{8,4},{9,5... | collective-permute-start | bytes 196616 | tf_op jit(solution)/shard_map/ppermute | solution.py:29
  10.3 0.8 select_add_fusion.table
  11.1 1.2 %copy-done.2 = bf16[16,256,128]{2,1,0:T(8,128)(2,1)S(1)} copy-done((bf16[16,256,128]{2,1,0:T(8,128)(2,1)S(1)}, bf16[16,256,128]{2,1,0:T(8,128)(2,1)}, u32[]{:S(2)}) %copy-start.2) | copy-done | bytes 1048600
  12.3 1.1 %shard_map.55 = (bf16[16,64,256]{2,1,0:T(8,128)(2,1)S(1)}, bf16[16,128,256]{2,1,0:T(8,128)(2,1)S(1)}) custom-call(s32[3,16]{1,0:T(4,128)S(1)} %select_add_fusion.table, bf16[16,256,128]{2,1,0:T(8,128)(2,1)S(1)} %copy-done.2), custom_call_target="tpu_custom_call" | custom-call | flops 8589934592 | bytes 4194304 | tf_op jit(solution)/shard_map/pallas_call | solution.py:245
  13.5 0.0 collective-permute-done.halo
  13.5 2.2 %shard_map.56 = bf16[4,576,128]{2,1,0:T(8,128)(2,1)S(1)} custom-call(s32[3,16]{1,0:T(4,128)S(1)} %select_add_fusion.table, bf16[4,16,256]{2,1,0:T(8,128)(2,1)S(1)} %copy-done.1, bf16[16,64,256]{2,1,0:T(8,128)(2,1)S(1)} %get-tuple-element.11.ku_t, bf16[16,128,256]{2,1,0:T(8,128)(2,1)S(1)} %get-tuple-element.12.kv_t, bf16[4,512,128]{2,1,0:T(8,128)(2,1)S(1)} %copy-done, ...), custom_call_target="tpu_custom_call" | custom-call | flops 8589934592 | bytes 4194304 | tf_op jit(solution)/shard_map/pallas_call | solution.py:254
  15.7 9.7 %all_to_all.10 = bf16[4,576,128]{2,1,0:T(8,128)(2,1)S(1)} all-to-all(bf16[4,576,128]{2,1,0:T(8,128)(2,1)S(1)} %shard_map.56), channel_id=1, replica_groups=mesh['tile'=128,'vis'=4] {'vis'}, dimensions={0} | all-to-all | bytes 1179648 | tf_op jit(solution)/shard_map/all_to_all | solution.py:265
  25.4 0.1 convert_reduce_fusion.own
  25.5 3.3 %collective-permute-start.1 = (bf16[128,128]{1,0:T(8,128)(2,1)S(1)}, bf16[128,128]{1,0:T(8,128)(2,1)S(1)}, u32[]{:S(2)}, u32[]{:S(2)}) collective-permute-start(bf16[128,128]{1,0:T(8,128)(2,1)S(1)} %slice.19), channel_id=1, source_target_pairs={{0,4},{1,5},{2,6},{3,7},{4,8},{5,9},{6,10},{7,11},{8,12},{9,13},{1... | collective-permute-start | bytes 98312 | tf_op jit(solution)/shard_map/ppermute | solution.py:29
  28.9 9.3 %collective-permute-start.2 = (bf16[64,128]{1,0:T(8,128)(2,1)S(1)}, bf16[64,128]{1,0:T(8,128)(2,1)S(1)}, u32[]{:S(2)}, u32[]{:S(2)}) collective-permute-start(bf16[64,128]{1,0:T(8,128)(2,1)S(1)} %slice.20), channel_id=1, source_target_pairs={{0,508},{1,509},{2,510},{3,511},{4,0},{5,1},{6,2},{7,3},{8,4},{9,5... | collective-permute-start | bytes 49160 | tf_op jit(solution)/shard_map/ppermute | solution.py:29
  38.2 0.0 collective-permute-done.1.before
  38.3 18.1 %all-gather = bf16[1152,128]{1,0:T(8,128)(2,1)S(1)} all-gather(bf16[576,128]{1,0:T(8,128)(2,1)S(1)} %add_convert_fusion.1), channel_id=2, replica_groups={{0,508},{1,509},{2,510},{3,511},{4,504},{5,505},{6,506},{7,507},{8,500}..., dimensions={0}, use_global_device_ids=true | all-gather | bytes 442368 | tf_op jit(solution)/shard_map/all_gather | solution.py:40
  56.4 1.0 shard_map.57
  57.4 10.0 %all-gather.1 = bf16[2304,128]{1,0:T(8,128)(2,1)S(1)} all-gather(bf16[576,128]{1,0:T(8,128)(2,1)S(1)} %shard_map.57), channel_id=3, replica_groups=mesh['tile'=128,'vis'=4] {'vis'}, dimensions={0}, use_global_device_ids=true | all-gather | bytes 737280 | tf_op jit(solution)/shard_map/all_gather | solution.py:279
  67.4 0.6 shard_map.58
  68.1 3.6 %collective-permute-start.3 = (bf16[4,64,128]{2,1,0:T(8,128)(2,1)S(1)}, bf16[4,64,128]{2,1,0:T(8,128)(2,1)S(1)}, u32[]{:S(2)}, u32[]{:S(2)}) collective-permute-start(bf16[4,64,128]{2,1,0:T(8,128)(2,1)S(1)} %get-tuple-element.16), channel_id=1, source_target_pairs={{0,4},{1,5},{2,6},{3,7},{4,8},{5,9},{6,10},{7,11},{8,12},{9,13},{1... | collective-permute-start | bytes 196616 | tf_op jit(solution)/shard_map/ppermute | solution.py:29
  71.7 2.2 %shard_map.59 = bf16[4,4,128,128]{3,2,1,0:T(8,128)(2,1)S(1)} custom-call(s32[3,16]{1,0:T(4,128)S(1)} %select_add_fusion.table, bf16[4,16,256]{2,1,0:T(8,128)(2,1)S(1)} %copy-done.1, bf16[16,64,256]{2,1,0:T(8,128)(2,1)S(1)} %get-tuple-element.11.ku_t, bf16[16,128,256]{2,1,0:T(8,128)(2,1)S(1)} %get-tuple-element.12.kv_t, bf16[4,576,128]{2,1,0:T(8,128)(2,1)S(1)} %bitcast.8, ...), custom_call_target="tpu_custom_call" | custom-call | flops 8589934592 | bytes 4194304 | tf_op jit(solution)/shard_map/pallas_call | solution.py:291
  73.9 1.7 %collective-permute-done.3 = bf16[4,64,128]{2,1,0:T(8,128)(2,1)S(1)} collective-permute-done((bf16[4,64,128]{2,1,0:T(8,128)(2,1)S(1)}, bf16[4,64,128]{2,1,0:T(8,128)(2,1)S(1)}, u32[]{:S(2)}, u32[]{:S(2)}) %collective-permute-start.3) | collective-permute-done | bytes 65568 | tf_op jit(solution)/shard_map/ppermute | solution.py:29
  75.5 0.1 add_convert_fusion
  75.6 9.3 %all_to_all.11 = bf16[4,4,128,128]{3,2,1,0:T(8,128)(2,1)S(1)} all-to-all(bf16[4,4,128,128]{3,2,1,0:T(8,128)(2,1)S(1)} %add_convert_fusion), channel_id=1, replica_groups=mesh['tile'=128,'vis'=4] {'vis'}, dimensions={0} | all-to-all | bytes 1048576 | tf_op jit(solution)/shard_map/all_to_all | solution.py:302
  84.9 0.1 convert_reduce_fusion.1.own
  85.0 21.8 %all-gather.2 = bf16[8,128,128]{2,1,0:T(8,128)(2,1)S(1)} all-gather(bf16[4,128,128]{2,1,0:T(8,128)(2,1)S(1)} %convert_element_type.47), channel_id=4, replica_groups={{0,511},{1,510},{2,509},{3,508},{4,507},{5,506},{6,505},{7,504},{8,503}..., dimensions={0}, use_global_device_ids=true | all-gather | bytes 393216 | tf_op jit(solution)/shard_map/all_gather | solution.py:40
  106.9 1.6 %shard_map.60 = bf16[4,128,128]{2,1,0:T(8,128)(2,1)} custom-call(s32[3,16]{1,0:T(4,128)S(1)} %select_add_fusion.table, bf16[2,4,128,128]{3,2,1,0:T(8,128)(2,1)S(1)} %bitcast.11, f32[4,128,128]{2,1,0:T(8,128)S(1)} %convert_reduce_fusion.1.own, bf16[4,576,128]{2,1,0:T(8,128)(2,1)S(1)} %bitcast.9), custom_call_target="tpu_custom_call" | custom-call | bytes 4194304 | tf_op jit(solution)/shard_map/pallas_call | solution.py:305
  (15 shorter events, 0.1 us)
Async XLA Ops:
  0.8 12.6 %collective-permute-start = (bf16[4,64,128]{2,1,0:T(8,128)(2,1)S(1)}, bf16[4,64,128]{2,1,0:T(8,128)(2,1)S(1)}, u32[]{:S(2)}, u32[]{:S(2)}) collective-permute-start(bf16[4,64,128]{2,1,0:T(8,128)(2,1)S(1)} %slice.14), channel_id=1, source_target_pairs={{0,508},{1,509},{2,510},{3,511},{4,0},{5,1},{6,2},{7,3},{8,4},{9,5... | collective-permute-start | bytes 196616 | tf_op jit(solution)/shard_map/ppermute | solution.py:29
  11.1 1.2 %copy-start.2 = (bf16[16,256,128]{2,1,0:T(8,128)(2,1)S(1)}, bf16[16,256,128]{2,1,0:T(8,128)(2,1)}, u32[]{:S(2)}) copy-start(bf16[16,256,128]{2,1,0:T(8,128)(2,1)} %kernels.1) | copy-start | bytes 3145732
  12.3 1.2 %copy-start = (bf16[4,512,128]{2,1,0:T(8,128)(2,1)S(1)}, bf16[4,512,128]{2,1,0:T(8,128)(2,1)}, u32[]{:S(2)}) copy-start(bf16[4,512,128]{2,1,0:T(8,128)(2,1)} %model.3) | copy-start | bytes 1572868
  12.3 1.2 %copy-start.1 = (bf16[4,16,256]{2,1,0:T(8,128)(2,1)S(1)}, bf16[4,16,256]{2,1,0:T(8,128)(2,1)}, u32[]{:S(2)}) copy-start(bf16[4,16,256]{2,1,0:T(8,128)(2,1)} %observed.5) | copy-start | bytes 98308
  25.5 12.7 %collective-permute-start.1 = (bf16[128,128]{1,0:T(8,128)(2,1)S(1)}, bf16[128,128]{1,0:T(8,128)(2,1)S(1)}, u32[]{:S(2)}, u32[]{:S(2)}) collective-permute-start(bf16[128,128]{1,0:T(8,128)(2,1)S(1)} %slice.19), channel_id=1, source_target_pairs={{0,4},{1,5},{2,6},{3,7},{4,8},{5,9},{6,10},{7,11},{8,12},{9,13},{1... | collective-permute-start | bytes 98312 | tf_op jit(solution)/shard_map/ppermute | solution.py:29
  28.9 27.5 %collective-permute-start.2 = (bf16[64,128]{1,0:T(8,128)(2,1)S(1)}, bf16[64,128]{1,0:T(8,128)(2,1)S(1)}, u32[]{:S(2)}, u32[]{:S(2)}) collective-permute-start(bf16[64,128]{1,0:T(8,128)(2,1)S(1)} %slice.20), channel_id=1, source_target_pairs={{0,508},{1,509},{2,510},{3,511},{4,0},{5,1},{6,2},{7,3},{8,4},{9,5... | collective-permute-start | bytes 49160 | tf_op jit(solution)/shard_map/ppermute | solution.py:29
  68.1 7.5 %collective-permute-start.3 = (bf16[4,64,128]{2,1,0:T(8,128)(2,1)S(1)}, bf16[4,64,128]{2,1,0:T(8,128)(2,1)S(1)}, u32[]{:S(2)}, u32[]{:S(2)}) collective-permute-start(bf16[4,64,128]{2,1,0:T(8,128)(2,1)S(1)} %get-tuple-element.16), channel_id=1, source_target_pairs={{0,4},{1,5},{2,6},{3,7},{4,8},{5,9},{6,10},{7,11},{8,12},{9,13},{1... | collective-permute-start | bytes 196616 | tf_op jit(solution)/shard_map/ppermute | solution.py:29

commit v8 on v7

--- a/solution.py
+++ b/solution.py
@@ -144,10 +144,10 @@
 
     limit = lax.fori_loop(0, blocks, add, 0, unroll=True)
 
-    def pair(index, carry):
+    def four(index, carry):
         staged = []
-        for lane in range(2):
-            place = 2 * index + lane
+        for lane in range(4):
+            place = 4 * index + lane
             block = picks[jnp.minimum(place, limit - 1)]
             row = table[0, block] - base
             along_u = ku_t[block].astype(F32)
@@ -159,7 +159,7 @@
             add_one(row, fresh, acc)
         return carry
 
-    lax.fori_loop(0, (limit + 1) // 2, pair, 0)
+    lax.fori_loop(0, (limit + 3) // 4, four, 0)
 
 
 def border_body(table, observed, ku_t, kv_t, model, spill, tail, picks, obs, grid, acc):

time: 109 us -> 108 us (level)
  no operation moved by 1% of the time
where the time goes in v8:
time: 108 us
  blocking collectives  68.9 us (64%)
  starting transfers between devices  25.3 us (23%)
  Pallas kernels  8.66 us (8%)
  local copies, waits for them, and re-layouts  2.1 us (2%)
  waiting for transfers between devices  1.18 us (1%)
    all_gather x2, blocking collectives, with_mirror(): return lax.all_gather(value, ('tile', 'vis'), axis_index_groups=pairs)  39.9 us
    ppermute x4, starting transfers between devices, send(): return lax.ppermute(value, ('tile', 'vis'), pairs)  25.3 us
    all_to_all x2, blocking collectives, on_device(): parts = lax.all_to_all(partial, 'vis', 0, 0, tiled=True)  19 us
    all_gather x1, blocking collectives, on_device(): band = lax.all_gather(piece, 'vis', axis=0, tiled=False)  10 us
    pallas_call x1, Pallas kernels, on_device(): call(first_body, sds((4, full, cols), BF16), [obs, full_rows, full_rows],...  2.2 us
    pallas_call x1, Pallas kernels, on_device(): call(inside_body, sds((views, 4, quarter, cols), BF16), [obs, inner_rows,...  2.16 us
  transfers between devices with their start and end apart: 4, of which 1 were waited for; matrix products, arithmetic and copies ran while one was open for 1% of the time, Pallas kernels for 3%

profile of v8, /device:TPU:1, one launch (start us, length us, event | category | flops | bytes accessed | tf_op | source)
XLA Modules:
  0.0 108.0 jit_solution(9648589678370380634)
XLA Ops:
  0.0 0.8 slice.14
  0.8 8.8 %collective-permute-start = (bf16[4,64,128]{2,1,0:T(8,128)(2,1)S(1)}, bf16[4,64,128]{2,1,0:T(8,128)(2,1)S(1)}, u32[]{:S(2)}, u32[]{:S(2)}) collective-permute-start(bf16[4,64,128]{2,1,0:T(8,128)(2,1)S(1)} %slice.14), channel_id=1, source_target_pairs={{0,508},{1,509},{2,510},{3,511},{4,0},{5,1},{6,2},{7,3},{8,4},{9,5... | collective-permute-start | bytes 196616 | tf_op jit(solution)/shard_map/ppermute | solution.py:29
  10.3 0.8 select_add_fusion.table
  11.1 1.2 %copy-done.2 = bf16[16,256,128]{2,1,0:T(8,128)(2,1)S(1)} copy-done((bf16[16,256,128]{2,1,0:T(8,128)(2,1)S(1)}, bf16[16,256,128]{2,1,0:T(8,128)(2,1)}, u32[]{:S(2)}) %copy-start.2) | copy-done | bytes 1048600
  12.3 1.1 %shard_map.55 = (bf16[16,64,256]{2,1,0:T(8,128)(2,1)S(1)}, bf16[16,128,256]{2,1,0:T(8,128)(2,1)S(1)}) custom-call(s32[3,16]{1,0:T(4,128)S(1)} %select_add_fusion.table, bf16[16,256,128]{2,1,0:T(8,128)(2,1)S(1)} %copy-done.2), custom_call_target="tpu_custom_call" | custom-call | flops 8589934592 | bytes 4194304 | tf_op jit(solution)/shard_map/pallas_call | solution.py:245
  13.5 0.0 collective-permute-done.halo
  13.5 2.2 %shard_map.56 = bf16[4,576,128]{2,1,0:T(8,128)(2,1)S(1)} custom-call(s32[3,16]{1,0:T(4,128)S(1)} %select_add_fusion.table, bf16[4,16,256]{2,1,0:T(8,128)(2,1)S(1)} %copy-done.1, bf16[16,64,256]{2,1,0:T(8,128)(2,1)S(1)} %get-tuple-element.11.ku_t, bf16[16,128,256]{2,1,0:T(8,128)(2,1)S(1)} %get-tuple-element.12.kv_t, bf16[4,512,128]{2,1,0:T(8,128)(2,1)S(1)} %copy-done, ...), custom_call_target="tpu_custom_call" | custom-call | flops 8589934592 | bytes 4194304 | tf_op jit(solution)/shard_map/pallas_call | solution.py:254
  15.7 9.7 %all_to_all.10 = bf16[4,576,128]{2,1,0:T(8,128)(2,1)S(1)} all-to-all(bf16[4,576,128]{2,1,0:T(8,128)(2,1)S(1)} %shard_map.56), channel_id=1, replica_groups=mesh['tile'=128,'vis'=4] {'vis'}, dimensions={0} | all-to-all | bytes 1179648 | tf_op jit(solution)/shard_map/all_to_all | solution.py:265
  25.4 0.1 convert_reduce_fusion.own
  25.5 3.3 %collective-permute-start.1 = (bf16[128,128]{1,0:T(8,128)(2,1)S(1)}, bf16[128,128]{1,0:T(8,128)(2,1)S(1)}, u32[]{:S(2)}, u32[]{:S(2)}) collective-permute-start(bf16[128,128]{1,0:T(8,128)(2,1)S(1)} %slice.19), channel_id=1, source_target_pairs={{0,4},{1,5},{2,6},{3,7},{4,8},{5,9},{6,10},{7,11},{8,12},{9,13},{1... | collective-permute-start | bytes 98312 | tf_op jit(solution)/shard_map/ppermute | solution.py:29
  28.9 9.3 %collective-permute-start.2 = (bf16[64,128]{1,0:T(8,128)(2,1)S(1)}, bf16[64,128]{1,0:T(8,128)(2,1)S(1)}, u32[]{:S(2)}, u32[]{:S(2)}) collective-permute-start(bf16[64,128]{1,0:T(8,128)(2,1)S(1)} %slice.20), channel_id=1, source_target_pairs={{0,508},{1,509},{2,510},{3,511},{4,0},{5,1},{6,2},{7,3},{8,4},{9,5... | collective-permute-start | bytes 49160 | tf_op jit(solution)/shard_map/ppermute | solution.py:29
  38.3 18.1 %all-gather = bf16[1152,128]{1,0:T(8,128)(2,1)S(1)} all-gather(bf16[576,128]{1,0:T(8,128)(2,1)S(1)} %add_convert_fusion.1), channel_id=2, replica_groups={{0,508},{1,509},{2,510},{3,511},{4,504},{5,505},{6,506},{7,507},{8,500}..., dimensions={0}, use_global_device_ids=true | all-gather | bytes 442368 | tf_op jit(solution)/shard_map/all_gather | solution.py:40
  56.3 0.0 collective-permute-done.2.after
  56.3 1.0 shard_map.57
  57.3 10.0 %all-gather.1 = bf16[2304,128]{1,0:T(8,128)(2,1)S(1)} all-gather(bf16[576,128]{1,0:T(8,128)(2,1)S(1)} %shard_map.57), channel_id=3, replica_groups=mesh['tile'=128,'vis'=4] {'vis'}, dimensions={0}, use_global_device_ids=true | all-gather | bytes 737280 | tf_op jit(solution)/shard_map/all_gather | solution.py:279
  67.3 0.6 shard_map.58
  68.0 3.8 %collective-permute-start.3 = (bf16[4,64,128]{2,1,0:T(8,128)(2,1)S(1)}, bf16[4,64,128]{2,1,0:T(8,128)(2,1)S(1)}, u32[]{:S(2)}, u32[]{:S(2)}) collective-permute-start(bf16[4,64,128]{2,1,0:T(8,128)(2,1)S(1)} %get-tuple-element.16), channel_id=1, source_target_pairs={{0,4},{1,5},{2,6},{3,7},{4,8},{5,9},{6,10},{7,11},{8,12},{9,13},{1... | collective-permute-start | bytes 196616 | tf_op jit(solution)/shard_map/ppermute | solution.py:29
  71.8 2.2 %shard_map.59 = bf16[4,4,128,128]{3,2,1,0:T(8,128)(2,1)S(1)} custom-call(s32[3,16]{1,0:T(4,128)S(1)} %select_add_fusion.table, bf16[4,16,256]{2,1,0:T(8,128)(2,1)S(1)} %copy-done.1, bf16[16,64,256]{2,1,0:T(8,128)(2,1)S(1)} %get-tuple-element.11.ku_t, bf16[16,128,256]{2,1,0:T(8,128)(2,1)S(1)} %get-tuple-element.12.kv_t, bf16[4,576,128]{2,1,0:T(8,128)(2,1)S(1)} %bitcast.8, ...), custom_call_target="tpu_custom_call" | custom-call | flops 8589934592 | bytes 4194304 | tf_op jit(solution)/shard_map/pallas_call | solution.py:291
  74.0 1.2 %collective-permute-done.3 = bf16[4,64,128]{2,1,0:T(8,128)(2,1)S(1)} collective-permute-done((bf16[4,64,128]{2,1,0:T(8,128)(2,1)S(1)}, bf16[4,64,128]{2,1,0:T(8,128)(2,1)S(1)}, u32[]{:S(2)}, u32[]{:S(2)}) %collective-permute-start.3) | collective-permute-done | bytes 65568 | tf_op jit(solution)/shard_map/ppermute | solution.py:29
  75.2 0.1 add_convert_fusion
  75.2 9.3 %all_to_all.11 = bf16[4,4,128,128]{3,2,1,0:T(8,128)(2,1)S(1)} all-to-all(bf16[4,4,128,128]{3,2,1,0:T(8,128)(2,1)S(1)} %add_convert_fusion), channel_id=1, replica_groups=mesh['tile'=128,'vis'=4] {'vis'}, dimensions={0} | all-to-all | bytes 1048576 | tf_op jit(solution)/shard_map/all_to_all | solution.py:302
  84.6 0.1 convert_reduce_fusion.1.own
  84.7 21.8 %all-gather.2 = bf16[8,128,128]{2,1,0:T(8,128)(2,1)S(1)} all-gather(bf16[4,128,128]{2,1,0:T(8,128)(2,1)S(1)} %convert_element_type.47), channel_id=4, replica_groups={{0,511},{1,510},{2,509},{3,508},{4,507},{5,506},{6,505},{7,504},{8,503}..., dimensions={0}, use_global_device_ids=true | all-gather | bytes 393216 | tf_op jit(solution)/shard_map/all_gather | solution.py:40
  106.5 1.6 %shard_map.60 = bf16[4,128,128]{2,1,0:T(8,128)(2,1)} custom-call(s32[3,16]{1,0:T(4,128)S(1)} %select_add_fusion.table, bf16[2,4,128,128]{3,2,1,0:T(8,128)(2,1)S(1)} %bitcast.11, f32[4,128,128]{2,1,0:T(8,128)S(1)} %convert_reduce_fusion.1.own, bf16[4,576,128]{2,1,0:T(8,128)(2,1)S(1)} %bitcast.9), custom_call_target="tpu_custom_call" | custom-call | bytes 4194304 | tf_op jit(solution)/shard_map/pallas_call | solution.py:305
  (15 shorter events, 0.1 us)
Async XLA Ops:
  0.8 12.6 %collective-permute-start = (bf16[4,64,128]{2,1,0:T(8,128)(2,1)S(1)}, bf16[4,64,128]{2,1,0:T(8,128)(2,1)S(1)}, u32[]{:S(2)}, u32[]{:S(2)}) collective-permute-start(bf16[4,64,128]{2,1,0:T(8,128)(2,1)S(1)} %slice.14), channel_id=1, source_target_pairs={{0,508},{1,509},{2,510},{3,511},{4,0},{5,1},{6,2},{7,3},{8,4},{9,5... | collective-permute-start | bytes 196616 | tf_op jit(solution)/shard_map/ppermute | solution.py:29
  11.1 1.2 %copy-start.2 = (bf16[16,256,128]{2,1,0:T(8,128)(2,1)S(1)}, bf16[16,256,128]{2,1,0:T(8,128)(2,1)}, u32[]{:S(2)}) copy-start(bf16[16,256,128]{2,1,0:T(8,128)(2,1)} %kernels.1) | copy-start | bytes 3145732
  12.3 1.2 %copy-start = (bf16[4,512,128]{2,1,0:T(8,128)(2,1)S(1)}, bf16[4,512,128]{2,1,0:T(8,128)(2,1)}, u32[]{:S(2)}) copy-start(bf16[4,512,128]{2,1,0:T(8,128)(2,1)} %model.3) | copy-start | bytes 1572868
  12.3 1.2 %copy-start.1 = (bf16[4,16,256]{2,1,0:T(8,128)(2,1)S(1)}, bf16[4,16,256]{2,1,0:T(8,128)(2,1)}, u32[]{:S(2)}) copy-start(bf16[4,16,256]{2,1,0:T(8,128)(2,1)} %observed.5) | copy-start | bytes 98308
  25.5 12.8 %collective-permute-start.1 = (bf16[128,128]{1,0:T(8,128)(2,1)S(1)}, bf16[128,128]{1,0:T(8,128)(2,1)S(1)}, u32[]{:S(2)}, u32[]{:S(2)}) collective-permute-start(bf16[128,128]{1,0:T(8,128)(2,1)S(1)} %slice.19), channel_id=1, source_target_pairs={{0,4},{1,5},{2,6},{3,7},{4,8},{5,9},{6,10},{7,11},{8,12},{9,13},{1... | collective-permute-start | bytes 98312 | tf_op jit(solution)/shard_map/ppermute | solution.py:29
  28.9 27.5 %collective-permute-start.2 = (bf16[64,128]{1,0:T(8,128)(2,1)S(1)}, bf16[64,128]{1,0:T(8,128)(2,1)S(1)}, u32[]{:S(2)}, u32[]{:S(2)}) collective-permute-start(bf16[64,128]{1,0:T(8,128)(2,1)S(1)} %slice.20), channel_id=1, source_target_pairs={{0,508},{1,509},{2,510},{3,511},{4,0},{5,1},{6,2},{7,3},{8,4},{9,5... | collective-permute-start | bytes 49160 | tf_op jit(solution)/shard_map/ppermute | solution.py:29
  68.0 7.2 %collective-permute-start.3 = (bf16[4,64,128]{2,1,0:T(8,128)(2,1)S(1)}, bf16[4,64,128]{2,1,0:T(8,128)(2,1)S(1)}, u32[]{:S(2)}, u32[]{:S(2)}) collective-permute-start(bf16[4,64,128]{2,1,0:T(8,128)(2,1)S(1)} %get-tuple-element.16), channel_id=1, source_target_pairs={{0,4},{1,5},{2,6},{3,7},{4,8},{5,9},{6,10},{7,11},{8,12},{9,13},{1... | collective-permute-start | bytes 196616 | tf_op jit(solution)/shard_map/ppermute | solution.py:29

commit v9 on v8

--- a/solution.py
+++ b/solution.py
@@ -200,23 +200,6 @@
         out[part, :] = (start.astype(F32) + STEP * total + sign * mirrored).astype(BF16)
 
 
-def finish_body(table, pair, own, band, out, done, sems):
-    far = table[2, 1]
-    quarter, cols = own.shape[1:]
-    low = pl.multiple_of(table[2, 2] * quarter, quarter)
-    turned = dot_nn(pair[far].reshape(4 * quarter, cols), backwards(cols)).astype(BF16)
-    swap = backwards(quarter)
-    stores = [pltpu.make_async_copy(done.at[comp], out.at[comp], sems.at[comp]) for comp in range(4)]
-    for comp in range(4):
-        start = band[comp, pl.ds(low, quarter), :].astype(F32)
-        mirrored = dot_nn(swap, turned[comp * quarter : (comp + 1) * quarter])
-        step = SIGNS[comp] * STEP
-        done[comp] = (start + STEP * own[comp] + step * mirrored).astype(BF16)
-        stores[comp].start()
-    for store in stores:
-        store.wait()
-
-
 def on_device(model, observed, kernels, offsets, counts):
     views = lax.axis_size("vis")
     view = lax.axis_index("vis")
@@ -261,7 +244,12 @@
         table, observed, ku_t, kv_t, model, halo
     )
 
-    partial, table = lax.optimization_barrier((partial, table))
+    none = jnp.zeros((), jnp.uint32)
+    far_at = low.astype(jnp.uint32)
+    first_row = view.astype(jnp.uint32) * quarter
+    partial, table, far_at, first_row = lax.optimization_barrier(
+        (partial, table, far_at, first_row)
+    )
     parts = lax.all_to_all(partial, "vis", 0, 0, tiled=True)
     own = jnp.sum(parts.astype(F32), axis=0)
     before = send(own[rows - SUB :].astype(BF16), lambda tile, view: (tile + 1, view))
@@ -302,12 +290,10 @@
     parts = lax.all_to_all(partial, "vis", 0, 0, tiled=True)
     own = jnp.sum(parts.astype(F32), axis=0)
     pair = with_mirror(own.astype(BF16), lambda tile, view: (tiles - 1 - tile, views - 1 - view))
-    return call(
-        finish_body,
-        sds((4, quarter, cols), BF16),
-        [pltpu.VMEM((4, quarter, cols), BF16), pltpu.SemaphoreType.DMA((4,))],
-        moved=moved,
-    )(in_specs=[SMEM] + [VMEM] * 3, out_specs=pl.BlockSpec(memory_space=pltpu.HBM))(table, pair, own, band)
+    far = lax.dynamic_slice(pair, (far_at, none, none, none), (1, 4, quarter, cols))[0]
+    signs = jnp.array(SIGNS, F32)[:, None, None]
+    start = lax.dynamic_slice(band, (none, first_row, none), (4, quarter, cols)).astype(F32)
+    return (start + STEP * (own + signs * far[:, ::-1, ::-1].astype(F32))).astype(BF16)
 
 
 def solution(mesh):

time: 108 us -> 108 us (level)
    pallas_call x1 -> x0, Pallas kernels: 1.55 us -> none  [on_device(): call(finish_body, sds((4, quarter, cols), BF16), [pltpu.VMEM((4, quarter,...]
where the time goes in v9:
time: 108 us
  blocking collectives  68.3 us (63%)
  starting transfers between devices  24.8 us (23%)
  Pallas kernels  7.66 us (7%)
  local copies, waits for them, and re-layouts  2.55 us (2%)
  other arithmetic  1.82 us (2%)
  waiting for transfers between devices  1.66 us (2%)
    all_gather x2, blocking collectives, with_mirror(): return lax.all_gather(value, ('tile', 'vis'), axis_index_groups=pairs)  39.3 us
    ppermute x4, starting transfers between devices, send(): return lax.ppermute(value, ('tile', 'vis'), pairs)  24.8 us
    all_to_all x2, blocking collectives, on_device(): parts = lax.all_to_all(partial, 'vis', 0, 0, tiled=True)  19 us
    all_gather x1, blocking collectives, on_device(): band = lax.all_gather(piece, 'vis', axis=0, tiled=False)  10 us
    pallas_call x1, Pallas kernels, on_device(): call(first_body, sds((4, full, cols), BF16), [obs, full_rows, full_rows],...  2.21 us
  transfers between devices with their start and end apart: 4, of which 1 were waited for; matrix products, arithmetic and copies ran while one was open for 1% of the time, Pallas kernels for 3%

profile of v9, /device:TPU:1, one launch (start us, length us, event | category | flops | bytes accessed | tf_op | source)
XLA Modules:
  0.0 107.8 jit_solution(15943579764014754927)
XLA Ops:
  0.0 0.8 slice.14
  0.8 8.8 %collective-permute-start = (bf16[4,64,128]{2,1,0:T(8,128)(2,1)S(1)}, bf16[4,64,128]{2,1,0:T(8,128)(2,1)S(1)}, u32[]{:S(2)}, u32[]{:S(2)}) collective-permute-start(bf16[4,64,128]{2,1,0:T(8,128)(2,1)S(1)} %slice.14), channel_id=1, source_target_pairs={{0,508},{1,509},{2,510},{3,511},{4,0},{5,1},{6,2},{7,3},{8,4},{9,5... | collective-permute-start | bytes 196616 | tf_op jit(solution)/shard_map/ppermute | solution.py:29
  10.3 0.8 select_add_fusion.table
  11.1 1.2 %copy-done.2 = bf16[16,256,128]{2,1,0:T(8,128)(2,1)S(1)} copy-done((bf16[16,256,128]{2,1,0:T(8,128)(2,1)S(1)}, bf16[16,256,128]{2,1,0:T(8,128)(2,1)}, u32[]{:S(2)}) %copy-start.2) | copy-done | bytes 1048600
  12.3 1.1 %shard_map.64 = (bf16[16,64,256]{2,1,0:T(8,128)(2,1)S(1)}, bf16[16,128,256]{2,1,0:T(8,128)(2,1)S(1)}) custom-call(s32[3,16]{1,0:T(4,128)S(1)} %select_add_fusion.table, bf16[16,256,128]{2,1,0:T(8,128)(2,1)S(1)} %copy-done.2), custom_call_target="tpu_custom_call" | custom-call | flops 8589934592 | bytes 4194304 | tf_op jit(solution)/shard_map/pallas_call | solution.py:228
  13.5 2.2 %shard_map.65 = bf16[4,576,128]{2,1,0:T(8,128)(2,1)S(1)} custom-call(s32[3,16]{1,0:T(4,128)S(1)} %select_add_fusion.table, bf16[4,16,256]{2,1,0:T(8,128)(2,1)S(1)} %copy-done.1, bf16[16,64,256]{2,1,0:T(8,128)(2,1)S(1)} %get-tuple-element.13.ku_t, bf16[16,128,256]{2,1,0:T(8,128)(2,1)S(1)} %get-tuple-element.14.kv_t, bf16[4,512,128]{2,1,0:T(8,128)(2,1)S(1)} %copy-done, ...), custom_call_target="tpu_custom_call" | custom-call | flops 8589934592 | bytes 4194304 | tf_op jit(solution)/shard_map/pallas_call | solution.py:237
  15.7 9.7 %all_to_all.10 = bf16[4,576,128]{2,1,0:T(8,128)(2,1)S(1)} all-to-all(bf16[4,576,128]{2,1,0:T(8,128)(2,1)S(1)} %shard_map.65), channel_id=1, replica_groups=mesh['tile'=128,'vis'=4] {'vis'}, dimensions={0} | all-to-all | bytes 1179648 | tf_op jit(solution)/shard_map/all_to_all | solution.py:253
  25.4 0.1 convert_reduce_fusion.own
  25.5 3.3 %collective-permute-start.1 = (bf16[128,128]{1,0:T(8,128)(2,1)S(1)}, bf16[128,128]{1,0:T(8,128)(2,1)S(1)}, u32[]{:S(2)}, u32[]{:S(2)}) collective-permute-start(bf16[128,128]{1,0:T(8,128)(2,1)S(1)} %slice.19), channel_id=1, source_target_pairs={{0,4},{1,5},{2,6},{3,7},{4,8},{5,9},{6,10},{7,11},{8,12},{9,13},{1... | collective-permute-start | bytes 98312 | tf_op jit(solution)/shard_map/ppermute | solution.py:29
  28.9 9.3 %collective-permute-start.2 = (bf16[64,128]{1,0:T(8,128)(2,1)S(1)}, bf16[64,128]{1,0:T(8,128)(2,1)S(1)}, u32[]{:S(2)}, u32[]{:S(2)}) collective-permute-start(bf16[64,128]{1,0:T(8,128)(2,1)S(1)} %slice.20), channel_id=1, source_target_pairs={{0,508},{1,509},{2,510},{3,511},{4,0},{5,1},{6,2},{7,3},{8,4},{9,5... | collective-permute-start | bytes 49160 | tf_op jit(solution)/shard_map/ppermute | solution.py:29
  38.2 0.0 collective-permute-done.1.before
  38.3 18.2 %all-gather = bf16[1152,128]{1,0:T(8,128)(2,1)S(1)} all-gather(bf16[576,128]{1,0:T(8,128)(2,1)S(1)} %add_convert_fusion.1), channel_id=2, replica_groups={{0,508},{1,509},{2,510},{3,511},{4,504},{5,505},{6,506},{7,507},{8,500}..., dimensions={0}, use_global_device_ids=true | all-gather | bytes 442368 | tf_op jit(solution)/shard_map/all_gather | solution.py:40
  56.4 0.0 collective-permute-done.2.after
  56.4 1.0 shard_map.66
  57.4 10.0 %all-gather.1 = bf16[2304,128]{1,0:T(8,128)(2,1)S(1)} all-gather(bf16[576,128]{1,0:T(8,128)(2,1)S(1)} %shard_map.66), channel_id=3, replica_groups=mesh['tile'=128,'vis'=4] {'vis'}, dimensions={0}, use_global_device_ids=true | all-gather | bytes 737280 | tf_op jit(solution)/shard_map/all_gather | solution.py:267
  67.4 1.2 %shard_map.67 = (bf16[4,64,128]{2,1,0:T(8,128)(2,1)S(1)}, f32[4,64,128]{2,1,0:T(8,128)S(1)}) custom-call(s32[3,16]{1,0:T(4,128)S(1)} %select_add_fusion.table, bf16[4,16,256]{2,1,0:T(8,128)(2,1)S(1)} %copy-done.1, bf16[16,64,256]{2,1,0:T(8,128)(2,1)S(1)} %get-tuple-element.13.ku_t, bf16[16,128,256]{2,1,0:T(8,128)(2,1)S(1)} %get-tuple-element.14.kv_t, ...), custom_call_target="tpu_custom_call" | custom-call | flops 536870912 | bytes 4194304 | tf_op jit(solution)/shard_map/pallas_call | solution.py:269
  68.6 3.4 %collective-permute-start.3 = (bf16[4,64,128]{2,1,0:T(8,128)(2,1)S(1)}, bf16[4,64,128]{2,1,0:T(8,128)(2,1)S(1)}, u32[]{:S(2)}, u32[]{:S(2)}) collective-permute-start(bf16[4,64,128]{2,1,0:T(8,128)(2,1)S(1)} %get-tuple-element.19), channel_id=1, source_target_pairs={{0,4},{1,5},{2,6},{3,7},{4,8},{5,9},{6,10},{7,11},{8,12},{9,13},{1... | collective-permute-start | bytes 196616 | tf_op jit(solution)/shard_map/ppermute | solution.py:29
  72.0 2.2 %shard_map.68 = bf16[4,4,128,128]{3,2,1,0:T(8,128)(2,1)S(1)} custom-call(s32[3,16]{1,0:T(4,128)S(1)} %select_add_fusion.table, bf16[4,16,256]{2,1,0:T(8,128)(2,1)S(1)} %copy-done.1, bf16[16,64,256]{2,1,0:T(8,128)(2,1)S(1)} %get-tuple-element.13.ku_t, bf16[16,128,256]{2,1,0:T(8,128)(2,1)S(1)} %get-tuple-element.14.kv_t, bf16[4,576,128]{2,1,0:T(8,128)(2,1)S(1)} %bitcast.10, ...), custom_call_target="tpu_custom_call" | custom-call | flops 8589934592 | bytes 4194304 | tf_op jit(solution)/shard_map/pallas_call | solution.py:279
  74.2 1.7 %collective-permute-done.3 = bf16[4,64,128]{2,1,0:T(8,128)(2,1)S(1)} collective-permute-done((bf16[4,64,128]{2,1,0:T(8,128)(2,1)S(1)}, bf16[4,64,128]{2,1,0:T(8,128)(2,1)S(1)}, u32[]{:S(2)}, u32[]{:S(2)}) %collective-permute-start.3) | collective-permute-done | bytes 65568 | tf_op jit(solution)/shard_map/ppermute | solution.py:29
  75.9 9.3 %all_to_all.11 = bf16[4,4,128,128]{3,2,1,0:T(8,128)(2,1)S(1)} all-to-all(bf16[4,4,128,128]{3,2,1,0:T(8,128)(2,1)S(1)} %add_convert_fusion), channel_id=1, replica_groups=mesh['tile'=128,'vis'=4] {'vis'}, dimensions={0} | all-to-all | bytes 1048576 | tf_op jit(solution)/shard_map/all_to_all | solution.py:290
  85.2 0.1 convert_reduce_fusion.1
  85.3 21.1 %all-gather.2 = bf16[8,128,128]{2,1,0:T(8,128)(2,1)S(1)} all-gather(bf16[4,128,128]{2,1,0:T(8,128)(2,1)S(1)} %convert_element_type.65), channel_id=4, replica_groups={{0,511},{1,510},{2,509},{3,508},{4,507},{5,506},{6,505},{7,504},{8,503}..., dimensions={0}, use_global_device_ids=true | all-gather | bytes 393216 | tf_op jit(solution)/shard_map/all_gather | solution.py:40
  106.5 0.4 rev.3
  107.0 0.8 add_convert_fusion.2
  (19 shorter events, 0.2 us)
Async XLA Ops:
  0.8 12.6 %collective-permute-start = (bf16[4,64,128]{2,1,0:T(8,128)(2,1)S(1)}, bf16[4,64,128]{2,1,0:T(8,128)(2,1)S(1)}, u32[]{:S(2)}, u32[]{:S(2)}) collective-permute-start(bf16[4,64,128]{2,1,0:T(8,128)(2,1)S(1)} %slice.14), channel_id=1, source_target_pairs={{0,508},{1,509},{2,510},{3,511},{4,0},{5,1},{6,2},{7,3},{8,4},{9,5... | collective-permute-start | bytes 196616 | tf_op jit(solution)/shard_map/ppermute | solution.py:29
  11.1 1.2 %copy-start.2 = (bf16[16,256,128]{2,1,0:T(8,128)(2,1)S(1)}, bf16[16,256,128]{2,1,0:T(8,128)(2,1)}, u32[]{:S(2)}) copy-start(bf16[16,256,128]{2,1,0:T(8,128)(2,1)} %kernels.1) | copy-start | bytes 3145732
  12.3 1.2 %copy-start = (bf16[4,512,128]{2,1,0:T(8,128)(2,1)S(1)}, bf16[4,512,128]{2,1,0:T(8,128)(2,1)}, u32[]{:S(2)}) copy-start(bf16[4,512,128]{2,1,0:T(8,128)(2,1)} %model.3) | copy-start | bytes 1572868
  12.3 1.2 %copy-start.1 = (bf16[4,16,256]{2,1,0:T(8,128)(2,1)S(1)}, bf16[4,16,256]{2,1,0:T(8,128)(2,1)}, u32[]{:S(2)}) copy-start(bf16[4,16,256]{2,1,0:T(8,128)(2,1)} %observed.5) | copy-start | bytes 98308
  25.5 12.7 %collective-permute-start.1 = (bf16[128,128]{1,0:T(8,128)(2,1)S(1)}, bf16[128,128]{1,0:T(8,128)(2,1)S(1)}, u32[]{:S(2)}, u32[]{:S(2)}) collective-permute-start(bf16[128,128]{1,0:T(8,128)(2,1)S(1)} %slice.19), channel_id=1, source_target_pairs={{0,4},{1,5},{2,6},{3,7},{4,8},{5,9},{6,10},{7,11},{8,12},{9,13},{1... | collective-permute-start | bytes 98312 | tf_op jit(solution)/shard_map/ppermute | solution.py:29
  28.9 27.6 %collective-permute-start.2 = (bf16[64,128]{1,0:T(8,128)(2,1)S(1)}, bf16[64,128]{1,0:T(8,128)(2,1)S(1)}, u32[]{:S(2)}, u32[]{:S(2)}) collective-permute-start(bf16[64,128]{1,0:T(8,128)(2,1)S(1)} %slice.20), channel_id=1, source_target_pairs={{0,508},{1,509},{2,510},{3,511},{4,0},{5,1},{6,2},{7,3},{8,4},{9,5... | collective-permute-start | bytes 49160 | tf_op jit(solution)/shard_map/ppermute | solution.py:29
  68.6 7.2 %collective-permute-start.3 = (bf16[4,64,128]{2,1,0:T(8,128)(2,1)S(1)}, bf16[4,64,128]{2,1,0:T(8,128)(2,1)S(1)}, u32[]{:S(2)}, u32[]{:S(2)}) collective-permute-start(bf16[4,64,128]{2,1,0:T(8,128)(2,1)S(1)} %get-tuple-element.19), channel_id=1, source_target_pairs={{0,4},{1,5},{2,6},{3,7},{4,8},{5,9},{6,10},{7,11},{8,12},{9,13},{1... | collective-permute-start | bytes 196616 | tf_op jit(solution)/shard_map/ppermute | solution.py:29
  85.2 21.7 %copy-start.3 = (f32[4]{0:T(128)S(1)}, f32[4]{0:T(128)}, u32[]{:S(2)}) copy-start(f32[4]{0:T(128)} %constant.30.clone) | copy-start | bytes 52
